TPU v7x, 32 devices: a whole 2x2x4 slice. The times are simulated.
32 devices in a mesh: genes: 16 (over z, y, x), batch: 2 (over core).
Axes of the slice: x: 2, y: 2, z: 4, core: 2. Of those that a mesh axis runs over, the one named last changes fastest.
Arguments:
- genotypes: bfloat16 [256, 786432], P('batch', 'genes'), may hold values from 0 to 2, as said below
- gene_weight: bfloat16 [16, 786432], P(None, 'genes'), may hold values from -0.375 to 0.375
- gene_lengths: int32 [3072], P('genes'), may hold values from 128 to 384, as said below
- membership: int32 [3072, 2], replicated, may hold values from 0 to 511, as said below
- pathway_slot: int32 [512], replicated, may hold values from 0 to 511, as said below
- pathway_weight: bfloat16 [6144, 1024], P('genes'), may hold values from -0.4375 to 0.4375
- head_weight: bfloat16 [32768], P('genes'), may hold values from -0.75 to 0.75
- cotangent: float32 [256], P('batch'), may hold values from -3 to 3
Outputs:
- grad_gene: float32 [16, 786432], P(None, 'genes')
- grad_pathway: float32 [6144, 1024], P('genes')
- grad_head: float32 [32768], P('genes')
Inputs may be any that keep to these rules, and one draw needn't show every extreme that they name: `genotypes`: dosages 0, 1 or 2. `gene_lengths`: the 192 genes of each index of genes together hold exactly its 49152 variants. `membership`: the 2 pathways of a gene differ; of the links of one index's genes at most 48 go to pathways whose slots lie in one index's range of 32 slots, and some index receives exactly 48 from every index. `pathway_slot`: a permutation of the pathways; slot s is held by index s // 32 of genes.
All inputs are finite; a program needn't handle non-finite values.
Results may differ from a plain program's by a relative error of at most 0.0062.
Values may be sent and summed in bfloat16 or wider, within the bound.
No kernel may reach another device: no remote copies, remote signals or barrier semaphores. Data moves between devices by JAX's collectives and lax.ppermute only.
A program may use at most 128 MiB of HBM per device.

v0:
```python
import jax
import jax.numpy as jnp
from jax import lax
from jax.sharding import PartitionSpec as P

GLEN = 256


block_cols = 512


def gene_window_count():
    return block_cols // (GLEN // 2) + 2


def gene_windows(lengths, var_count, window):
    starts = jnp.cumsum(lengths) - lengths
    blocks = var_count // block_cols
    block_start = jnp.arange(blocks) * block_cols
    first_gene = jnp.sum((starts[None, :] <= block_start[:, None]).astype(jnp.int32), axis=1) - 1
    padded = jnp.concatenate([starts, jnp.full((window,), var_count, jnp.int32)])
    upcoming = padded[first_gene[:, None] + jnp.arange(1, window, dtype=jnp.int32)[None, :]]
    position = block_start[:, None] + jnp.arange(block_cols, dtype=jnp.int32)[None, :]
    which = jnp.sum((upcoming[:, None, :] <= position[:, :, None]).astype(jnp.int32), axis=2)
    select = which[:, None, :] == jnp.arange(window, dtype=jnp.int32)[None, :, None]
    gene_ids = first_gene[:, None] + jnp.arange(window, dtype=jnp.int32)[None, :]
    return (gene_ids, select)


def contract_first(left, right, highest):
    if highest:
        return lax.dot_general(
            left,
            right,
            (((0,), (0,)), ((), ())),
            precision=lax.Precision.HIGHEST,
            preferred_element_type=jnp.float32,
        )
    return lax.dot_general(
        left, right, (((0,), (0,)), ((), ())), preferred_element_type=jnp.float32
    )


def gene_forward(genotype_rows, weight_rows, lengths):
    samples, var_count = genotype_rows.shape
    unit_count = weight_rows.shape[0]
    gene_count = lengths.shape[0]
    window_genes = gene_window_count()
    gene_ids, select = gene_windows(lengths, var_count, window_genes)
    blocks = var_count // block_cols
    rows = genotype_rows.reshape(samples, blocks, block_cols)
    weight_blocks = weight_rows.reshape(unit_count, blocks, block_cols).transpose(1, 0, 2)
    basis = jnp.where(
        select[:, :, None, :], weight_blocks[:, None, :, :], jnp.zeros((), weight_rows.dtype)
    )
    basis = basis.reshape(blocks, window_genes * unit_count, block_cols)
    partial_sums = jnp.einsum("bkv,kcv->kcb", rows, basis, preferred_element_type=jnp.float32)
    partial_sums = partial_sums.reshape(blocks * window_genes, unit_count * samples)
    gene_table = (
        gene_ids.reshape(-1)[None, :] == jnp.arange(gene_count, dtype=jnp.int32)[:, None]
    ).astype(jnp.float32)
    preact = jnp.dot(
        gene_table,
        partial_sums,
        precision=lax.Precision.HIGHEST,
        preferred_element_type=jnp.float32,
    )
    return (preact.reshape(gene_count, unit_count, samples), gene_ids, select)


def gene_backward(genotype_rows, preact_delta, gene_ids, select):
    samples, var_count = genotype_rows.shape
    gene_count, unit_count, _ = preact_delta.shape
    blocks = var_count // block_cols
    window = gene_ids.shape[1]
    rows = genotype_rows.reshape(samples, blocks, block_cols)
    clipped_ids = jnp.minimum(gene_ids, gene_count - 1).reshape(-1)
    window_table = (
        clipped_ids[:, None] == jnp.arange(gene_count, dtype=jnp.int32)[None, :]
    ).astype(jnp.bfloat16)
    windowed = jnp.dot(
        window_table,
        preact_delta.reshape(gene_count, unit_count * samples),
        preferred_element_type=jnp.float32,
    ).astype(jnp.bfloat16)
    windowed = windowed.reshape(blocks, window * unit_count, samples)
    full_terms = jnp.einsum("bkv,kcb->kcv", rows, windowed, preferred_element_type=jnp.float32)
    full_terms = full_terms.reshape(blocks, window, unit_count, block_cols)
    selected_entries = jnp.sum(
        jnp.where(select[:, :, None, :], full_terms, jnp.zeros((), jnp.float32)), axis=1
    )
    return selected_entries.transpose(1, 0, 2).reshape(unit_count, var_count)


def head_step(pathway_sum, head_rows, sample_grad):
    active = jnp.tanh(pathway_sum)
    grad_head = jnp.sum(active * sample_grad[None, None, :], axis=2).reshape(-1)
    pathway_delta = (
        sample_grad[None, None, :] * head_rows[:, :, None] * (1.0 - active * active)
    ).astype(jnp.bfloat16)
    return (grad_head, pathway_delta)


def on_device(
    genotypes,
    gene_weight,
    gene_lengths,
    membership,
    pathway_slot,
    pathway_weight,
    head_weight,
    cotangent,
):
    devices = lax.axis_size("genes")
    own_index = lax.axis_index("genes")
    gene_count = gene_lengths.shape[0]
    edge_count = pathway_weight.shape[0]
    link_count = edge_count // gene_count
    unit_count = gene_weight.shape[0]
    path_units = pathway_weight.shape[1] // unit_count
    owned_paths = head_weight.shape[0] // path_units
    capacity = 2 * edge_count // devices
    samples = genotypes.shape[0]
    total_slots = devices * capacity
    preact, gene_ids, select = gene_forward(genotypes, gene_weight, gene_lengths)
    hidden = jnp.tanh(preact).astype(jnp.bfloat16)
    slot_all = jnp.take(pathway_slot, membership.reshape(-1))
    target_all = slot_all // owned_paths
    own_slots = lax.dynamic_slice_in_dim(slot_all, own_index * edge_count, edge_count)
    own_target = own_slots // owned_paths
    edge_pos = jnp.arange(edge_count, dtype=jnp.int32)
    earlier = edge_pos[None, :] < edge_pos[:, None]
    same_owner = own_target[None, :] == own_target[:, None]
    send_rank = jnp.sum((earlier & same_owner).astype(jnp.int32), axis=1)
    send_place = own_target * capacity + send_rank
    place_table = (send_place[None, :] == jnp.arange(total_slots, dtype=jnp.int32)[:, None]).astype(
        jnp.bfloat16
    )
    arrive = (target_all.reshape(devices, edge_count) == own_index).astype(jnp.int32)
    arrive_rank = jnp.cumsum(arrive, axis=1) - arrive
    local_path = (slot_all % owned_paths).reshape(devices, edge_count)
    hits = (arrive[:, :, None] > 0) & (
        arrive_rank[:, :, None] == jnp.arange(capacity, dtype=jnp.int32)[None, None, :]
    )
    recv_local = jnp.sum(jnp.where(hits, local_path[:, :, None], 0), axis=1)
    filled = jnp.any(hits, axis=1)
    recv_path = jnp.where(filled, recv_local, owned_paths).reshape(-1)
    pick_rows = (recv_path[None, :] == jnp.arange(owned_paths, dtype=jnp.int32)[:, None]).astype(
        jnp.bfloat16
    )
    hidden_links = jnp.repeat(hidden, link_count, axis=0)
    head_rows = head_weight.reshape(owned_paths, path_units).astype(jnp.float32)
    hidden_out = jnp.dot(
        place_table,
        hidden_links.reshape(edge_count, unit_count * samples),
        preferred_element_type=jnp.float32,
    ).astype(jnp.bfloat16)
    weight_out = jnp.dot(place_table, pathway_weight, preferred_element_type=jnp.float32).astype(
        jnp.bfloat16
    )
    hidden_in, weight_in = (
        lax.all_to_all(
            hidden_out.reshape(devices, capacity, unit_count, samples),
            "genes",
            split_axis=0,
            concat_axis=0,
            tiled=True,
        ),
        lax.all_to_all(
            weight_out.reshape(devices, capacity, unit_count * path_units),
            "genes",
            split_axis=0,
            concat_axis=0,
            tiled=True,
        ),
    )
    hidden_in = hidden_in.reshape(total_slots, unit_count, samples)
    weight_in = weight_in.reshape(total_slots, unit_count, path_units)
    message = jnp.einsum(
        "nub,nuk->nkb", hidden_in, weight_in, preferred_element_type=jnp.float32
    ).astype(jnp.bfloat16)
    pathway_sum = jnp.dot(
        pick_rows,
        message.reshape(total_slots, path_units * samples),
        preferred_element_type=jnp.float32,
    )
    grad_head, pathway_delta = head_step(
        pathway_sum.reshape(owned_paths, path_units, samples), head_rows, cotangent
    )
    delta_slots = contract_first(
        pick_rows, pathway_delta.reshape(owned_paths, path_units * samples), False
    ).astype(jnp.bfloat16)
    delta_slots = delta_slots.reshape(total_slots, path_units, samples)
    hidden_back = jnp.einsum(
        "nuk,nkb->nub", weight_in, delta_slots, preferred_element_type=jnp.float32
    )
    weight_back = jnp.einsum(
        "nub,nkb->nuk", hidden_in, delta_slots, preferred_element_type=jnp.float32
    )
    hidden_ret, weight_ret = (
        lax.all_to_all(
            hidden_back.reshape(devices, capacity, unit_count, samples),
            "genes",
            split_axis=0,
            concat_axis=0,
            tiled=True,
        ),
        lax.all_to_all(
            weight_back.reshape(devices, capacity, unit_count * path_units),
            "genes",
            split_axis=0,
            concat_axis=0,
            tiled=True,
        ),
    )
    place_wide = place_table.astype(jnp.float32)
    hidden_delta = contract_first(
        place_wide, hidden_ret.reshape(total_slots, unit_count * samples), True
    )
    hidden_delta = hidden_delta.reshape(edge_count, unit_count, samples)
    grad_links = contract_first(
        place_wide, weight_ret.reshape(total_slots, unit_count * path_units), True
    )
    hidden_delta = jnp.sum(
        hidden_delta.reshape(gene_count, link_count, unit_count, samples), axis=1
    )
    latent_broad_matrix = hidden.astype(jnp.float32)
    preact_delta = (hidden_delta * (1.0 - latent_broad_matrix * latent_broad_matrix)).astype(
        jnp.bfloat16
    )
    grad_rows = gene_backward(genotypes, preact_delta, gene_ids, select)
    grad_gene, grad_pathway, grad_head = lax.psum((grad_rows, grad_links, grad_head), "batch")
    return (grad_gene, grad_pathway, grad_head)


def solution(mesh):
    return jax.shard_map(
        on_device,
        mesh=mesh,
        in_specs=(
            P("batch", "genes"),
            P(None, "genes"),
            P("genes"),
            P(),
            P(),
            P("genes", None),
            P("genes"),
            P("batch"),
        ),
        out_specs=(P(None, "genes"), P("genes", None), P("genes")),
        check_vma=False,
    )
```

profile of v0, /device:TPU:0, one launch (start us, length us, event | category | flops | bytes accessed | tf_op | source)
XLA Modules:
  0.0 577.4 jit_solution(3310463471448420835)
XLA Ops:
  10.4 38.6 %gather_fusion.1 = s32[6144]{0:T(1024)S(1)} fusion(s32[512]{0:T(512)S(1)} %copy-done.2, s32[6144]{0:T(1024)S(1)} %broadcast_clamp_fusion), kind=kCustom, calls=%fused_computation.1 | custom fusion | bytes 73728 | tf_op jit(solution)/shard_map/jit(_take)/gather | solution.py:127
  51.4 8.5 %all-to-all-start = ((bf16[16,48,1024]{2,1,0:T(8,128)(2,1)}), bf16[16,48,1024]{2,1,0:T(8,128)(2,1)}, u32[]{:S(2)}, u32[]{:S(2)}) async-start(bf16[16,48,1024]{2,1,0:T(8,128)(2,1)} %bitcast.127), calls=%async_computation | async-start | bytes 3145728 | tf_op jit(solution)/shard_map/all_to_all | solution.py:169
  69.5 6.4 %broadcast_select_fusion = bf16[96,6,16,512]{3,2,1,0:T(8,128)(2,1)} fusion(pred[96,6,512]{2,1,0:T(8,128)(4,1)S(1)} %iota_compare_fusion, bf16[96,16,512]{2,1,0:T(8,128)(2,1)} %copy.102), kind=kLoop, calls=%fused_computation.11 | loop fusion | flops 4718592 | bytes 11304960 | tf_op jit(solution)/shard_map/jit(_where)/select_n | solution.py:53
  75.9 11.7 %fusion.2 = f32[96,96,128]{2,1,0:T(8,128)} fusion(bf16[96,96,512]{2,1,0:T(8,128)(2,1)} %bitcast.115, bf16[16,96,8,512]{3,2,1,0:T(8,128)(2,1)} %bitcast.113), kind=kOutput, calls=%fused_computation.7 | convolution fusion | flops 1207959552 | bytes 26738688 | tf_op jit(solution)/shard_map/bkv,kcv->kcb/dot_general | solution.py:57
  103.6 7.5 %all-to-all-start.1 = ((bf16[16,48,16,128]{3,2,1,0:T(8,128)(2,1)}), bf16[16,48,16,128]{3,2,1,0:T(8,128)(2,1)}, u32[]{:S(2)}, u32[]{:S(2)}) async-start(bf16[16,48,16,128]{3,2,1,0:T(8,128)(2,1)} %bitcast.121), calls=%async_computation.1 | async-start | bytes 6291456 | tf_op jit(solution)/shard_map/all_to_all | solution.py:162
  120.3 51.5 %all-to-all-done.1 = bf16[16,48,16,128]{3,2,1,0:T(8,128)(2,1)} async-done(((bf16[16,48,16,128]{3,2,1,0:T(8,128)(2,1)}), bf16[16,48,16,128]{3,2,1,0:T(8,128)(2,1)}, u32[]{:S(2)}, u32[]{:S(2)}) %all-to-all-start.1) | async-done | bytes 3145760 | tf_op jit(solution)/shard_map/all_to_all | solution.py:162
  171.8 11.1 %convolution_convert_fusion.1 = bf16[768,64,128]{2,1,0:T(8,128)(2,1)} fusion(bf16[768,16,64]{2,1,0:T(8,128)(2,1)} %reshape.401, bf16[768,16,128]{2,1,0:T(8,128)(2,1)} %bitcast.12), kind=kOutput, calls=%fused_computation.12 | convolution fusion | flops 207618048 | bytes 17301504 | tf_op jit(solution)/shard_map/nub,nuk->nkb/dot_general | solution.py:179
  182.9 15.7 %copy.161 = bf16[96,8,64,128]{3,1,2,0:T(8,128)(2,1)} copy(bf16[96,8,64,128]{3,2,1,0:T(8,128)(2,1)} %bitcast.118) | data formatting | bytes 25165824
  198.6 16.6 %copy.106 = bf16[8192,768]{1,0:T(8,128)(2,1)} copy(bf16[8192,768]{0,1:T(8,128)(2,1)} %bitcast.117) | data formatting | bytes 25165824 | tf_op jit(solution)/shard_map/dot_general | solution.py:182
  215.3 9.0 %multiply_reduce_fusion = (f32[32,64]{0,1:T(8,128)}, bf16[64,4,8,128]{3,2,1,0:T(8,128)(2,1)S(1)}) fusion(f32[128]{0:T(128)S(1)} %copy-done.7, f32[32,64]{0,1:T(8,128)S(1)} %copy.101, bf16[64,128,768]{2,1,0:T(8,128)(2,1)} %bitcast.116, s32[768]{0:T(1024)S(1)} %select_n.138), kind=kOutput, calls=%fused_computation.37 | convolution fusion | flops 404510720 | bytes 13127168 | tf_op jit(solution)/shard_map/dot_general | solution.py:182
  228.1 6.5 %copy.124 = bf16[96,8,64,128]{3,2,1,0:T(8,128)(2,1)} copy(bf16[96,8,64,128]{3,1,2,0:T(8,128)(2,1)S(1)} %fusion.6) | data formatting | bytes 25165824
  234.5 14.8 %fusion.52 = f32[768,16,64]{2,1,0:T(8,128)} fusion(bf16[768,16,128]{2,1,0:T(8,128)(2,1)} %bitcast.12, bf16[768,64,128]{2,1,0:T(8,128)(2,1)} %bitcast.110), kind=kOutput, calls=%fused_computation.115 | convolution fusion | flops 201326592 | bytes 18874368 | tf_op jit(solution)/shard_map/nub,nkb->nuk/dot_general | solution.py:197
  249.4 6.3 %reshape.419 = f32[16,48,1024]{2,1,0:T(8,128)} reshape(f32[768,16,64]{2,1,0:T(8,128)} %fusion.52) | data formatting | bytes 6291456 | tf_op jit(solution)/shard_map/reshape | solution.py:209
  255.7 14.2 %all-to-all-start.3 = ((f32[16,48,1024]{2,1,0:T(8,128)}), f32[16,48,1024]{2,1,0:T(8,128)}, u32[]{:S(2)}, u32[]{:S(2)}) async-start(f32[16,48,1024]{2,1,0:T(8,128)} %reshape.419), calls=%async_computation.3 | async-start | bytes 6291456 | tf_op jit(solution)/shard_map/all_to_all | solution.py:208
  269.9 11.5 %fusion.51 = f32[768,16,128]{2,1,0:T(8,128)} fusion(bf16[768,16,64]{2,1,0:T(8,128)(2,1)} %reshape.401, bf16[768,64,128]{2,1,0:T(8,128)(2,1)} %bitcast.111), kind=kOutput, calls=%fused_computation.114 | convolution fusion | flops 201326592 | bytes 20447232 | tf_op jit(solution)/shard_map/nuk,nkb->nub/dot_general | solution.py:194
  281.5 49.2 %all-to-all-done.3 = f32[16,48,1024]{2,1,0:T(8,128)} async-done(((f32[16,48,1024]{2,1,0:T(8,128)}), f32[16,48,1024]{2,1,0:T(8,128)}, u32[]{:S(2)}, u32[]{:S(2)}) %all-to-all-start.3) | async-done | bytes 3145760 | tf_op jit(solution)/shard_map/all_to_all | solution.py:208
  330.6 14.1 %all-to-all-start.2 = ((f32[16,48,16,128]{3,2,1,0:T(8,128)}), f32[16,48,16,128]{3,2,1,0:T(8,128)}, u32[]{:S(2)}, u32[]{:S(2)}) async-start(f32[16,48,16,128]{3,2,1,0:T(8,128)} %bitcast.119), calls=%async_computation.2 | async-start | bytes 12582912 | tf_op jit(solution)/shard_map/all_to_all | solution.py:201
  350.3 110.7 %all-to-all-done.2 = f32[16,48,16,128]{3,2,1,0:T(8,128)} async-done(((f32[16,48,16,128]{3,2,1,0:T(8,128)}), f32[16,48,16,128]{3,2,1,0:T(8,128)}, u32[]{:S(2)}, u32[]{:S(2)}) %all-to-all-start.2) | async-done | bytes 6291488 | tf_op jit(solution)/shard_map/all_to_all | solution.py:201
  461.0 8.5 %copy.162 = f32[96,8,16,128]{3,1,2,0:T(8,128)} copy(f32[96,8,16,128]{3,2,1,0:T(8,128)} %bitcast.51) | data formatting | bytes 12582912
  469.4 6.8 %copy.108 = f32[768,2048]{0,1:T(8,128)} copy(f32[768,2048]{1,0:T(8,128)} %bitcast.120) | data formatting | bytes 12582912 | tf_op jit(solution)/shard_map/reshape | solution.py:218
  476.2 6.7 %convolution_reduce_fusion = f32[192,16,128]{2,0,1:T(8,128)S(1)} fusion(f32[16,128,768,1]{2,1,0,3:T(8,128)} %bitcast.124, s32[192,2]{0,1:T(2,128)S(1)} %copy.93), kind=kOutput, calls=%fused_computation.21 | convolution fusion | flops 7248445440 | bytes 7865856 | tf_op jit(solution)/shard_map/dot_general | solution.py:32
  488.8 13.7 %fusion = f32[96,96,512]{2,1,0:T(8,128)} fusion(bf16[96,96,128]{2,1,0:T(8,128)(2,1)S(1)} %reshape.416, bf16[16,96,8,512]{3,2,1,0:T(8,128)(2,1)} %bitcast.114), kind=kOutput, calls=%fused_computation.5 | convolution fusion | flops 1207959552 | bytes 33816576 | tf_op jit(solution)/shard_map/bkv,kcb->kcv/dot_general | solution.py:87
  502.5 8.3 %select_reduce_fusion = f32[96,16,512]{2,1,0:T(8,128)S(1)} fusion(f32[96,6,16,512]{3,2,1,0:T(8,128)} %bitcast.112, pred[96,6,512]{2,1,0:T(8,128)(4,1)S(1)} %iota_compare_fusion), kind=kLoop, calls=%fused_computation.2 | loop fusion | flops 8650752 | bytes 22315008 | tf_op jit(solution)/shard_map/reduce_sum | solution.py:89
  516.8 48.5 %all-reduce.5.cloned.1.call-done = (f32[16,49152]{1,0:T(8,128)}, f32[384,1024]{1,0:T(8,128)}) async-done(((f32[16,49152]{1,0:T(8,128)}, f32[384,1024]{1,0:T(8,128)}), (f32[16,49152]{1,0:T(8,128)}, f32[384,1024]{1,0:T(8,128)})) %all-reduce.5.cloned.1.call-update) | async-done | bytes 4718608 | tf_op jit(solution)/shard_map/psum | solution.py:232
  (89 shorter events, 66.6 us)
Async XLA Ops:
  7.2 42.1 %copy-start = (bf16[384,1024]{1,0:T(8,128)(2,1)S(1)}, bf16[384,1024]{1,0:T(8,128)(2,1)}, u32[]{:S(2)}) copy-start(bf16[384,1024]{1,0:T(8,128)(2,1)} %param.13) | copy-start | bytes 2359300
  7.2 3.2 copy-start.2
  48.9 11.1 %copy-start.6 = (s32[192]{0:T(256)S(1)}, s32[192]{0:T(256)}, u32[]{:S(2)}) copy-start(s32[192]{0:T(256)} %param.10) | copy-start | bytes 2308
  51.4 52.2 %all-to-all-start = ((bf16[16,48,1024]{2,1,0:T(8,128)(2,1)}), bf16[16,48,1024]{2,1,0:T(8,128)(2,1)}, u32[]{:S(2)}, u32[]{:S(2)}) async-start(bf16[16,48,1024]{2,1,0:T(8,128)(2,1)} %bitcast.127), calls=%async_computation | async-start | bytes 3145728 | tf_op jit(solution)/shard_map/all_to_all | solution.py:169
  103.6 68.2 %all-to-all-start.1 = ((bf16[16,48,16,128]{3,2,1,0:T(8,128)(2,1)}), bf16[16,48,16,128]{3,2,1,0:T(8,128)(2,1)}, u32[]{:S(2)}, u32[]{:S(2)}) async-start(bf16[16,48,16,128]{3,2,1,0:T(8,128)(2,1)} %bitcast.121), calls=%async_computation.1 | async-start | bytes 6291456 | tf_op jit(solution)/shard_map/all_to_all | solution.py:162
  111.1 1.7 copy-start.5
  198.6 16.6 %copy-start.7 = (f32[128]{0:T(128)S(1)}, f32[128]{0:T(128)}, u32[]{:S(2)}) copy-start(f32[128]{0:T(128)} %param.15) | copy-start | bytes 1540
  255.7 74.9 %all-to-all-start.3 = ((f32[16,48,1024]{2,1,0:T(8,128)}), f32[16,48,1024]{2,1,0:T(8,128)}, u32[]{:S(2)}, u32[]{:S(2)}) async-start(f32[16,48,1024]{2,1,0:T(8,128)} %reshape.419), calls=%async_computation.3 | async-start | bytes 6291456 | tf_op jit(solution)/shard_map/all_to_all | solution.py:208
  330.6 130.3 %all-to-all-start.2 = ((f32[16,48,16,128]{3,2,1,0:T(8,128)}), f32[16,48,16,128]{3,2,1,0:T(8,128)}, u32[]{:S(2)}, u32[]{:S(2)}) async-start(f32[16,48,16,128]{3,2,1,0:T(8,128)} %bitcast.119), calls=%async_computation.2 | async-start | bytes 12582912 | tf_op jit(solution)/shard_map/all_to_all | solution.py:201
  344.7 220.6 %all-reduce.5.cloned.1.call-start = ((), (), s32[]{:S(2)}) async-start(), calls=%async_computation.4 | async-start | bytes 9437184 | tf_op jit(solution)/shard_map/psum | solution.py:232
  512.8 0.8 copy-start.4
  565.3 3.9 copy-start.3
  565.3 5.1 copy-start.1
Sparse Core Ops, SparseCore 0:
  513.0 52.2 all-reduce.4
where the time goes:
time: 583 us; the launch traced here: 577 us
  waiting for transfers between devices  260 us (45%)
  local copies, waits for them, and re-layouts  139 us (24%)
  matrix products  98.6 us (17%)
  starting transfers between devices  44.3 us (8%)
  other arithmetic  18.2 us (3%)
  between operations  14.6 us (3%)
    all_to_all x1, waiting for transfers between devices, on_device(): lax.all_to_all(hidden_back.reshape(devices, capacity, unit_count, samples...  111 us
    all_to_all x1, waiting for transfers between devices, on_device(): lax.all_to_all(hidden_out.reshape(devices, capacity, unit_count, samples)...  51.5 us
    all_to_all x1, waiting for transfers between devices, on_device(): lax.all_to_all(weight_back.reshape(devices, capacity, unit_count * path_u...  49.2 us
    psum x1, waiting for transfers between devices, on_device(): lax.psum((grad_rows, grad_links, grad_head), 'batch')  48.5 us
    unnamed x24, local copies, waits for them, and re-layouts  42.4 us
    gather x3, local copies, waits for them, and re-layouts, on_device(): slot_all = jnp.take(pathway_slot, membership.reshape(-1))  38.6 us
    dot_general x1, local copies, waits for them, and re-layouts, on_device(): jnp.dot(pick_rows, message.reshape(total_slots, path_units * samples), pr...  16.6 us
    dot_general x1, matrix products, on_device(): jnp.einsum('nub,nkb->nuk', hidden_in, delta_slots, preferred_element_type...  14.8 us
  transfers between devices with their start and end apart: 5, of which 4 were waited for; matrix products, arithmetic and copies ran while one was open for 12% of the time, Pallas kernels for 0%

commit v1 on v0

v1 whole, which is shorter than its diff:
```python
import functools

import jax
import jax.numpy as jnp
from jax import lax
from jax.experimental import pallas as pl
from jax.experimental.pallas import tpu as pltpu
from jax.sharding import PartitionSpec as P

BLOCK = 512
MIN_GENE = 128
WINDOW = BLOCK // MIN_GENE + 1
GROUP = 4
LANES = 128
ROWS = 16
VMEM_LIMIT = 56 * 1024 * 1024

smem = pl.BlockSpec(memory_space=pltpu.SMEM)
vmem = pl.BlockSpec(memory_space=pltpu.VMEM)


def nt_dot(left, right):
    return lax.dot_general(
        left, right, (((1,), (1,)), ((), ())), preferred_element_type=jnp.float32
    )


def nn_dot(left, right):
    return jnp.dot(left, right, preferred_element_type=jnp.float32)


def fill_tables(gene_count, var_count, lengths, starts, first):
    def body(gene, start):
        starts[gene] = start
        end = start + lengths[gene]
        block = (start + (BLOCK - 1)) // BLOCK

        @pl.when(block * BLOCK < end)
        def _():
            first[block] = gene

        return end

    lax.fori_loop(0, gene_count, body, jnp.int32(0))
    for extra in range(WINDOW + 1):
        starts[gene_count + extra] = jnp.int32(var_count)


def window_masks(starts, gene, base, rows):
    position = lax.broadcasted_iota(jnp.int32, (rows, BLOCK), 1)
    masks = []
    for j in range(WINDOW):
        low = starts[gene + j] - base
        high = starts[gene + j + 1] - base
        masks.append((position >= low) & (position < high))
    return masks


def gene_forward_kernel(
    gene_count, var_count, blocks, lengths, geno, weight, out, pre, starts, first
):
    step = pl.program_id(0)
    units = weight.shape[0]

    @pl.when(step == 0)
    def _():
        fill_tables(gene_count, var_count, lengths, starts, first)
        pre[...] = jnp.zeros_like(pre)

    for i in range(blocks):
        block = step * blocks + i
        gene = first[block]
        masks = window_masks(starts, gene, block * BLOCK, units)
        wide = weight[:, i * BLOCK : (i + 1) * BLOCK].astype(jnp.float32)
        basis = jnp.concatenate(
            [jnp.where(mask, wide, 0.0).astype(jnp.bfloat16) for mask in masks], axis=0
        )
        part = nt_dot(basis, geno[:, i * BLOCK : (i + 1) * BLOCK])
        where = pl.ds(pl.multiple_of(gene * units, units), WINDOW * units)
        pre[where, :] += part

    @pl.when(step == pl.num_programs(0) - 1)
    def _():
        def body(i, _):
            at = pl.multiple_of(i * LANES, LANES)
            tile = jnp.tanh(pre[pl.ds(at, LANES), :])
            out[:, pl.ds(at, LANES)] = tile.T.astype(jnp.bfloat16)
            return 0

        lax.fori_loop(0, gene_count * units // LANES, body, 0, unroll=4)


def gene_forward(genotypes, gene_weight, lengths):
    samples, var_count = genotypes.shape
    units = gene_weight.shape[0]
    gene_count = lengths.shape[0]
    total = var_count // BLOCK
    blocks = next(n for n in (8, 4, 2, 1) if total % n == 0)
    cols = blocks * BLOCK
    return pl.pallas_call(
        functools.partial(gene_forward_kernel, gene_count, var_count, blocks),
        out_shape=jax.ShapeDtypeStruct((samples, gene_count * units), jnp.bfloat16),
        grid=(total // blocks,),
        in_specs=[
            smem,
            pl.BlockSpec((samples, cols), lambda i: (0, i)),
            pl.BlockSpec((units, cols), lambda i: (0, i)),
        ],
        out_specs=pl.BlockSpec((samples, gene_count * units), lambda i: (0, 0)),
        scratch_shapes=[
            pltpu.VMEM(((gene_count + WINDOW) * units, samples), jnp.float32),
            pltpu.SMEM((gene_count + WINDOW + 1,), jnp.int32),
            pltpu.SMEM((total,), jnp.int32),
        ],
        compiler_params=pltpu.CompilerParams(vmem_limit_bytes=VMEM_LIMIT),
        cost_estimate=pl.CostEstimate(
            flops=2 * WINDOW * units * samples * var_count,
            bytes_accessed=2 * (samples + units) * var_count,
            transcendentals=gene_count * units * samples,
        ),
        name="gene_forward",
    )(lengths, genotypes, gene_weight)


def gene_backward_kernel(
    gene_count, var_count, blocks, lengths, geno, delta, out, rows, starts, first
):
    step = pl.program_id(0)
    units = out.shape[0]

    @pl.when(step == 0)
    def _():
        fill_tables(gene_count, var_count, lengths, starts, first)
        tail = WINDOW * units
        rows[gene_count * units :, :] = jnp.zeros((tail, rows.shape[1]), rows.dtype)

        def body(i, _):
            at = pl.multiple_of(i * LANES, LANES)
            tile = delta[:, pl.ds(at, LANES)].astype(jnp.float32)
            rows[pl.ds(at, LANES), :] = tile.T.astype(jnp.bfloat16)
            return 0

        lax.fori_loop(0, gene_count * units // LANES, body, 0, unroll=4)

    for i in range(blocks):
        block = step * blocks + i
        gene = first[block]
        masks = window_masks(starts, gene, block * BLOCK, units)
        where = pl.ds(pl.multiple_of(gene * units, units), WINDOW * units)
        terms = nn_dot(rows[where, :], geno[:, i * BLOCK : (i + 1) * BLOCK])
        total = jnp.where(masks[0], terms[:units], 0.0)
        for j in range(1, WINDOW):
            total = jnp.where(masks[j], terms[j * units : (j + 1) * units], total)
        out[:, i * BLOCK : (i + 1) * BLOCK] = total.astype(out.dtype)


def gene_backward(genotypes, delta, lengths, units):
    samples, var_count = genotypes.shape
    gene_count = lengths.shape[0]
    total = var_count // BLOCK
    blocks = next(n for n in (8, 4, 2, 1) if total % n == 0)
    cols = blocks * BLOCK
    return pl.pallas_call(
        functools.partial(gene_backward_kernel, gene_count, var_count, blocks),
        out_shape=jax.ShapeDtypeStruct((units, var_count), jnp.bfloat16),
        grid=(total // blocks,),
        in_specs=[
            smem,
            pl.BlockSpec((samples, cols), lambda i: (0, i)),
            pl.BlockSpec((samples, gene_count * units), lambda i: (0, 0)),
        ],
        out_specs=pl.BlockSpec((units, cols), lambda i: (0, i)),
        scratch_shapes=[
            pltpu.VMEM(((gene_count + WINDOW) * units, samples), jnp.bfloat16),
            pltpu.SMEM((gene_count + WINDOW + 1,), jnp.int32),
            pltpu.SMEM((total,), jnp.int32),
        ],
        compiler_params=pltpu.CompilerParams(vmem_limit_bytes=VMEM_LIMIT),
        cost_estimate=pl.CostEstimate(
            flops=2 * WINDOW * units * samples * var_count,
            bytes_accessed=2 * (samples + units) * var_count,
            transcendentals=0,
        ),
        name="gene_backward",
    )(lengths, genotypes, delta)


def lane_groups(dtype, rows, width):
    lane = lax.broadcasted_iota(jnp.int32, (rows, LANES), 1) // width
    return [(lane == r).astype(jnp.float32).astype(dtype) for r in range(LANES // width)]


def swap_halves(x):
    half = LANES // 2
    return jnp.concatenate([x[:, half:], x[:, :half]], axis=1)


def link_forward_kernel(half_genes, units, place, members, slots, hidden, *refs):
    weights, outs, sums = refs[: 2 * GROUP], refs[2 * GROUP : -2], refs[-2:]
    quarter, core = place[0], place[1]
    tiles = LANES // units
    for total in sums:
        total[...] = jnp.zeros_like(total)
    keep = lane_groups(jnp.bfloat16, ROWS, units)
    low, high = lane_groups(jnp.bfloat16, LANES, LANES // 2)
    for piece in range(2 * GROUP):
        source = quarter ^ (piece % GROUP)
        half = core ^ (piece // GROUP)

        def body(t, _, piece=piece, source=source, half=half):
            first = half * half_genes + t * tiles
            at = pl.multiple_of(first * units, LANES)
            own = hidden[source, :, pl.ds(at, LANES)]
            upper, lower = own[:ROWS], own[ROWS:]
            left = jnp.concatenate(
                [jnp.concatenate([upper * k, lower * k], axis=1) for k in keep], axis=0
            )
            block = weights[piece][pl.ds(pl.multiple_of(t * LANES, LANES), LANES), :]
            turned = swap_halves(block)
            right = jnp.concatenate(
                [
                    jnp.concatenate([block * low, turned * low], axis=1),
                    jnp.concatenate([turned * high, block * high], axis=1),
                ],
                axis=0,
            )
            message = nn_dot(left, right)
            gene = source * (2 * half_genes) + first
            for r in range(tiles):
                for m in range(2):
                    slot = slots[members[m, gene + r]]
                    sums[m][slot] += message[
                        r * ROWS : (r + 1) * ROWS, m * LANES : (m + 1) * LANES
                    ]
            return 0

        lax.fori_loop(0, half_genes // tiles, body, 0, unroll=2)
    shard = outs[0].shape[0]
    for i, out in enumerate(outs):
        out[...] = (
            sums[0][i * shard : (i + 1) * shard] + sums[1][i * shard : (i + 1) * shard]
        ).astype(out.dtype)


def link_forward(place, members, slots, hidden, weights, shards):
    units = weights[0].shape[1] // 8
    half_genes = weights[0].shape[0] // units
    slot_count = slots.shape[0]
    out = jax.ShapeDtypeStruct((slot_count // shards, ROWS, LANES), jnp.bfloat16)
    return pl.pallas_call(
        functools.partial(link_forward_kernel, half_genes, units),
        out_shape=[out] * shards,
        in_specs=[smem, smem, smem, vmem] + [vmem] * len(weights),
        out_specs=[vmem] * shards,
        scratch_shapes=[pltpu.VMEM((slot_count, ROWS, LANES), jnp.float32)] * 2,
        compiler_params=pltpu.CompilerParams(vmem_limit_bytes=VMEM_LIMIT),
        cost_estimate=pl.CostEstimate(
            flops=4 * 10**9, bytes_accessed=8 * 10**6, transcendentals=0
        ),
        name="link_forward",
    )(place, members, slots, hidden, *weights)


def link_backward_kernel(half_genes, units, shards, place, members, slots, hidden, *refs):
    weights = refs[: 2 * GROUP]
    deltas = refs[2 * GROUP : 2 * GROUP + shards]
    out, grads, table = refs[2 * GROUP + shards], refs[2 * GROUP + shards + 1 : -1], refs[-1]
    quarter, core = place[0], place[1]
    tiles = LANES // units
    shard = deltas[0].shape[0]
    for i, delta in enumerate(deltas):
        table[i * shard : (i + 1) * shard] = delta[...]
    low, high = lane_groups(jnp.bfloat16, ROWS, LANES // 2)
    samples = hidden.shape[1]
    keep = lane_groups(jnp.float32, samples, units)
    row_gene = lax.broadcasted_iota(jnp.int32, (LANES, LANES), 0) // units
    lane_gene = lax.broadcasted_iota(jnp.int32, (LANES, LANES), 1) // samples
    fits = [
        (row_gene == lane_gene + i * (LANES // samples)).astype(jnp.float32)
        for i in range(tiles * samples // LANES)
    ]
    for piece in range(2 * GROUP):
        source = quarter ^ (piece % GROUP)
        half = core ^ (piece // GROUP)

        def body(t, _, piece=piece, source=source, half=half):
            first = half * half_genes + t * tiles
            at = pl.multiple_of(first * units, LANES)
            here = pl.ds(pl.multiple_of(t * LANES, LANES), LANES)
            own = hidden[source, :, pl.ds(at, LANES)].astype(jnp.float32)
            gene = source * (2 * half_genes) + first
            parts = []
            for r in range(tiles):
                one = table[slots[members[0, gene + r]]]
                two = table[slots[members[1, gene + r]]]
                parts.append(one * low + swap_halves(two) * high)
                parts.append(swap_halves(one) * low + two * high)
            right = jnp.concatenate(parts, axis=0)
            wide = nt_dot(right, weights[piece][here, :])
            back = wide[:samples] * keep[0]
            for r in range(1, tiles):
                back += wide[r * samples : (r + 1) * samples] * keep[r]
            out[source, :, pl.ds(at, LANES)] = (back * (1.0 - own * own)).astype(out.dtype)
            flat = jnp.concatenate([own] * (LANES // samples), axis=0).T
            left = jnp.concatenate([(flat * fit).astype(jnp.bfloat16) for fit in fits], axis=1)
            grads[piece][here, :] = nn_dot(left, right).astype(grads[piece].dtype)
            return 0

        lax.fori_loop(0, half_genes // tiles, body, 0, unroll=2)


def link_backward(place, members, slots, hidden, weights, deltas):
    units = weights[0].shape[1] // 8
    half_genes = weights[0].shape[0] // units
    slot_count = slots.shape[0]
    shards = len(deltas)
    grad = jax.ShapeDtypeStruct(weights[0].shape, jnp.bfloat16)
    return pl.pallas_call(
        functools.partial(link_backward_kernel, half_genes, units, shards),
        out_shape=[jax.ShapeDtypeStruct(hidden.shape, jnp.bfloat16)] + [grad] * len(weights),
        in_specs=[smem, smem, smem, vmem] + [vmem] * (len(weights) + shards),
        out_specs=[vmem] * (1 + len(weights)),
        scratch_shapes=[pltpu.VMEM((slot_count, ROWS, LANES), jnp.bfloat16)],
        compiler_params=pltpu.CompilerParams(vmem_limit_bytes=VMEM_LIMIT),
        cost_estimate=pl.CostEstimate(
            flops=6 * 10**9, bytes_accessed=10 * 10**6, transcendentals=0
        ),
        name="link_backward",
    )(place, members, slots, hidden, *weights, *deltas)


def on_device(
    genotypes,
    gene_weight,
    gene_lengths,
    membership,
    pathway_slot,
    pathway_weight,
    head_weight,
    cotangent,
):
    devices = lax.axis_size("genes")
    index = lax.axis_index("genes")
    core = lax.axis_index("batch")
    planes = devices // GROUP
    plane, quarter = index // GROUP, index % GROUP
    gene_count = gene_lengths.shape[0]
    units = gene_weight.shape[0]
    path_units = pathway_weight.shape[1] // units
    slot_count = pathway_slot.shape[0]
    shard = slot_count // planes
    samples = genotypes.shape[0]
    part = samples // GROUP
    half_rows = gene_count * units // 2
    in_plane = [[GROUP * z + q for q in range(GROUP)] for z in range(planes)]
    along = [[GROUP * z + q for z in range(planes)] for q in range(GROUP)]
    paired = planes == 4

    def swap_plane(x, d):
        pairs = [(GROUP * z + q, GROUP * z + (q ^ d)) for z in range(planes) for q in range(GROUP)]
        return lax.ppermute(x, "genes", pairs)

    def swap_along(x, d):
        pairs = [(GROUP * z + q, GROUP * (z ^ d) + q) for z in range(planes) for q in range(GROUP)]
        return lax.ppermute(x, "genes", pairs)

    def swap_core(x):
        return lax.ppermute(x, "batch", [(0, 1), (1, 0)])

    def spread(x, groups):
        return lax.all_to_all(
            x, "genes", split_axis=0, concat_axis=0, tiled=True, axis_index_groups=groups
        )

    with jax.named_scope("link_weights"):
        folded = pathway_weight.reshape(gene_count, 2, units, path_units)
        folded = folded.transpose(0, 2, 1, 3).reshape(gene_count * units, 2 * path_units)
        mine = lax.dynamic_slice_in_dim(folded, core * half_rows, half_rows)
        other = lax.dynamic_slice_in_dim(folded, (1 - core) * half_rows, half_rows)
        near = [mine] + [swap_plane(mine, d) for d in range(1, GROUP)]
        far = [other] + [swap_core(x) for x in near[1:]]
        weights = near + far

    with jax.named_scope("tables"):
        place = jnp.stack([quarter, core]).astype(jnp.int32)
        members = lax.dynamic_slice_in_dim(
            membership, plane * GROUP * gene_count, GROUP * gene_count
        ).T
        slots = pathway_slot ^ (plane * shard) if paired else pathway_slot
        head = lax.all_gather(
            head_weight, "genes", axis=0, tiled=True, axis_index_groups=in_plane
        )
        head = head.reshape(shard, 1, 1, path_units).astype(jnp.float32)
        cot = lax.dynamic_slice_in_dim(cotangent, quarter * part, part)
        cot = cot.reshape(part // ROWS, ROWS).T.reshape(1, ROWS, part // ROWS, 1)

    with jax.named_scope("hidden"):
        hidden = gene_forward(genotypes, gene_weight, gene_lengths)
        hidden = spread(hidden.reshape(GROUP, part, gene_count * units), in_plane)

    with jax.named_scope("pathway_sum"):
        sums = link_forward(place, members, slots, hidden, weights, planes)
        if paired:
            passed = sums[2].astype(jnp.float32) + swap_along(sums[3], 1).astype(jnp.float32)
            crossed = swap_along(passed.astype(jnp.bfloat16), 2)
            beside = swap_along(sums[1], 1)
            total = (
                sums[0].astype(jnp.float32)
                + crossed.astype(jnp.float32)
                + beside.astype(jnp.float32)
            )
        else:
            parts = spread(jnp.stack(sums), along)
            total = jnp.sum(parts.astype(jnp.float32), axis=0)

    with jax.named_scope("head"):
        total = total.reshape(shard, ROWS, part // ROWS, path_units)
        active = jnp.tanh(total)
        head_part = jnp.sum(active * cot, axis=(1, 2)).reshape(-1)
        delta = (cot * head * (1.0 - active * active)).astype(jnp.bfloat16)
        delta = delta.reshape(shard, ROWS, LANES)

    with jax.named_scope("pathway_delta"):
        if paired:
            one, two = swap_along(delta, 1), swap_along(delta, 2)
            deltas = [delta, one, two, swap_along(two, 1)]
        else:
            every = lax.all_gather(delta, "genes", axis=0, axis_index_groups=along)
            deltas = [every[i] for i in range(planes)]

    with jax.named_scope("link_grads"):
        back, *grads = link_backward(place, members, slots, hidden, weights, deltas)
        back = spread(back, in_plane).reshape(samples, gene_count * units)

    with jax.named_scope("grad_gene"):
        rows = gene_backward(genotypes, back, gene_lengths, units)
        grad_gene = rows.astype(jnp.float32) + swap_core(rows).astype(jnp.float32)

    with jax.named_scope("grad_pathway"):
        summed = [
            keep.astype(jnp.float32) + swap_core(give).astype(jnp.float32)
            for keep, give in zip(grads[:GROUP], grads[GROUP:])
        ]
        own = summed[0]
        for d in range(1, GROUP):
            own = own + swap_plane(summed[d].astype(jnp.bfloat16), d).astype(jnp.float32)
        theirs = swap_core(own)
        first = jnp.where(core == 0, own, theirs)
        second = jnp.where(core == 0, theirs, own)
        links = jnp.concatenate([first, second], axis=0)
        links = links.reshape(gene_count, units, 2, path_units).transpose(0, 2, 1, 3)
        grad_pathway = links.reshape(pathway_weight.shape)

    with jax.named_scope("grad_head"):
        head_part = spread(head_part.reshape(GROUP, -1), in_plane)
        head_part = jnp.sum(head_part, axis=0)
        grad_head = head_part + swap_core(head_part)

    return (grad_gene, grad_pathway, grad_head)


def solution(mesh):
    return jax.shard_map(
        on_device,
        mesh=mesh,
        in_specs=(
            P("batch", "genes"),
            P(None, "genes"),
            P("genes"),
            P(),
            P(),
            P("genes", None),
            P("genes"),
            P("batch"),
        ),
        out_specs=(P(None, "genes"), P("genes", None), P("genes")),
        check_vma=False,
    )
```

time: 583 us -> 233 us (0.40)
  waiting for transfers between devices: 260 us -> 59.3 us
  local copies, waits for them, and re-layouts: 139 us -> 19.2 us
  matrix products: 98.6 us -> 0 us
  Pallas kernels: 0 us -> 69.6 us
  blocking collectives: 3.06 us -> 20.6 us
  between operations: 14.6 us -> 0.97 us
  other arithmetic: 18.2 us -> 12.1 us
  starting transfers between devices: 44.3 us -> 50.2 us
    all_to_all x4 -> x2, waiting for transfers between devices: 211 us -> 9.04 us  [spread(): lax.all_to_all(x, 'genes', split_axis=0, concat_axis=0, tiled=True, axis_...]
    dot_general x13 -> x0, matrix products: 98.6 us -> none  [the longest x1 14.8 us: on_device(): jnp.einsum('nub,nkb->nuk', hidden_in, delta_slots, preferred_element_type...]
    pallas_call x0 -> x4, Pallas kernels: none -> 69.6 us  [the longest x1 20.1 us: link_backward(): pl.pallas_call(functools.partial(link_backward_kernel, half_genes, units,...]
    ppermute x0 -> x22, waiting for transfers between devices: none -> 50.3 us  [the longest x6 29.2 us: swap_along(): return lax.ppermute(x, 'genes', pairs)]
    psum x1 -> x0, waiting for transfers between devices: 48.5 us -> none  [on_device(): lax.psum((grad_rows, grad_links, grad_head), 'batch')]
    gather x6 -> x0, local copies, waits for them, and re-layouts: 42.3 us -> none  [the longest x3 38.6 us: on_device(): slot_all = jnp.take(pathway_slot, membership.reshape(-1))]
    ppermute x0 -> x22, starting transfers between devices: none -> 42.1 us  [the longest x6 28.8 us: swap_along(): return lax.ppermute(x, 'genes', pairs)]
    unnamed x24 -> x42, local copies, waits for them, and re-layouts: 42.4 us -> 2.94 us
  transfers between devices with their start and end apart: 5 -> 24, of which waited for: 4 -> 12; matrix products, arithmetic and copies ran while one was open for 12% -> 8% of each run, Pallas kernels for 0% -> 13%
where the time goes in v1:
time: 233 us; the launch traced here: 232 us
  Pallas kernels  69.6 us (30%)
  waiting for transfers between devices  59.3 us (25%)
  starting transfers between devices  50.2 us (22%)
  blocking collectives  20.6 us (9%)
  local copies, waits for them, and re-layouts  19.2 us (8%)
  other arithmetic  12.1 us (5%)
    ppermute x6, waiting for transfers between devices, swap_along(): return lax.ppermute(x, 'genes', pairs)  29.2 us
    ppermute x6, starting transfers between devices, swap_along(): return lax.ppermute(x, 'genes', pairs)  28.8 us
    pallas_call x1, Pallas kernels, link_backward(): pl.pallas_call(functools.partial(link_backward_kernel, half_genes, units,...  20.1 us
    ppermute x6, waiting for transfers between devices, swap_plane(): return lax.ppermute(x, 'genes', pairs)  19 us
    pallas_call x1, Pallas kernels, link_forward(): pl.pallas_call(functools.partial(link_forward_kernel, half_genes, units),...  18.4 us
    pallas_call x1, Pallas kernels, gene_forward(): pl.pallas_call(functools.partial(gene_forward_kernel, gene_count, var_cou...  15.9 us
    pallas_call x1, Pallas kernels, gene_backward(): pl.pallas_call(functools.partial(gene_backward_kernel, gene_count, var_co...  15.1 us
    all_gather x1, blocking collectives, on_device(): lax.all_gather(head_weight, 'genes', axis=0, tiled=True, axis_index_group...  12.9 us
  transfers between devices with their start and end apart: 24, of which 12 were waited for; matrix products, arithmetic and copies ran while one was open for 8% of the time, Pallas kernels for 13%

profile of v1, /device:TPU:0, one launch (start us, length us, event | category | flops | bytes accessed | tf_op | source)
XLA Modules:
  0.0 231.9 jit_solution(4633054901667310489)
XLA Ops:
  0.7 2.5 %reshape.50 = bf16[192,2,16,64]{3,2,1,0:T(8,128)(2,1)S(1)} reshape(bf16[384,1024]{1,0:T(8,128)(2,1)} %param.13) | data formatting | bytes 1572864 | tf_op jit(solution)/shard_map/link_weights/reshape | solution.py:376
  6.4 3.9 %collective-permute-start.2 = (bf16[1536,128]{1,0:T(8,128)(2,1)S(1)}, bf16[1536,128]{1,0:T(8,128)(2,1)S(1)}, u32[]{:S(2)}, u32[]{:S(2)}) collective-permute-start(bf16[1536,128]{1,0:T(8,128)(2,1)S(1)} %get-tuple-element.34.refs_0_), channel_id=1, source_target_pairs={{0,6},{2,4},{4,2},{6,0},{8,14},{10,12},{12,10},{14,8},{16,22},{18,... | collective-permute-start | bytes 1179656 | tf_op jit(solution)/shard_map/link_weights/ppermute | solution.py:361
  10.9 15.9 %gene_forward.1 = bf16[128,3072]{1,0:T(8,128)(2,1)} custom-call(s32[192]{0:T(256)} %lengths.3, bf16[128,49152]{1,0:T(8,128)(2,1)} %geno.3, bf16[16,49152]{1,0:T(8,128)(2,1)} %weight.1), custom_call_target="tpu_custom_call" | custom-call | flops 1006632960 | bytes 14155776 | tf_op jit(solution)/shard_map/hidden/gene_forward/pallas_call | solution.py:100
  26.8 4.3 %all-to-all-start = ((bf16[4,32,3072]{2,1,0:T(8,128)(2,1)}), bf16[4,32,3072]{2,1,0:T(8,128)(2,1)S(1)}, u32[]{:S(2)}, u32[]{:S(2)}) async-start(bf16[4,32,3072]{2,1,0:T(8,128)(2,1)} %bitcast.15), calls=%async_computation | async-start | bytes 1572864 | tf_op jit(solution)/shard_map/hidden/all_to_all | solution.py:371
  33.6 7.6 %all-to-all-done.hidden = bf16[4,32,3072]{2,1,0:T(8,128)(2,1)S(1)} async-done(((bf16[4,32,3072]{2,1,0:T(8,128)(2,1)}), bf16[4,32,3072]{2,1,0:T(8,128)(2,1)S(1)}, u32[]{:S(2)}, u32[]{:S(2)}) %all-to-all-start) | async-done | bytes 786464 | tf_op jit(solution)/shard_map/hidden/all_to_all | solution.py:371
  42.4 18.4 %link_forward.1 = (bf16[128,16,128]{2,1,0:T(8,128)(2,1)}, bf16[128,16,128]{2,1,0:T(8,128)(2,1)}, bf16[128,16,128]{2,1,0:T(8,128)(2,1)}, bf16[128,16,128]{2,1,0:T(8,128)(2,1)}) custom-call(s32[2]{0:T(128)} %pad_add_fusion.place, s32[2,768]{1,0:T(2,128)} %dynamic-slice_bitcast_fusion.members, s32[512]{0:T(512)} %broadcast_xor_fusion.slots, ...), custom_call_target="tpu_custom_call" | custom-call | flops 4000000000 | bytes 8000000 | tf_op jit(solution)/shard_map/pathway_sum/link_forward/pallas_call | solution.py:250
  63.0 13.0 %collective-permute-done.6 = bf16[128,16,128]{2,1,0:T(8,128)(2,1)S(1)} collective-permute-done((bf16[128,16,128]{2,1,0:T(8,128)(2,1)}, bf16[128,16,128]{2,1,0:T(8,128)(2,1)S(1)}, u32[]{:S(2)}, u32[]{:S(2)}) %collective-permute-start.6) | collective-permute-done | bytes 524320 | tf_op jit(solution)/shard_map/pathway_sum/ppermute | solution.py:365
  77.2 2.7 %collective-permute-start.7 = (bf16[128,16,128]{2,1,0:T(8,128)(2,1)S(1)}, bf16[128,16,128]{2,1,0:T(8,128)(2,1)S(1)}, u32[]{:S(2)}, u32[]{:S(2)}) collective-permute-start(bf16[128,16,128]{2,1,0:T(8,128)(2,1)S(1)} %add_convert_fusion), channel_id=1, source_target_pairs={{0,16},{2,18},{4,20},{6,22},{8,24},{10,26},{12,28},{14,30},{16,0},... | collective-permute-start | bytes 1572872 | tf_op jit(solution)/shard_map/pathway_sum/ppermute | solution.py:365
  80.3 12.9 %all_gather.3 = bf16[8192]{0:T(1024)(128)(2,1)S(1)} all-gather(bf16[2048]{0:T(1024)(128)(2,1)S(1)} %copy-done.9), channel_id=1, replica_groups={{0,2,4,6},{8,10,12,14},{16,18,20,22},{24,26,28,30},{1,3,5,7},{9,11,13,1..., dimensions={0}, use_global_device_ids=true | all-gather | bytes 20480 | tf_op jit(solution)/shard_map/tables/all_gather | solution.py:390
  95.7 4.2 %collective-permute-done.7 = bf16[128,16,128]{2,1,0:T(8,128)(2,1)S(1)} collective-permute-done((bf16[128,16,128]{2,1,0:T(8,128)(2,1)S(1)}, bf16[128,16,128]{2,1,0:T(8,128)(2,1)S(1)}, u32[]{:S(2)}, u32[]{:S(2)}) %collective-permute-start.7) | collective-permute-done | bytes 524320 | tf_op jit(solution)/shard_map/pathway_sum/ppermute | solution.py:365
  100.7 15.2 %collective-permute-start.9 = (bf16[128,16,128]{2,1,0:T(8,128)(2,1)S(1)}, bf16[128,16,128]{2,1,0:T(8,128)(2,1)S(1)}, u32[]{:S(2)}, u32[]{:S(2)}) collective-permute-start(bf16[128,16,128]{2,1,0:T(8,128)(2,1)S(1)} %get-tuple-element.30.refs_8_), channel_id=1, source_target_pairs={{0,8},{2,10},{4,12},{6,14},{8,0},{10,2},{12,4},{14,6},{16,24},{18,... | collective-permute-start | bytes 1572872 | tf_op jit(solution)/shard_map/pathway_delta/ppermute | solution.py:365
  116.2 8.7 %collective-permute-start.11 = (bf16[128,16,128]{2,1,0:T(8,128)(2,1)S(1)}, bf16[128,16,128]{2,1,0:T(8,128)(2,1)S(1)}, u32[]{:S(2)}, u32[]{:S(2)}) collective-permute-start(bf16[128,16,128]{2,1,0:T(8,128)(2,1)S(1)} %collective-permute-done.10.refs_10_), channel_id=1, source_target_pairs={{0,8},{2,10},{4,12},{6,14},{8,0},{10,2},{12,4},{14,6},{16,24},{18,... | collective-permute-start | bytes 1572872 | tf_op jit(solution)/shard_map/pathway_delta/ppermute | solution.py:365
  124.9 3.3 %collective-permute-done.9.refs_9_ = bf16[128,16,128]{2,1,0:T(8,128)(2,1)S(1)} collective-permute-done((bf16[128,16,128]{2,1,0:T(8,128)(2,1)S(1)}, bf16[128,16,128]{2,1,0:T(8,128)(2,1)S(1)}, u32[]{:S(2)}, u32[]{:S(2)}) %collective-permute-start.9) | collective-permute-done | bytes 524320 | tf_op jit(solution)/shard_map/pathway_delta/ppermute | solution.py:365
  128.2 6.1 %collective-permute-done.11.refs_11_ = bf16[128,16,128]{2,1,0:T(8,128)(2,1)S(1)} collective-permute-done((bf16[128,16,128]{2,1,0:T(8,128)(2,1)S(1)}, bf16[128,16,128]{2,1,0:T(8,128)(2,1)S(1)}, u32[]{:S(2)}, u32[]{:S(2)}) %collective-permute-start.11) | collective-permute-done | bytes 524320 | tf_op jit(solution)/shard_map/pathway_delta/ppermute | solution.py:365
  135.1 20.1 %link_backward.1 = (bf16[4,32,3072]{2,1,0:T(8,128)(2,1)}, bf16[1536,128]{1,0:T(8,128)(2,1)}, bf16[1536,128]{1,0:T(8,128)(2,1)}, bf16[1536,128]{1,0:T(8,128)(2,1)...) custom-call(s32[2]{0:T(128)} %pad_add_fusion.place, ...), custom_call_target="tpu_custom_call" | custom-call | flops 6000000000 | bytes 10000000 | tf_op jit(solution)/shard_map/link_grads/link_backward/pallas_call | solution.py:318
  158.3 5.0 %collective-permute-start.15 = (bf16[1536,128]{1,0:T(8,128)(2,1)S(1)}, bf16[1536,128]{1,0:T(8,128)(2,1)S(1)}, u32[]{:S(2)}, u32[]{:S(2)}) collective-permute-start(bf16[1536,128]{1,0:T(8,128)(2,1)S(1)} %add_convert_fusion.3), channel_id=1, source_target_pairs={{0,2},{2,0},{4,6},{6,4},{8,10},{10,8},{12,14},{14,12},{16,18},{18,... | collective-permute-start | bytes 1179656 | tf_op jit(solution)/shard_map/grad_pathway/ppermute | solution.py:361
  166.6 3.7 %all-to-all-start.1 = ((bf16[4,32,3072]{2,1,0:T(8,128)(2,1)}), bf16[4,32,3072]{2,1,0:T(8,128)(2,1)S(1)}, u32[]{:S(2)}, u32[]{:S(2)}) async-start(bf16[4,32,3072]{2,1,0:T(8,128)(2,1)} %get-tuple-element.20), calls=%async_computation.1 | async-start | bytes 1572864 | tf_op jit(solution)/shard_map/link_grads/all_to_all | solution.py:371
  170.2 3.0 %collective-permute-done.15 = bf16[1536,128]{1,0:T(8,128)(2,1)S(1)} collective-permute-done((bf16[1536,128]{1,0:T(8,128)(2,1)S(1)}, bf16[1536,128]{1,0:T(8,128)(2,1)S(1)}, u32[]{:S(2)}, u32[]{:S(2)}) %collective-permute-start.15) | collective-permute-done | bytes 393248 | tf_op jit(solution)/shard_map/grad_pathway/ppermute | solution.py:361
  173.2 16.0 %collective-permute-done.17 = bf16[1536,128]{1,0:T(8,128)(2,1)} collective-permute-done((bf16[1536,128]{1,0:T(8,128)(2,1)S(1)}, bf16[1536,128]{1,0:T(8,128)(2,1)}, u32[]{:S(2)}, u32[]{:S(2)}) %collective-permute-start.17) | collective-permute-done | bytes 393248 | tf_op jit(solution)/shard_map/grad_pathway/ppermute | solution.py:361
  193.1 15.1 %gene_backward.1 = bf16[16,49152]{1,0:T(8,128)(2,1)} custom-call(s32[192]{0:T(256)} %lengths.3, bf16[128,49152]{1,0:T(8,128)(2,1)} %geno.3, bf16[128,3072]{1,0:T(8,128)(2,1)} %bitcast.16), custom_call_target="tpu_custom_call" | custom-call | flops 1006632960 | bytes 14155776 | tf_op jit(solution)/shard_map/grad_gene/gene_backward/pallas_call | solution.py:163
  208.5 7.7 %all_to_all.20 = f32[4,1,2048]{2,1,0:T(1,128)S(1)} all-to-all(f32[4,1,2048]{2,1,0:T(1,128)S(1)} %all_to_all.16), channel_id=1, replica_groups={{0,2,4,6},{8,10,12,14},{16,18,20,22},{24,26,28,30},{1,3,5,7},{9,11,13,1..., dimensions={0} | all-to-all | bytes 65536 | tf_op jit(solution)/shard_map/grad_head/all_to_all | solution.py:371
  219.4 3.2 %reshape.54 = f32[192,16,2,64]{3,2,1,0:T(2,128)S(1)} reshape(f32[3072,128]{1,0:T(8,128)} %pad_maximum_fusion) | data formatting | bytes 3145728 | tf_op jit(solution)/shard_map/grad_pathway/reshape | solution.py:451
  224.6 3.8 %reshape.55 = f32[384,1024]{1,0:T(8,128)} reshape(f32[192,2,16,64]{3,2,1,0:T(8,128)} %copy.23) | data formatting | bytes 3145728 | tf_op jit(solution)/shard_map/grad_pathway/reshape | solution.py:452
  228.5 3.5 %convert_add_fusion = f32[16,49152]{1,0:T(8,128)} fusion(bf16[16,49152]{1,0:T(8,128)(2,1)} %collective-permute-done.12, bf16[16,49152]{1,0:T(8,128)(2,1)S(1)} %copy-done.1), kind=kLoop, calls=%fused_computation | loop fusion | flops 2359296 | bytes 6291456 | tf_op jit(solution)/shard_map/grad_gene/add | solution.py:437
  (106 shorter events, 31.0 us)
Async XLA Ops:
  6.4 24.7 %collective-permute-start.2 = (bf16[1536,128]{1,0:T(8,128)(2,1)S(1)}, bf16[1536,128]{1,0:T(8,128)(2,1)S(1)}, u32[]{:S(2)}, u32[]{:S(2)}) collective-permute-start(bf16[1536,128]{1,0:T(8,128)(2,1)S(1)} %get-tuple-element.34.refs_0_), channel_id=1, source_target_pairs={{0,6},{2,4},{4,2},{6,0},{8,14},{10,12},{12,10},{14,8},{16,22},{18,... | collective-permute-start | bytes 1179656 | tf_op jit(solution)/shard_map/link_weights/ppermute | solution.py:361
  10.3 20.9 %collective-permute-start.1 = (bf16[1536,128]{1,0:T(8,128)(2,1)S(1)}, bf16[1536,128]{1,0:T(8,128)(2,1)S(1)}, u32[]{:S(2)}, u32[]{:S(2)}) collective-permute-start(bf16[1536,128]{1,0:T(8,128)(2,1)S(1)} %get-tuple-element.34.refs_0_), channel_id=1, source_target_pairs={{0,4},{2,6},{4,0},{6,2},{8,12},{10,14},{12,8},{14,10},{16,20},{18,... | collective-permute-start | bytes 1179656 | tf_op jit(solution)/shard_map/link_weights/ppermute | solution.py:361
  10.8 20.9 %collective-permute-start = (bf16[1536,128]{1,0:T(8,128)(2,1)S(1)}, bf16[1536,128]{1,0:T(8,128)(2,1)S(1)}, u32[]{:S(2)}, u32[]{:S(2)}) collective-permute-start(bf16[1536,128]{1,0:T(8,128)(2,1)S(1)} %get-tuple-element.34.refs_0_), channel_id=1, source_target_pairs={{0,2},{2,0},{4,6},{6,4},{8,10},{10,8},{12,14},{14,12},{16,18},{18,... | collective-permute-start | bytes 1179656 | tf_op jit(solution)/shard_map/link_weights/ppermute | solution.py:361
  26.8 14.3 %all-to-all-start = ((bf16[4,32,3072]{2,1,0:T(8,128)(2,1)}), bf16[4,32,3072]{2,1,0:T(8,128)(2,1)S(1)}, u32[]{:S(2)}, u32[]{:S(2)}) async-start(bf16[4,32,3072]{2,1,0:T(8,128)(2,1)} %bitcast.15), calls=%async_computation | async-start | bytes 1572864 | tf_op jit(solution)/shard_map/hidden/all_to_all | solution.py:371
  31.2 10.0 %collective-permute-start.5 = (bf16[1536,128]{1,0:T(8,128)(2,1)S(1)}, bf16[1536,128]{1,0:T(8,128)(2,1)S(1)}, u32[]{:S(2)}, u32[]{:S(2)}) collective-permute-start(bf16[1536,128]{1,0:T(8,128)(2,1)S(1)} %collective-permute-done.2.refs_3_), channel_id=1, source_target_pairs={{0,1},{1,0},{2,3},{3,2},{4,5},{5,4},{6,7},{7,6},{8,9},{9,8},{10,11... | collective-permute-start | bytes 1179656 | tf_op jit(solution)/shard_map/link_weights/ppermute | solution.py:368
  31.3 9.9 %collective-permute-start.4 = (bf16[1536,128]{1,0:T(8,128)(2,1)S(1)}, bf16[1536,128]{1,0:T(8,128)(2,1)S(1)}, u32[]{:S(2)}, u32[]{:S(2)}) collective-permute-start(bf16[1536,128]{1,0:T(8,128)(2,1)S(1)} %collective-permute-done.1.refs_2_), channel_id=1, source_target_pairs={{0,1},{1,0},{2,3},{3,2},{4,5},{5,4},{6,7},{7,6},{8,9},{9,8},{10,11... | collective-permute-start | bytes 1179656 | tf_op jit(solution)/shard_map/link_weights/ppermute | solution.py:368
  31.7 9.4 %collective-permute-start.3 = (bf16[1536,128]{1,0:T(8,128)(2,1)S(1)}, bf16[1536,128]{1,0:T(8,128)(2,1)S(1)}, u32[]{:S(2)}, u32[]{:S(2)}) collective-permute-start(bf16[1536,128]{1,0:T(8,128)(2,1)S(1)} %collective-permute-done.refs_1_), channel_id=1, source_target_pairs={{0,1},{1,0},{2,3},{3,2},{4,5},{5,4},{6,7},{7,6},{8,9},{9,8},{10,11... | collective-permute-start | bytes 1179656 | tf_op jit(solution)/shard_map/link_weights/ppermute | solution.py:368
  60.9 15.1 %collective-permute-start.6 = (bf16[128,16,128]{2,1,0:T(8,128)(2,1)}, bf16[128,16,128]{2,1,0:T(8,128)(2,1)S(1)}, u32[]{:S(2)}, u32[]{:S(2)}) collective-permute-start(bf16[128,16,128]{2,1,0:T(8,128)(2,1)} %get-tuple-element.18), channel_id=1, source_target_pairs={{0,8},{2,10},{4,12},{6,14},{8,0},{10,2},{12,4},{14,6},{16,24},{18,... | collective-permute-start | bytes 1572872 | tf_op jit(solution)/shard_map/pathway_sum/ppermute | solution.py:365
  62.5 33.2 %collective-permute-start.8 = (bf16[128,16,128]{2,1,0:T(8,128)(2,1)}, bf16[128,16,128]{2,1,0:T(8,128)(2,1)S(1)}, u32[]{:S(2)}, u32[]{:S(2)}) collective-permute-start(bf16[128,16,128]{2,1,0:T(8,128)(2,1)} %get-tuple-element.19), channel_id=1, source_target_pairs={{0,8},{2,10},{4,12},{6,14},{8,0},{10,2},{12,4},{14,6},{16,24},{18,... | collective-permute-start | bytes 1572872 | tf_op jit(solution)/shard_map/pathway_sum/ppermute | solution.py:365
  77.2 22.8 %collective-permute-start.7 = (bf16[128,16,128]{2,1,0:T(8,128)(2,1)S(1)}, bf16[128,16,128]{2,1,0:T(8,128)(2,1)S(1)}, u32[]{:S(2)}, u32[]{:S(2)}) collective-permute-start(bf16[128,16,128]{2,1,0:T(8,128)(2,1)S(1)} %add_convert_fusion), channel_id=1, source_target_pairs={{0,16},{2,18},{4,20},{6,22},{8,24},{10,26},{12,28},{14,30},{16,0},... | collective-permute-start | bytes 1572872 | tf_op jit(solution)/shard_map/pathway_sum/ppermute | solution.py:365
  100.6 15.6 %collective-permute-start.10 = (bf16[128,16,128]{2,1,0:T(8,128)(2,1)S(1)}, bf16[128,16,128]{2,1,0:T(8,128)(2,1)S(1)}, u32[]{:S(2)}, u32[]{:S(2)}) collective-permute-start(bf16[128,16,128]{2,1,0:T(8,128)(2,1)S(1)} %get-tuple-element.30.refs_8_), channel_id=1, source_target_pairs={{0,16},{2,18},{4,20},{6,22},{8,24},{10,26},{12,28},{14,30},{16,0},... | collective-permute-start | bytes 1572872 | tf_op jit(solution)/shard_map/pathway_delta/ppermute | solution.py:365
  100.7 27.6 %collective-permute-start.9 = (bf16[128,16,128]{2,1,0:T(8,128)(2,1)S(1)}, bf16[128,16,128]{2,1,0:T(8,128)(2,1)S(1)}, u32[]{:S(2)}, u32[]{:S(2)}) collective-permute-start(bf16[128,16,128]{2,1,0:T(8,128)(2,1)S(1)} %get-tuple-element.30.refs_8_), channel_id=1, source_target_pairs={{0,8},{2,10},{4,12},{6,14},{8,0},{10,2},{12,4},{14,6},{16,24},{18,... | collective-permute-start | bytes 1572872 | tf_op jit(solution)/shard_map/pathway_delta/ppermute | solution.py:365
  116.2 18.1 %collective-permute-start.11 = (bf16[128,16,128]{2,1,0:T(8,128)(2,1)S(1)}, bf16[128,16,128]{2,1,0:T(8,128)(2,1)S(1)}, u32[]{:S(2)}, u32[]{:S(2)}) collective-permute-start(bf16[128,16,128]{2,1,0:T(8,128)(2,1)S(1)} %collective-permute-done.10.refs_10_), channel_id=1, source_target_pairs={{0,8},{2,10},{4,12},{6,14},{8,0},{10,2},{12,4},{14,6},{16,24},{18,... | collective-permute-start | bytes 1572872 | tf_op jit(solution)/shard_map/pathway_delta/ppermute | solution.py:365
  155.2 2.0 collective-permute-start.14
  155.3 14.9 %collective-permute-start.13 = (bf16[1536,128]{1,0:T(8,128)(2,1)}, bf16[1536,128]{1,0:T(8,128)(2,1)S(1)}, u32[]{:S(2)}, u32[]{:S(2)}) collective-permute-start(bf16[1536,128]{1,0:T(8,128)(2,1)} %get-tuple-element.22), channel_id=1, source_target_pairs={{0,1},{1,0},{2,3},{3,2},{4,5},{5,4},{6,7},{7,6},{8,9},{9,8},{10,11... | collective-permute-start | bytes 1179656 | tf_op jit(solution)/shard_map/grad_pathway/ppermute | solution.py:368
  155.8 7.5 %collective-permute-start.16 = (bf16[1536,128]{1,0:T(8,128)(2,1)}, bf16[1536,128]{1,0:T(8,128)(2,1)S(1)}, u32[]{:S(2)}, u32[]{:S(2)}) collective-permute-start(bf16[1536,128]{1,0:T(8,128)(2,1)} %get-tuple-element.26), channel_id=1, source_target_pairs={{0,1},{1,0},{2,3},{3,2},{4,5},{5,4},{6,7},{7,6},{8,9},{9,8},{10,11... | collective-permute-start | bytes 1179656 | tf_op jit(solution)/shard_map/grad_pathway/ppermute | solution.py:368
  155.9 9.5 %collective-permute-start.18 = (bf16[1536,128]{1,0:T(8,128)(2,1)}, bf16[1536,128]{1,0:T(8,128)(2,1)S(1)}, u32[]{:S(2)}, u32[]{:S(2)}) collective-permute-start(bf16[1536,128]{1,0:T(8,128)(2,1)} %get-tuple-element.28), channel_id=1, source_target_pairs={{0,1},{1,0},{2,3},{3,2},{4,5},{5,4},{6,7},{7,6},{8,9},{9,8},{10,11... | collective-permute-start | bytes 1179656 | tf_op jit(solution)/shard_map/grad_pathway/ppermute | solution.py:368
  158.3 14.9 %collective-permute-start.15 = (bf16[1536,128]{1,0:T(8,128)(2,1)S(1)}, bf16[1536,128]{1,0:T(8,128)(2,1)S(1)}, u32[]{:S(2)}, u32[]{:S(2)}) collective-permute-start(bf16[1536,128]{1,0:T(8,128)(2,1)S(1)} %add_convert_fusion.3), channel_id=1, source_target_pairs={{0,2},{2,0},{4,6},{6,4},{8,10},{10,8},{12,14},{14,12},{16,18},{18,... | collective-permute-start | bytes 1179656 | tf_op jit(solution)/shard_map/grad_pathway/ppermute | solution.py:361
  164.4 24.8 %collective-permute-start.17 = (bf16[1536,128]{1,0:T(8,128)(2,1)S(1)}, bf16[1536,128]{1,0:T(8,128)(2,1)}, u32[]{:S(2)}, u32[]{:S(2)}) collective-permute-start(bf16[1536,128]{1,0:T(8,128)(2,1)S(1)} %add_convert_fusion.2), channel_id=1, source_target_pairs={{0,4},{2,6},{4,0},{6,2},{8,12},{10,14},{12,8},{14,10},{16,20},{18,... | collective-permute-start | bytes 1179656 | tf_op jit(solution)/shard_map/grad_pathway/ppermute | solution.py:361
  165.5 23.8 %collective-permute-start.19 = (bf16[1536,128]{1,0:T(8,128)(2,1)S(1)}, bf16[1536,128]{1,0:T(8,128)(2,1)}, u32[]{:S(2)}, u32[]{:S(2)}) collective-permute-start(bf16[1536,128]{1,0:T(8,128)(2,1)S(1)} %add_convert_fusion.1), channel_id=1, source_target_pairs={{0,6},{2,4},{4,2},{6,0},{8,14},{10,12},{12,10},{14,8},{16,22},{18,... | collective-permute-start | bytes 1179656 | tf_op jit(solution)/shard_map/grad_pathway/ppermute | solution.py:361
  166.6 25.7 %all-to-all-start.1 = ((bf16[4,32,3072]{2,1,0:T(8,128)(2,1)}), bf16[4,32,3072]{2,1,0:T(8,128)(2,1)S(1)}, u32[]{:S(2)}, u32[]{:S(2)}) async-start(bf16[4,32,3072]{2,1,0:T(8,128)(2,1)} %get-tuple-element.20), calls=%async_computation.1 | async-start | bytes 1572864 | tf_op jit(solution)/shard_map/link_grads/all_to_all | solution.py:371
  190.7 27.4 %collective-permute-start.20 = (f32[1536,128]{1,0:T(8,128)S(1)}, f32[1536,128]{1,0:T(8,128)S(1)}, u32[]{:S(2)}, u32[]{:S(2)}) collective-permute-start(f32[1536,128]{1,0:T(8,128)S(1)} %convert_add_fusion.1), channel_id=1, source_target_pairs={{0,1},{1,0},{2,3},{3,2},{4,5},{5,4},{6,7},{7,6},{8,9},{9,8},{10,11... | collective-permute-start | bytes 2359304 | tf_op jit(solution)/shard_map/grad_pathway/ppermute | solution.py:368
  208.2 20.3 %collective-permute-start.12 = (bf16[16,49152]{1,0:T(8,128)(2,1)}, bf16[16,49152]{1,0:T(8,128)(2,1)}, u32[]{:S(2)}, u32[]{:S(2)}) collective-permute-start(bf16[16,49152]{1,0:T(8,128)(2,1)} %gene_backward.1), channel_id=1, source_target_pairs={{0,1},{1,0},{2,3},{3,2},{4,5},{5,4},{6,7},{7,6},{8,9},{9,8},{10,11... | collective-permute-start | bytes 4718600 | tf_op jit(solution)/shard_map/grad_gene/ppermute | solution.py:368
  216.2 1.2 collective-permute-start.21
  (21 other events, 268.0 us)

commit v2 on v1

v2 whole, which is shorter than its diff:
```python
import functools

import jax
import jax.numpy as jnp
from jax import lax
from jax.experimental import pallas as pl
from jax.experimental.pallas import tpu as pltpu
from jax.sharding import PartitionSpec as P

BLOCK = 512
MIN_GENE = 128
WINDOW = BLOCK // MIN_GENE + 1
GROUP = 4
LANES = 128
ROWS = 16
SUBLANES = 8
UNROLL = 12
VMEM_LIMIT = 56 * 1024 * 1024

smem = pl.BlockSpec(memory_space=pltpu.SMEM)
vmem = pl.BlockSpec(memory_space=pltpu.VMEM)
hbm = pl.BlockSpec(memory_space=pl.ANY)


def nt_dot(left, right):
    return lax.dot_general(
        left, right, (((1,), (1,)), ((), ())), preferred_element_type=jnp.float32
    )


def nn_dot(left, right):
    return jnp.dot(left, right, preferred_element_type=jnp.float32)


def chunk_blocks(var_count):
    total = var_count // BLOCK
    return next(n for n in (8, 6, 4, 3, 2, 1) if total % n == 0)


def window_edges(lengths, gene_count, gene, start):
    edges = [start]
    for j in range(WINDOW):
        at = gene + j
        length = lengths[jnp.minimum(at, gene_count - 1)]
        edges.append(edges[-1] + jnp.where(at < gene_count, length, 0))
    return edges


def next_window(edges, gene, base):
    start = edges[0]
    for edge in edges[1:]:
        passed = edge <= base
        gene = gene + passed.astype(jnp.int32)
        start = jnp.where(passed, edge, start)
    return gene, start


def reached(edges, base):
    position = lax.broadcasted_iota(jnp.int32, (SUBLANES, BLOCK), 1)
    return [position >= edge - base for edge in edges]


def gene_forward_kernel(
    gene_count, blocks, lengths, geno_hbm, weight_hbm, out, geno, weight, pre, sems
):
    units = weight.shape[0]
    cols = blocks * BLOCK
    chunks = geno.shape[1] // cols

    def copies(c):
        at = pl.ds(pl.multiple_of(c * cols, cols), cols)
        return (
            pltpu.make_async_copy(geno_hbm.at[:, at], geno.at[:, at], sems.at[0, c]),
            pltpu.make_async_copy(weight_hbm.at[:, at], weight.at[:, at], sems.at[1, c]),
        )

    for c in range(chunks):
        for copy in copies(c):
            copy.start()
    pre[...] = jnp.zeros_like(pre)

    def chunk(c, carry):
        gene, start = carry
        for copy in copies(c):
            copy.wait()
        for i in range(blocks):
            base = c * cols + i * BLOCK
            at = pl.ds(pl.multiple_of(base, BLOCK), BLOCK)
            edges = window_edges(lengths, gene_count, gene, start)
            marks = reached(edges, base)
            wide = weight[:, at]
            rows = []
            for j in range(WINDOW):
                mark = (marks[j] & ~marks[j + 1]).astype(jnp.float32)
                mark = jnp.concatenate([mark] * (units // SUBLANES), axis=0)
                rows.append(wide * mark.astype(wide.dtype))
            part = nt_dot(jnp.concatenate(rows, axis=0), geno[:, at])
            where = pl.ds(pl.multiple_of(gene * units, units), WINDOW * units)
            pre[where, :] += part
            gene, start = next_window(edges, gene, base + BLOCK)
        return gene, start

    lax.fori_loop(0, chunks, chunk, (jnp.int32(0), jnp.int32(0)))

    def body(i, _):
        at = pl.multiple_of(i * LANES, LANES)
        tile = jnp.concatenate(
            [pre[pl.ds(at + u, LANES // units, stride=units), :] for u in range(units)], axis=0
        )
        out[:, pl.ds(at, LANES)] = jnp.tanh(tile).T.astype(jnp.bfloat16)
        return 0

    lax.fori_loop(0, gene_count * units // LANES, body, 0, unroll=4)


def gene_forward(genotypes, gene_weight, lengths):
    samples, var_count = genotypes.shape
    units = gene_weight.shape[0]
    gene_count = lengths.shape[0]
    blocks = chunk_blocks(var_count)
    return pl.pallas_call(
        functools.partial(gene_forward_kernel, gene_count, blocks),
        out_shape=jax.ShapeDtypeStruct((samples, gene_count * units), jnp.bfloat16),
        in_specs=[smem, hbm, hbm],
        out_specs=vmem,
        scratch_shapes=[
            pltpu.VMEM(genotypes.shape, jnp.bfloat16),
            pltpu.VMEM(gene_weight.shape, jnp.bfloat16),
            pltpu.VMEM(((gene_count + WINDOW) * units, samples), jnp.float32),
            pltpu.SemaphoreType.DMA((2, var_count // (blocks * BLOCK))),
        ],
        compiler_params=pltpu.CompilerParams(vmem_limit_bytes=VMEM_LIMIT),
        cost_estimate=pl.CostEstimate(
            flops=2 * WINDOW * units * samples * var_count,
            bytes_accessed=2 * (samples + units) * var_count,
            transcendentals=gene_count * units * samples,
        ),
        name="gene_forward",
    )(lengths, genotypes, gene_weight)


def gene_backward_kernel(
    gene_count, blocks, lengths, geno_hbm, delta, out_hbm, geno, out, rows, sems
):
    units = out.shape[0]
    cols = blocks * BLOCK
    chunks = geno.shape[1] // cols

    def chunk_copy(c):
        at = pl.ds(pl.multiple_of(c * cols, cols), cols)
        return pltpu.make_async_copy(geno_hbm.at[:, at], geno.at[:, at], sems.at[0, c])

    def chunk_store(c):
        at = pl.ds(pl.multiple_of(c * cols, cols), cols)
        return pltpu.make_async_copy(out.at[:, at], out_hbm.at[:, at], sems.at[1, c])

    for c in range(chunks):
        chunk_copy(c).start()
    tail = WINDOW * units
    rows[gene_count * units :, :] = jnp.zeros((tail, rows.shape[1]), rows.dtype)

    count = LANES // units

    def body(i, _):
        at = pl.multiple_of(i * LANES, LANES)
        tile = delta[:, pl.ds(at, LANES)].astype(jnp.float32).T
        for u in range(units):
            here = pl.ds(at + u, count, stride=units)
            rows[here, :] = tile[u * count : (u + 1) * count]
        return 0

    lax.fori_loop(0, delta.shape[1] // LANES, body, 0, unroll=4)

    def chunk(c, carry):
        gene, start = carry
        chunk_copy(c).wait()
        for i in range(blocks):
            base = c * cols + i * BLOCK
            at = pl.ds(pl.multiple_of(base, BLOCK), BLOCK)
            edges = window_edges(lengths, gene_count, gene, start)
            marks = reached(edges, base)
            where = pl.ds(pl.multiple_of(gene * units, units), WINDOW * units)
            terms = nn_dot(rows[where, :].astype(jnp.bfloat16), geno[:, at])
            pieces = []
            for u in range(0, units, SUBLANES):
                total = terms[u : u + SUBLANES]
                for j in range(1, WINDOW):
                    here = j * units + u
                    total = jnp.where(marks[j], terms[here : here + SUBLANES], total)
                pieces.append(total)
            out[:, at] = jnp.concatenate(pieces, axis=0).astype(out.dtype)
            gene, start = next_window(edges, gene, base + BLOCK)
        chunk_store(c).start()
        return gene, start

    lax.fori_loop(0, chunks, chunk, (jnp.int32(0), jnp.int32(0)))
    for c in range(chunks):
        chunk_store(c).wait()


def gene_backward(genotypes, delta, lengths, units):
    samples, var_count = genotypes.shape
    gene_count = lengths.shape[0]
    blocks = chunk_blocks(var_count)
    return pl.pallas_call(
        functools.partial(gene_backward_kernel, gene_count, blocks),
        out_shape=jax.ShapeDtypeStruct((units, var_count), jnp.bfloat16),
        in_specs=[smem, hbm, vmem],
        out_specs=hbm,
        scratch_shapes=[
            pltpu.VMEM(genotypes.shape, jnp.bfloat16),
            pltpu.VMEM((units, var_count), jnp.bfloat16),
            pltpu.VMEM(((gene_count + WINDOW) * units, samples), jnp.float32),
            pltpu.SemaphoreType.DMA((2, var_count // (blocks * BLOCK))),
        ],
        compiler_params=pltpu.CompilerParams(vmem_limit_bytes=VMEM_LIMIT),
        cost_estimate=pl.CostEstimate(
            flops=2 * WINDOW * units * samples * var_count,
            bytes_accessed=4 * (samples + units) * var_count,
            transcendentals=0,
        ),
        name="gene_backward",
    )(lengths, genotypes, delta)


def lane_mask(rows, low):
    lane = lax.broadcasted_iota(jnp.int32, (rows, LANES), 1)
    return lane < LANES // 2 if low else lane >= LANES // 2


def gene_lanes(rows, tiles):
    lane = lax.broadcasted_iota(jnp.int32, (rows, LANES), 1) % tiles
    return [(lane == r).astype(jnp.float32) for r in range(tiles)]


def swap_halves(x):
    half = LANES // 2
    return jnp.concatenate([x[:, half:], x[:, :half]], axis=1)


def fold_kernel(units, which, raw, head, out, wide):
    rows = wide.shape[1]
    start = pl.multiple_of(which[0] * rows, ROWS)
    for c in range(units // 2):
        lanes = slice(c * LANES, (c + 1) * LANES)
        wide[c] = raw[pl.ds(start, rows), lanes].astype(jnp.float32)
    low = lane_mask(SUBLANES, True)

    def body(t, _):
        for c in range(units // 2):
            one = wide[c, pl.ds(t * ROWS, SUBLANES, stride=2), :]
            two = wide[c, pl.ds(t * ROWS + 1, SUBLANES, stride=2), :]
            even = jnp.where(low, one, swap_halves(two))
            odd = jnp.where(low, swap_halves(one), two)
            both = jnp.concatenate([even, odd], axis=0).astype(out.dtype)
            out[pl.ds(pl.multiple_of(t * LANES + c * ROWS, ROWS), ROWS), :] = both
        return 0

    lax.fori_loop(0, rows // ROWS, body, 0, unroll=2)
    out[out.shape[0] - head.shape[0] :, :] = head[...]


def fold_links(raw, head, which, units):
    links, width = raw.shape
    half = links // 2
    rows = half * width // LANES + head.shape[0]
    return pl.pallas_call(
        functools.partial(fold_kernel, units),
        out_shape=jax.ShapeDtypeStruct((rows, LANES), raw.dtype),
        in_specs=[smem, vmem, vmem],
        out_specs=vmem,
        scratch_shapes=[pltpu.VMEM((width // LANES, half, LANES), jnp.float32)],
        compiler_params=pltpu.CompilerParams(vmem_limit_bytes=VMEM_LIMIT),
        cost_estimate=pl.CostEstimate(flops=10**6, bytes_accessed=4 * 10**6, transcendentals=0),
        name="fold_links",
    )(which, raw, head)


def unfold_kernel(units, extra, *refs):
    parts, out, wide = refs[:-2], refs[-2], refs[-1]
    low = lane_mask(SUBLANES, True)
    links = wide.shape[1]

    def body(t, _):
        for c in range(units // 2):
            here = pl.ds(pl.multiple_of(t * LANES + c * ROWS, ROWS), ROWS)
            total = parts[0][here, :].astype(jnp.float32)
            for part in parts[1:]:
                total += part[here, :].astype(jnp.float32)
            even, odd = total[:SUBLANES], total[SUBLANES:]
            one = jnp.where(low, even, swap_halves(odd))
            two = jnp.where(low, swap_halves(even), odd)
            wide[c, pl.ds(t * ROWS, SUBLANES, stride=2), :] = one
            wide[c, pl.ds(t * ROWS + 1, SUBLANES, stride=2), :] = two
        return 0

    lax.fori_loop(0, links // ROWS, body, 0, unroll=2)
    head = sum(part[part.shape[0] - extra :, :].astype(jnp.float32) for part in parts)
    for c in range(units // 2):
        lanes = slice(c * LANES, (c + 1) * LANES)
        out[:links, lanes] = wide[c]
        line = head[c : c + 1] if c < extra // 2 else jnp.zeros((1, LANES), jnp.float32)
        out[links:, lanes] = jnp.broadcast_to(line, (SUBLANES, LANES))


def unfold_sum(parts, units, extra):
    rows = (parts[0].shape[0] - extra) // (units // 2)
    return pl.pallas_call(
        functools.partial(unfold_kernel, units, extra),
        out_shape=jax.ShapeDtypeStruct((rows + SUBLANES, units // 2 * LANES), jnp.float32),
        in_specs=[vmem] * len(parts),
        out_specs=vmem,
        scratch_shapes=[pltpu.VMEM((units // 2, rows, LANES), jnp.float32)],
        compiler_params=pltpu.CompilerParams(vmem_limit_bytes=VMEM_LIMIT),
        cost_estimate=pl.CostEstimate(flops=10**6, bytes_accessed=4 * 10**6, transcendentals=0),
        name="unfold_sum",
    )(*parts)


def link_forward_kernel(half_genes, units, place, members, slots, hidden, *refs):
    weights, outs, sums = refs[: 2 * GROUP], refs[2 * GROUP : -2], refs[-2:]
    quarter, core = place[0], place[1]
    tiles = LANES // units
    for total in sums:
        total[...] = jnp.zeros_like(total)
    keep = [k.astype(jnp.bfloat16) for k in gene_lanes(ROWS, tiles)]
    low = lane_mask(LANES, True).astype(jnp.float32).astype(jnp.bfloat16)
    high = lane_mask(LANES, False).astype(jnp.float32).astype(jnp.bfloat16)
    for piece in range(2 * GROUP):
        source = quarter ^ (piece % GROUP)
        half = core ^ (piece // GROUP)

        def body(t, _, piece=piece, source=source, half=half):
            first = half * half_genes + t * tiles
            at = pl.multiple_of(first * units, LANES)
            own = hidden[source, :, pl.ds(at, LANES)]
            upper, lower = own[:ROWS], own[ROWS:]
            left = jnp.concatenate(
                [jnp.concatenate([upper * k, lower * k], axis=1) for k in keep], axis=0
            )
            block = weights[piece][pl.ds(pl.multiple_of(t * LANES, LANES), LANES), :]
            turned = swap_halves(block)
            right = jnp.concatenate(
                [
                    jnp.concatenate([block * low, turned * low], axis=1),
                    jnp.concatenate([turned * high, block * high], axis=1),
                ],
                axis=0,
            )
            message = nn_dot(left, right)
            gene = source * (2 * half_genes) + first
            for r in range(tiles):
                for m in range(2):
                    slot = slots[members[m, gene + r]]
                    sums[m][slot] += message[
                        r * ROWS : (r + 1) * ROWS, m * LANES : (m + 1) * LANES
                    ]
            return 0

        lax.fori_loop(0, half_genes // tiles, body, 0, unroll=UNROLL)
    shard = outs[0].shape[0]
    for i, out in enumerate(outs):
        out[...] = (
            sums[0][i * shard : (i + 1) * shard] + sums[1][i * shard : (i + 1) * shard]
        ).astype(out.dtype)


def link_forward(place, members, slots, hidden, weights, shards, units):
    half_genes = hidden.shape[2] // units // 2
    slot_count = slots.shape[0]
    out = jax.ShapeDtypeStruct((slot_count // shards, ROWS, LANES), jnp.bfloat16)
    return pl.pallas_call(
        functools.partial(link_forward_kernel, half_genes, units),
        out_shape=[out] * shards,
        in_specs=[smem, smem, smem, vmem] + [vmem] * len(weights),
        out_specs=[vmem] * shards,
        scratch_shapes=[pltpu.VMEM((slot_count, ROWS, LANES), jnp.float32)] * 2,
        compiler_params=pltpu.CompilerParams(vmem_limit_bytes=VMEM_LIMIT),
        cost_estimate=pl.CostEstimate(
            flops=4 * 10**9, bytes_accessed=8 * 10**6, transcendentals=0
        ),
        name="link_forward",
    )(place, members, slots, hidden, *weights)


def link_backward_kernel(half_genes, units, far, place, members, slots, hidden, head, *refs):
    weights, deltas = refs[:GROUP], refs[GROUP : -3 if far else -4]
    out, grads, table = refs[-3:]
    quarter, core = place[0], place[1]
    tiles = LANES // units
    samples = hidden.shape[1]
    shard = deltas[0].shape[0]
    for i, delta in enumerate(deltas):
        table[i * shard : (i + 1) * shard] = delta[...]
    low = lane_mask(ROWS, True).astype(jnp.float32).astype(jnp.bfloat16)
    high = lane_mask(ROWS, False).astype(jnp.float32).astype(jnp.bfloat16)
    keep = gene_lanes(samples, tiles)
    row_gene = lax.broadcasted_iota(jnp.int32, (LANES, LANES), 0) % tiles
    lane_gene = lax.broadcasted_iota(jnp.int32, (LANES, LANES), 1) // samples
    fits = [
        (row_gene == lane_gene + i * (LANES // samples)).astype(jnp.float32)
        for i in range(tiles * samples // LANES)
    ]
    half = core ^ far
    begin = pl.multiple_of(0 if far else half * (half_genes * units), LANES)
    if not far:
        other = pl.multiple_of((1 - half) * (half_genes * units), LANES)
        out[:, :, pl.ds(other, half_genes * units)] = refs[-4][...]
    for piece in range(GROUP):
        source = quarter ^ piece

        def body(t, _, piece=piece, source=source):
            first = half * half_genes + t * tiles
            at = pl.multiple_of(first * units, LANES)
            here = pl.multiple_of(t * LANES, LANES)
            own = hidden[source, :, pl.ds(at, LANES)].astype(jnp.float32)
            gene = source * (2 * half_genes) + first
            parts = []
            for r in range(tiles):
                one = table[slots[members[0, gene + r]]]
                two = table[slots[members[1, gene + r]]]
                parts.append(one * low + swap_halves(two) * high)
                parts.append(swap_halves(one) * low + two * high)
            right = jnp.concatenate(parts, axis=0)
            wide = nt_dot(right, weights[piece][pl.ds(here, LANES), :])
            back = wide[:samples] * keep[0]
            for r in range(1, tiles):
                back += wide[r * samples : (r + 1) * samples] * keep[r]
            back = (back * (1.0 - own * own)).astype(out.dtype)
            out[source, :, pl.ds(pl.multiple_of(begin + here, LANES), LANES)] = back
            flat = jnp.concatenate([own] * (LANES // samples), axis=0).T
            left = jnp.concatenate([(flat * fit).astype(jnp.bfloat16) for fit in fits], axis=1)
            grads[piece, pl.ds(here, LANES), :] = nn_dot(left, right).astype(grads.dtype)
            return 0

        lax.fori_loop(0, half_genes // tiles, body, 0, unroll=UNROLL)
        count = head.shape[0] // (2 * GROUP)
        lines = head[pl.ds(pl.multiple_of((2 * source + half) * count, count), count), :]
        lines = jnp.concatenate([lines, jnp.zeros_like(lines)], axis=0)
        grads[piece, half_genes * units :, :] = lines.astype(grads.dtype)


def link_backward(place, members, slots, hidden, head, weights, deltas, far, units):
    group, samples, width = hidden.shape
    rows = width // 2
    extra = head.shape[0] // GROUP
    grads = jax.ShapeDtypeStruct((GROUP, rows + extra, LANES), jnp.bfloat16)
    outside = far is None
    back = jax.ShapeDtypeStruct((group, samples, rows if outside else width), jnp.bfloat16)
    more = [] if outside else [far]
    operands = [*weights, *deltas, *more]
    return pl.pallas_call(
        functools.partial(link_backward_kernel, rows // units, units, int(outside)),
        out_shape=[back, grads],
        in_specs=[smem, smem, smem] + [vmem] * (2 + len(operands)),
        out_specs=[vmem, vmem],
        scratch_shapes=[pltpu.VMEM((slots.shape[0], ROWS, LANES), jnp.bfloat16)],
        compiler_params=pltpu.CompilerParams(vmem_limit_bytes=VMEM_LIMIT),
        cost_estimate=pl.CostEstimate(
            flops=3 * 10**9, bytes_accessed=20 * 10**6, transcendentals=0
        ),
        name="link_backward",
    )(place, members, slots, hidden, head, *operands)


def on_device(
    genotypes,
    gene_weight,
    gene_lengths,
    membership,
    pathway_slot,
    pathway_weight,
    head_weight,
    cotangent,
):
    devices = lax.axis_size("genes")
    index = lax.axis_index("genes")
    core = lax.axis_index("batch")
    planes = devices // GROUP
    plane, quarter = index // GROUP, index % GROUP
    gene_count = gene_lengths.shape[0]
    units = gene_weight.shape[0]
    path_units = pathway_weight.shape[1] // units
    slot_count = pathway_slot.shape[0]
    shard = slot_count // planes
    samples = genotypes.shape[0]
    part = samples // GROUP
    in_plane = [[GROUP * z + q for q in range(GROUP)] for z in range(planes)]
    along = [[GROUP * z + q for z in range(planes)] for q in range(GROUP)]
    paired = planes == 4

    def swap_plane(x, d):
        pairs = [(GROUP * z + q, GROUP * z + (q ^ d)) for z in range(planes) for q in range(GROUP)]
        return lax.ppermute(x, "genes", pairs)

    def swap_along(x, d):
        pairs = [(GROUP * z + q, GROUP * (z ^ d) + q) for z in range(planes) for q in range(GROUP)]
        return lax.ppermute(x, "genes", pairs)

    def swap_core(x):
        return lax.ppermute(x, "batch", [(0, 1), (1, 0)])

    def spread(x, groups):
        return lax.all_to_all(
            x, "genes", split_axis=0, concat_axis=0, tiled=True, axis_index_groups=groups
        )

    def after(x, *others):
        return lax.optimization_barrier((x, *others))[0]

    with jax.named_scope("link_weights"):
        head_rows = head_weight.reshape(-1, LANES)
        mine = fold_links(pathway_weight, head_rows, core[None].astype(jnp.int32), units)
        near = [mine] + [swap_plane(mine, d) for d in range(1, GROUP)]

    with jax.named_scope("hidden"):
        hidden = gene_forward(genotypes, gene_weight, gene_lengths)
        other_raw, hidden = lax.optimization_barrier((pathway_weight, hidden))
        hidden = spread(hidden.reshape(GROUP, part, gene_count * units), in_plane)

    with jax.named_scope("link_weights"):
        other = fold_links(other_raw, head_rows, (1 - core)[None].astype(jnp.int32), units)
        far = [other] + [swap_core(x) for x in near[1:]]

    with jax.named_scope("tables"):
        place = jnp.stack([quarter, core]).astype(jnp.int32)
        members = lax.dynamic_slice_in_dim(
            membership, plane * GROUP * gene_count, GROUP * gene_count
        ).T
        slots = pathway_slot ^ (plane * shard) if paired else pathway_slot
        heads = jnp.stack([x[-head_rows.shape[0] :] for x in near])
        head = jnp.concatenate(
            [lax.dynamic_slice_in_dim(heads, quarter ^ d, 1) for d in range(GROUP)]
        )
        head = head.reshape(shard, 1, 1, path_units).astype(jnp.float32)
        cot = lax.dynamic_slice_in_dim(cotangent, quarter * part, part)
        cot = cot.reshape(part // ROWS, ROWS).T.reshape(1, ROWS, part // ROWS, 1)

    def head_step(total, head):
        count = total.shape[0]
        active = jnp.tanh(total.reshape(count, ROWS, part // ROWS, path_units))
        delta = (cot * head * (1.0 - active * active)).astype(jnp.bfloat16)
        return jnp.sum(active * cot, axis=(1, 2)), delta.reshape(count, ROWS, LANES)

    if paired:
        cuts = 2
        count = shard // cuts
        with jax.named_scope("pathway_sum"):
            sums = link_forward(
                place, members, slots, hidden, near + far, planes * cuts, units
            )
            passed = [
                sums[2 * cuts + c].astype(jnp.float32)
                + swap_along(sums[3 * cuts + c], 1).astype(jnp.float32)
                for c in range(cuts)
            ]
            passed = [x.astype(jnp.bfloat16) for x in passed]
            crossed = [swap_along(x, 2) for x in passed]
            beside = [swap_along(after(sums[cuts + c], passed[c]), 1) for c in range(cuts)]
        own, heads = [], []
        for c in range(cuts):
            with jax.named_scope("head"):
                across = after(crossed[c], own[-1]) if c else crossed[c]
                total = (
                    sums[c].astype(jnp.float32)
                    + across.astype(jnp.float32)
                    + beside[c].astype(jnp.float32)
                )
                part_sum, delta = head_step(total, head[c * count : (c + 1) * count])
                own.append(delta)
                heads.append(part_sum)
        head_part = jnp.concatenate(heads)
        with jax.named_scope("pathway_delta"):
            two = [swap_along(x, 2) for x in own]
            one = [swap_along(x, 1) for x in own]
            three = [swap_along(x, 1) for x in two]
            deltas = own + one + two + three
    else:
        with jax.named_scope("pathway_sum"):
            sums = link_forward(place, members, slots, hidden, near + far, planes, units)
            parts = spread(jnp.stack(sums), along)
            total = jnp.sum(parts.astype(jnp.float32), axis=0)
        with jax.named_scope("head"):
            head_part, delta = head_step(total, head)
        with jax.named_scope("pathway_delta"):
            every = lax.all_gather(delta, "genes", axis=0, axis_index_groups=along)
            deltas = [every[i] for i in range(planes)]

    with jax.named_scope("link_grads"):
        head_part = head_part.reshape(-1, LANES)
        extra = head_part.shape[0] // GROUP
        back, give = link_backward(
            place, members, slots, hidden, head_part, far, deltas, None, units
        )
        back, give, *deltas = lax.optimization_barrier((back, give, *deltas))
        back, keep = link_backward(
            place, members, slots, hidden, head_part, near, deltas, back, units
        )
        back = spread(back, in_plane).reshape(samples, gene_count * units)

    with jax.named_scope("grad_pathway"):
        given = swap_core(give)
        summed = [
            (keep[d].astype(jnp.float32) + given[d].astype(jnp.float32)).astype(jnp.bfloat16)
            for d in range(GROUP)
        ]
        parts = [summed[0]] + [swap_plane(summed[d], d) for d in range(1, GROUP)]

    with jax.named_scope("grad_gene"):
        rows = gene_backward(genotypes, back, gene_lengths, units)

    with jax.named_scope("grad_pathway"):
        rows, *parts = lax.optimization_barrier((rows, *parts))
        own = unfold_sum(parts, units, extra)
        theirs = swap_core(own)
        links = pathway_weight.shape[0] // 2
        first = jnp.where(core == 0, own, theirs)
        second = jnp.where(core == 0, theirs, own)
        grad_pathway = jnp.concatenate([first[:links], second[:links]], axis=0)
        width = extra // 2 * LANES
        grad_head = jnp.concatenate([first[links, :width], second[links, :width]])

    with jax.named_scope("grad_gene"):
        grad_gene = rows.astype(jnp.float32) + swap_core(rows).astype(jnp.float32)

    return (grad_gene, grad_pathway, grad_head)


def solution(mesh):
    return jax.shard_map(
        on_device,
        mesh=mesh,
        in_specs=(
            P("batch", "genes"),
            P(None, "genes"),
            P("genes"),
            P(),
            P(),
            P("genes", None),
            P("genes"),
            P("batch"),
        ),
        out_specs=(P(None, "genes"), P("genes", None), P("genes")),
        check_vma=False,
    )
```

time: 233 us -> 175 us (0.75)
  Pallas kernels: 69.6 us -> 47 us
  blocking collectives: 20.6 us -> 0 us
  local copies, waits for them, and re-layouts: 19.2 us -> 6.78 us
  starting transfers between devices: 50.2 us -> 39.1 us
  waiting for transfers between devices: 59.3 us -> 67.4 us
    ppermute x6 -> x12, waiting for transfers between devices: 29.2 us -> 44.9 us  [swap_along(): return lax.ppermute(x, 'genes', pairs)]
    all_gather x1 -> x0, blocking collectives: 12.9 us -> none  [on_device(): lax.all_gather(head_weight, 'genes', axis=0, tiled=True, axis_index_group...]
    pallas_call x3 -> x7, Pallas kernels: 51.1 us -> 38.7 us  [the longest x2 13.3 us: link_backward(): pl.pallas_call(functools.partial(link_backward_kernel, rows // units, uni...]
    ppermute x6, waiting for transfers between devices: 19 us -> 8.43 us  [swap_plane(): return lax.ppermute(x, 'genes', pairs)]
    pallas_call x1, Pallas kernels: 18.4 us -> 8.32 us  [link_forward(): pl.pallas_call(functools.partial(link_forward_kernel, half_genes, units),...]
    reshape x4 -> x1, local copies, waits for them, and re-layouts: 10.3 us -> 0.7 us  [on_device(): head_part = head_part.reshape(-1, LANES)]
    all_to_all x1 -> x0, blocking collectives: 7.68 us -> none  [spread(): lax.all_to_all(x, 'genes', split_axis=0, concat_axis=0, tiled=True, axis_...]
    ppermute x6 -> x12, starting transfers between devices: 28.8 us -> 22.5 us  [swap_along(): return lax.ppermute(x, 'genes', pairs)]
  transfers between devices with their start and end apart: 24 -> 26, of which waited for: 12 -> 15; matrix products, arithmetic and copies ran while one was open for 8% -> 8% of each run, Pallas kernels for 13% -> 17%
where the time goes in v2:
time: 175 us; the launch traced here: 173 us
  waiting for transfers between devices  67.4 us (39%)
  Pallas kernels  47 us (27%)
  starting transfers between devices  39.1 us (22%)
  other arithmetic  12.1 us (7%)
  local copies, waits for them, and re-layouts  6.78 us (4%)
    ppermute x12, waiting for transfers between devices, swap_along(): return lax.ppermute(x, 'genes', pairs)  44.9 us
    ppermute x12, starting transfers between devices, swap_along(): return lax.ppermute(x, 'genes', pairs)  22.5 us
    pallas_call x2, Pallas kernels, link_backward(): pl.pallas_call(functools.partial(link_backward_kernel, rows // units, uni...  13.3 us
    all_to_all x2, waiting for transfers between devices, spread(): lax.all_to_all(x, 'genes', split_axis=0, concat_axis=0, tiled=True, axis_...  11.9 us
    pallas_call x1, Pallas kernels, gene_forward(): pl.pallas_call(functools.partial(gene_forward_kernel, gene_count, blocks)...  10 us
    ppermute x6, waiting for transfers between devices, swap_plane(): return lax.ppermute(x, 'genes', pairs)  8.43 us
    pallas_call x1, Pallas kernels, link_forward(): pl.pallas_call(functools.partial(link_forward_kernel, half_genes, units),...  8.32 us
    ppermute x6, starting transfers between devices, swap_plane(): return lax.ppermute(x, 'genes', pairs)  7.95 us
  transfers between devices with their start and end apart: 26, of which 15 were waited for; matrix products, arithmetic and copies ran while one was open for 8% of the time, Pallas kernels for 17%

profile of v2, /device:TPU:0, one launch (start us, length us, event | category | flops | bytes accessed | tf_op | source)
XLA Modules:
  0.0 173.4 jit_solution(4421421829336177711)
XLA Ops:
  3.1 3.9 %collective-permute-start.2 = (bf16[1552,128]{1,0:T(8,128)(2,1)}, bf16[1552,128]{1,0:T(8,128)(2,1)S(1)}, u32[]{:S(2)}, u32[]{:S(2)}) collective-permute-start(bf16[1552,128]{1,0:T(8,128)(2,1)} %fold_links.2.refs_0_), channel_id=1, source_target_pairs={{0,6},{2,4},{4,2},{6,0},{8,14},{10,12},{12,10},{14,8},{16,22},{18,... | collective-permute-start | bytes 1191944 | tf_op jit(solution)/shard_map/link_weights/ppermute | solution.py:494
  7.6 10.0 %gene_forward.1 = bf16[128,3072]{1,0:T(8,128)(2,1)} custom-call(s32[192]{0:T(256)} %lengths.3, bf16[128,49152]{1,0:T(8,128)(2,1)} %geno_hbm.3, bf16[16,49152]{1,0:T(8,128)(2,1)} %weight_hbm.1), custom_call_target="tpu_custom_call" | custom-call | flops 1006632960 | bytes 14155776 | tf_op jit(solution)/shard_map/hidden/gene_forward/pallas_call | solution.py:121
  17.6 4.2 %all-to-all-start = ((bf16[4,32,3072]{2,1,0:T(8,128)(2,1)}), bf16[4,32,3072]{2,1,0:T(8,128)(2,1)S(1)}, u32[]{:S(2)}, u32[]{:S(2)}) async-start(bf16[4,32,3072]{2,1,0:T(8,128)(2,1)} %bitcast.27), calls=%async_computation | async-start | bytes 1572864 | tf_op jit(solution)/shard_map/hidden/all_to_all | solution.py:504
  27.8 5.9 %all-to-all-done.hidden = bf16[4,32,3072]{2,1,0:T(8,128)(2,1)S(1)} async-done(((bf16[4,32,3072]{2,1,0:T(8,128)(2,1)}), bf16[4,32,3072]{2,1,0:T(8,128)(2,1)S(1)}, u32[]{:S(2)}, u32[]{:S(2)}) %all-to-all-start) | async-done | bytes 786464 | tf_op jit(solution)/shard_map/hidden/all_to_all | solution.py:504
  34.8 8.3 %link_forward.1 = (bf16[64,16,128]{2,1,0:T(8,128)(2,1)}, bf16[64,16,128]{2,1,0:T(8,128)(2,1)}, bf16[64,16,128]{2,1,0:T(8,128)(2,1)}, bf16[64,16,128]{2,1,0:T(8,1...) custom-call(s32[2]{0:T(128)} %pad_add_fusion.place, ...), custom_call_target="tpu_custom_call" | custom-call | flops 4000000000 | bytes 8000000 | tf_op jit(solution)/shard_map/pathway_sum/link_forward/pallas_call | solution.py:372
  45.3 7.3 %collective-permute-done.6 = bf16[64,16,128]{2,1,0:T(8,128)(2,1)S(1)} collective-permute-done((bf16[64,16,128]{2,1,0:T(8,128)(2,1)}, bf16[64,16,128]{2,1,0:T(8,128)(2,1)S(1)}, u32[]{:S(2)}, u32[]{:S(2)}) %collective-permute-start.6) | collective-permute-done | bytes 262176 | tf_op jit(solution)/shard_map/pathway_sum/ppermute | solution.py:498
  57.9 4.2 %collective-permute-done.9 = bf16[64,16,128]{2,1,0:T(8,128)(2,1)S(1)} collective-permute-done((bf16[64,16,128]{2,1,0:T(8,128)(2,1)}, bf16[64,16,128]{2,1,0:T(8,128)(2,1)S(1)}, u32[]{:S(2)}, u32[]{:S(2)}) %collective-permute-start.9) | collective-permute-done | bytes 262176 | tf_op jit(solution)/shard_map/pathway_sum/ppermute | solution.py:498
  65.8 7.7 %collective-permute-done.8 = bf16[64,16,128]{2,1,0:T(8,128)(2,1)S(1)} collective-permute-done((bf16[64,16,128]{2,1,0:T(8,128)(2,1)}, bf16[64,16,128]{2,1,0:T(8,128)(2,1)S(1)}, u32[]{:S(2)}, u32[]{:S(2)}) %collective-permute-start.8) | collective-permute-done | bytes 262176 | tf_op jit(solution)/shard_map/pathway_sum/ppermute | solution.py:498
  73.7 5.9 %collective-permute-done.10 = bf16[64,16,128]{2,1,0:T(8,128)(2,1)S(1)} collective-permute-done((bf16[64,16,128]{2,1,0:T(8,128)(2,1)S(1)}, bf16[64,16,128]{2,1,0:T(8,128)(2,1)S(1)}, u32[]{:S(2)}, u32[]{:S(2)}) %collective-permute-start.10) | collective-permute-done | bytes 262176 | tf_op jit(solution)/shard_map/pathway_sum/ppermute | solution.py:498
  79.6 3.8 %collective-permute-done.11 = bf16[64,16,128]{2,1,0:T(8,128)(2,1)S(1)} collective-permute-done((bf16[64,16,128]{2,1,0:T(8,128)(2,1)S(1)}, bf16[64,16,128]{2,1,0:T(8,128)(2,1)S(1)}, u32[]{:S(2)}, u32[]{:S(2)}) %collective-permute-start.11) | collective-permute-done | bytes 262176 | tf_op jit(solution)/shard_map/pathway_sum/ppermute | solution.py:498
  84.0 10.5 %collective-permute-start.12 = (bf16[64,16,128]{2,1,0:T(8,128)(2,1)S(1)}, bf16[64,16,128]{2,1,0:T(8,128)(2,1)S(1)}, u32[]{:S(2)}, u32[]{:S(2)}) collective-permute-start(bf16[64,16,128]{2,1,0:T(8,128)(2,1)S(1)} %multiply_convert_fusion.1.refs_4_), channel_id=1, source_target_pairs={{0,8},{2,10},{4,12},{6,14},{8,0},{10,2},{12,4},{14,6},{16,24},{18,... | collective-permute-start | bytes 786440 | tf_op jit(solution)/shard_map/pathway_delta/ppermute | solution.py:498
  94.5 2.8 %collective-permute-start.16 = (bf16[64,16,128]{2,1,0:T(8,128)(2,1)S(1)}, bf16[64,16,128]{2,1,0:T(8,128)(2,1)S(1)}, u32[]{:S(2)}, u32[]{:S(2)}) collective-permute-start(bf16[64,16,128]{2,1,0:T(8,128)(2,1)S(1)} %collective-permute-done.14.refs_8_), channel_id=1, source_target_pairs={{0,8},{2,10},{4,12},{6,14},{8,0},{10,2},{12,4},{14,6},{16,24},{18,... | collective-permute-start | bytes 786440 | tf_op jit(solution)/shard_map/pathway_delta/ppermute | solution.py:498
  97.3 3.2 %collective-permute-done.15.refs_9_ = bf16[64,16,128]{2,1,0:T(8,128)(2,1)S(1)} collective-permute-done((bf16[64,16,128]{2,1,0:T(8,128)(2,1)S(1)}, bf16[64,16,128]{2,1,0:T(8,128)(2,1)S(1)}, u32[]{:S(2)}, u32[]{:S(2)}) %collective-permute-start.15) | collective-permute-done | bytes 262176 | tf_op jit(solution)/shard_map/pathway_delta/ppermute | solution.py:498
  103.6 5.6 %collective-permute-done.13.refs_7_ = bf16[64,16,128]{2,1,0:T(8,128)(2,1)S(1)} collective-permute-done((bf16[64,16,128]{2,1,0:T(8,128)(2,1)S(1)}, bf16[64,16,128]{2,1,0:T(8,128)(2,1)S(1)}, u32[]{:S(2)}, u32[]{:S(2)}) %collective-permute-start.13) | collective-permute-done | bytes 262176 | tf_op jit(solution)/shard_map/pathway_delta/ppermute | solution.py:498
  109.2 3.0 %collective-permute-done.16.refs_10_ = bf16[64,16,128]{2,1,0:T(8,128)(2,1)S(1)} collective-permute-done((bf16[64,16,128]{2,1,0:T(8,128)(2,1)S(1)}, bf16[64,16,128]{2,1,0:T(8,128)(2,1)S(1)}, u32[]{:S(2)}, u32[]{:S(2)}) %collective-permute-start.16) | collective-permute-done | bytes 262176 | tf_op jit(solution)/shard_map/pathway_delta/ppermute | solution.py:498
  112.2 2.8 %collective-permute-done.17.refs_11_ = bf16[64,16,128]{2,1,0:T(8,128)(2,1)S(1)} collective-permute-done((bf16[64,16,128]{2,1,0:T(8,128)(2,1)S(1)}, bf16[64,16,128]{2,1,0:T(8,128)(2,1)S(1)}, u32[]{:S(2)}, u32[]{:S(2)}) %collective-permute-start.17) | collective-permute-done | bytes 262176 | tf_op jit(solution)/shard_map/pathway_delta/ppermute | solution.py:498
  115.7 6.4 %link_backward.2 = (bf16[4,32,1536]{2,1,0:T(8,128)(2,1)}, bf16[4,1552,128]{2,1,0:T(8,128)(2,1)}) custom-call(s32[2]{0:T(128)} %pad_add_fusion.place, s32[2,768]{1,0:T(2,128)} %dynamic-slice_bitcast_fusion.members, s32[512]{0:T(512)} %broadcast_xor_fusion.slots, bf16[4,32,3072]{2,1,0:T(8,128)(2,1)} %copy-done.4, f32[64,128]{1,0:T(8,128)} %reshape.72.head, ...), custom_call_target="tpu_custom_call" | custom-call | flops 3000000000 | bytes 20000000 | tf_op jit(solution)/shard_map/link_grads/link_backward/pallas_call | solution.py:452
  122.2 6.9 %link_backward.3 = (bf16[4,32,3072]{2,1,0:T(8,128)(2,1)}, bf16[4,1552,128]{2,1,0:T(8,128)(2,1)}) custom-call(s32[2]{0:T(128)} %pad_add_fusion.place, s32[2,768]{1,0:T(2,128)} %dynamic-slice_bitcast_fusion.members, s32[512]{0:T(512)} %broadcast_xor_fusion.slots, bf16[4,32,3072]{2,1,0:T(8,128)(2,1)} %copy-done.4, f32[64,128]{1,0:T(8,128)} %reshape.72.head, ...), custom_call_target="tpu_custom_call" | custom-call | flops 3000000000 | bytes 20000000 | tf_op jit(solution)/shard_map/link_grads/link_backward/pallas_call | solution.py:452
  129.1 3.5 %all-to-all-start.1 = ((bf16[4,32,3072]{2,1,0:T(8,128)(2,1)}), bf16[4,32,3072]{2,1,0:T(8,128)(2,1)S(1)}, u32[]{:S(2)}, u32[]{:S(2)}) async-start(bf16[4,32,3072]{2,1,0:T(8,128)(2,1)} %get-tuple-element.59), calls=%async_computation.1 | async-start | bytes 1572864 | tf_op jit(solution)/shard_map/link_grads/all_to_all | solution.py:504
  135.3 2.9 %collective-permute-start.21 = (bf16[1552,128]{1,0:T(8,128)(2,1)}, bf16[1552,128]{1,0:T(8,128)(2,1)S(1)}, u32[]{:S(2)}, u32[]{:S(2)}) collective-permute-start(bf16[1552,128]{1,0:T(8,128)(2,1)} %get-tuple-element.69), channel_id=1, source_target_pairs={{0,6},{2,4},{4,2},{6,0},{8,14},{10,12},{12,10},{14,8},{16,22},{18,... | collective-permute-start | bytes 1191944 | tf_op jit(solution)/shard_map/grad_pathway/ppermute | solution.py:494
  138.7 6.0 %all-to-all-done.1 = bf16[4,32,3072]{2,1,0:T(8,128)(2,1)S(1)} async-done(((bf16[4,32,3072]{2,1,0:T(8,128)(2,1)}), bf16[4,32,3072]{2,1,0:T(8,128)(2,1)S(1)}, u32[]{:S(2)}, u32[]{:S(2)}) %all-to-all-start.1) | async-done | bytes 786464 | tf_op jit(solution)/shard_map/link_grads/all_to_all | solution.py:504
  145.6 7.4 %gene_backward.1 = bf16[16,49152]{1,0:T(8,128)(2,1)} custom-call(s32[192]{0:T(256)} %lengths.3, bf16[128,49152]{1,0:T(8,128)(2,1)} %geno_hbm.3, bf16[128,3072]{1,0:T(8,128)(2,1)} %bitcast.28), custom_call_target="tpu_custom_call" | custom-call | flops 1006632960 | bytes 28311552 | tf_op jit(solution)/shard_map/grad_gene/gene_backward/pallas_call | solution.py:205
  154.2 7.3 %collective-permute-done.20.refs_2_ = bf16[1552,128]{1,0:T(8,128)(2,1)S(1)} collective-permute-done((bf16[1552,128]{1,0:T(8,128)(2,1)S(1)}, bf16[1552,128]{1,0:T(8,128)(2,1)S(1)}, u32[]{:S(2)}, u32[]{:S(2)}) %collective-permute-start.20) | collective-permute-done | bytes 397344 | tf_op jit(solution)/shard_map/grad_pathway/ppermute | solution.py:494
  162.4 3.0 %unfold_sum.1 = f32[200,1024]{1,0:T(8,128)} custom-call(bf16[1552,128]{1,0:T(8,128)(2,1)} %get-tuple-element.63.refs_0_, bf16[1552,128]{1,0:T(8,128)(2,1)} %copy-done.7, bf16[1552,128]{1,0:T(8,128)(2,1)} %copy-done.6, bf16[1552,128]{1,0:T(8,128)(2,1)} %copy-done.5), custom_call_target="tpu_custom_call" | custom-call | flops 1000000 | bytes 4000000 | tf_op jit(solution)/shard_map/grad_pathway/unfold_sum/pallas_call | solution.py:308
  (127 shorter events, 39.8 us)
Async XLA Ops:
  3.1 24.1 %collective-permute-start.2 = (bf16[1552,128]{1,0:T(8,128)(2,1)}, bf16[1552,128]{1,0:T(8,128)(2,1)S(1)}, u32[]{:S(2)}, u32[]{:S(2)}) collective-permute-start(bf16[1552,128]{1,0:T(8,128)(2,1)} %fold_links.2.refs_0_), channel_id=1, source_target_pairs={{0,6},{2,4},{4,2},{6,0},{8,14},{10,12},{12,10},{14,8},{16,22},{18,... | collective-permute-start | bytes 1191944 | tf_op jit(solution)/shard_map/link_weights/ppermute | solution.py:494
  7.0 20.2 %collective-permute-start.1 = (bf16[1552,128]{1,0:T(8,128)(2,1)}, bf16[1552,128]{1,0:T(8,128)(2,1)S(1)}, u32[]{:S(2)}, u32[]{:S(2)}) collective-permute-start(bf16[1552,128]{1,0:T(8,128)(2,1)} %fold_links.2.refs_0_), channel_id=1, source_target_pairs={{0,4},{2,6},{4,0},{6,2},{8,12},{10,14},{12,8},{14,10},{16,20},{18,... | collective-permute-start | bytes 1191944 | tf_op jit(solution)/shard_map/link_weights/ppermute | solution.py:494
  7.5 20.2 %collective-permute-start = (bf16[1552,128]{1,0:T(8,128)(2,1)}, bf16[1552,128]{1,0:T(8,128)(2,1)S(1)}, u32[]{:S(2)}, u32[]{:S(2)}) collective-permute-start(bf16[1552,128]{1,0:T(8,128)(2,1)} %fold_links.2.refs_0_), channel_id=1, source_target_pairs={{0,2},{2,0},{4,6},{6,4},{8,10},{10,8},{12,14},{14,12},{16,18},{18,... | collective-permute-start | bytes 1191944 | tf_op jit(solution)/shard_map/link_weights/ppermute | solution.py:494
  17.6 16.1 %all-to-all-start = ((bf16[4,32,3072]{2,1,0:T(8,128)(2,1)}), bf16[4,32,3072]{2,1,0:T(8,128)(2,1)S(1)}, u32[]{:S(2)}, u32[]{:S(2)}) async-start(bf16[4,32,3072]{2,1,0:T(8,128)(2,1)} %bitcast.27), calls=%async_computation | async-start | bytes 1572864 | tf_op jit(solution)/shard_map/hidden/all_to_all | solution.py:504
  27.2 6.5 %collective-permute-start.5 = (bf16[1552,128]{1,0:T(8,128)(2,1)S(1)}, bf16[1552,128]{1,0:T(8,128)(2,1)S(1)}, u32[]{:S(2)}, u32[]{:S(2)}) collective-permute-start(bf16[1552,128]{1,0:T(8,128)(2,1)S(1)} %collective-permute-done.2.refs_3_), channel_id=1, source_target_pairs={{0,1},{1,0},{2,3},{3,2},{4,5},{5,4},{6,7},{7,6},{8,9},{9,8},{10,11... | collective-permute-start | bytes 1191944 | tf_op jit(solution)/shard_map/link_weights/ppermute | solution.py:501
  27.2 6.5 %collective-permute-start.4 = (bf16[1552,128]{1,0:T(8,128)(2,1)S(1)}, bf16[1552,128]{1,0:T(8,128)(2,1)S(1)}, u32[]{:S(2)}, u32[]{:S(2)}) collective-permute-start(bf16[1552,128]{1,0:T(8,128)(2,1)S(1)} %collective-permute-done.1.refs_2_), channel_id=1, source_target_pairs={{0,1},{1,0},{2,3},{3,2},{4,5},{5,4},{6,7},{7,6},{8,9},{9,8},{10,11... | collective-permute-start | bytes 1191944 | tf_op jit(solution)/shard_map/link_weights/ppermute | solution.py:501
  43.2 9.5 %collective-permute-start.6 = (bf16[64,16,128]{2,1,0:T(8,128)(2,1)}, bf16[64,16,128]{2,1,0:T(8,128)(2,1)S(1)}, u32[]{:S(2)}, u32[]{:S(2)}) collective-permute-start(bf16[64,16,128]{2,1,0:T(8,128)(2,1)} %get-tuple-element.39), channel_id=1, source_target_pairs={{0,8},{2,10},{4,12},{6,14},{8,0},{10,2},{12,4},{14,6},{16,24},{18,... | collective-permute-start | bytes 786440 | tf_op jit(solution)/shard_map/pathway_sum/ppermute | solution.py:498
  44.8 17.4 %collective-permute-start.9 = (bf16[64,16,128]{2,1,0:T(8,128)(2,1)}, bf16[64,16,128]{2,1,0:T(8,128)(2,1)S(1)}, u32[]{:S(2)}, u32[]{:S(2)}) collective-permute-start(bf16[64,16,128]{2,1,0:T(8,128)(2,1)} %get-tuple-element.44), channel_id=1, source_target_pairs={{0,8},{2,10},{4,12},{6,14},{8,0},{10,2},{12,4},{14,6},{16,24},{18,... | collective-permute-start | bytes 786440 | tf_op jit(solution)/shard_map/pathway_sum/ppermute | solution.py:498
  53.7 19.7 %collective-permute-start.7 = (bf16[64,16,128]{2,1,0:T(8,128)(2,1)S(1)}, bf16[64,16,128]{2,1,0:T(8,128)(2,1)S(1)}, u32[]{:S(2)}, u32[]{:S(2)}) collective-permute-start(bf16[64,16,128]{2,1,0:T(8,128)(2,1)S(1)} %add_convert_fusion.5), channel_id=1, source_target_pairs={{0,16},{2,18},{4,20},{6,22},{8,24},{10,26},{12,28},{14,30},{16,0},... | collective-permute-start | bytes 786440 | tf_op jit(solution)/shard_map/pathway_sum/ppermute | solution.py:498
  56.4 17.1 %collective-permute-start.8 = (bf16[64,16,128]{2,1,0:T(8,128)(2,1)}, bf16[64,16,128]{2,1,0:T(8,128)(2,1)S(1)}, u32[]{:S(2)}, u32[]{:S(2)}) collective-permute-start(bf16[64,16,128]{2,1,0:T(8,128)(2,1)} %get-tuple-element.41), channel_id=1, source_target_pairs={{0,8},{2,10},{4,12},{6,14},{8,0},{10,2},{12,4},{14,6},{16,24},{18,... | collective-permute-start | bytes 786440 | tf_op jit(solution)/shard_map/pathway_sum/ppermute | solution.py:498
  63.2 16.4 %collective-permute-start.10 = (bf16[64,16,128]{2,1,0:T(8,128)(2,1)S(1)}, bf16[64,16,128]{2,1,0:T(8,128)(2,1)S(1)}, u32[]{:S(2)}, u32[]{:S(2)}) collective-permute-start(bf16[64,16,128]{2,1,0:T(8,128)(2,1)S(1)} %add_convert_fusion.4), channel_id=1, source_target_pairs={{0,16},{2,18},{4,20},{6,22},{8,24},{10,26},{12,28},{14,30},{16,0},... | collective-permute-start | bytes 786440 | tf_op jit(solution)/shard_map/pathway_sum/ppermute | solution.py:498
  63.3 20.1 %collective-permute-start.11 = (bf16[64,16,128]{2,1,0:T(8,128)(2,1)S(1)}, bf16[64,16,128]{2,1,0:T(8,128)(2,1)S(1)}, u32[]{:S(2)}, u32[]{:S(2)}) collective-permute-start(bf16[64,16,128]{2,1,0:T(8,128)(2,1)S(1)} %copy-done.18), channel_id=1, source_target_pairs={{0,8},{2,10},{4,12},{6,14},{8,0},{10,2},{12,4},{14,6},{16,24},{18,... | collective-permute-start | bytes 786440 | tf_op jit(solution)/shard_map/pathway_sum/ppermute | solution.py:498
  73.6 20.9 %collective-permute-start.14 = (bf16[64,16,128]{2,1,0:T(8,128)(2,1)S(1)}, bf16[64,16,128]{2,1,0:T(8,128)(2,1)S(1)}, u32[]{:S(2)}, u32[]{:S(2)}) collective-permute-start(bf16[64,16,128]{2,1,0:T(8,128)(2,1)S(1)} %multiply_convert_fusion.1.refs_4_), channel_id=1, source_target_pairs={{0,16},{2,18},{4,20},{6,22},{8,24},{10,26},{12,28},{14,30},{16,0},... | collective-permute-start | bytes 786440 | tf_op jit(solution)/shard_map/pathway_delta/ppermute | solution.py:498
  83.9 16.7 %collective-permute-start.15 = (bf16[64,16,128]{2,1,0:T(8,128)(2,1)S(1)}, bf16[64,16,128]{2,1,0:T(8,128)(2,1)S(1)}, u32[]{:S(2)}, u32[]{:S(2)}) collective-permute-start(bf16[64,16,128]{2,1,0:T(8,128)(2,1)S(1)} %get-tuple-element.51.refs_5_), channel_id=1, source_target_pairs={{0,16},{2,18},{4,20},{6,22},{8,24},{10,26},{12,28},{14,30},{16,0},... | collective-permute-start | bytes 786440 | tf_op jit(solution)/shard_map/pathway_delta/ppermute | solution.py:498
  84.0 19.6 %collective-permute-start.12 = (bf16[64,16,128]{2,1,0:T(8,128)(2,1)S(1)}, bf16[64,16,128]{2,1,0:T(8,128)(2,1)S(1)}, u32[]{:S(2)}, u32[]{:S(2)}) collective-permute-start(bf16[64,16,128]{2,1,0:T(8,128)(2,1)S(1)} %multiply_convert_fusion.1.refs_4_), channel_id=1, source_target_pairs={{0,8},{2,10},{4,12},{6,14},{8,0},{10,2},{12,4},{14,6},{16,24},{18,... | collective-permute-start | bytes 786440 | tf_op jit(solution)/shard_map/pathway_delta/ppermute | solution.py:498
  94.5 14.7 %collective-permute-start.13 = (bf16[64,16,128]{2,1,0:T(8,128)(2,1)S(1)}, bf16[64,16,128]{2,1,0:T(8,128)(2,1)S(1)}, u32[]{:S(2)}, u32[]{:S(2)}) collective-permute-start(bf16[64,16,128]{2,1,0:T(8,128)(2,1)S(1)} %get-tuple-element.51.refs_5_), channel_id=1, source_target_pairs={{0,8},{2,10},{4,12},{6,14},{8,0},{10,2},{12,4},{14,6},{16,24},{18,... | collective-permute-start | bytes 786440 | tf_op jit(solution)/shard_map/pathway_delta/ppermute | solution.py:498
  94.5 17.7 %collective-permute-start.16 = (bf16[64,16,128]{2,1,0:T(8,128)(2,1)S(1)}, bf16[64,16,128]{2,1,0:T(8,128)(2,1)S(1)}, u32[]{:S(2)}, u32[]{:S(2)}) collective-permute-start(bf16[64,16,128]{2,1,0:T(8,128)(2,1)S(1)} %collective-permute-done.14.refs_8_), channel_id=1, source_target_pairs={{0,8},{2,10},{4,12},{6,14},{8,0},{10,2},{12,4},{14,6},{16,24},{18,... | collective-permute-start | bytes 786440 | tf_op jit(solution)/shard_map/pathway_delta/ppermute | solution.py:498
  100.5 14.4 %collective-permute-start.17 = (bf16[64,16,128]{2,1,0:T(8,128)(2,1)S(1)}, bf16[64,16,128]{2,1,0:T(8,128)(2,1)S(1)}, u32[]{:S(2)}, u32[]{:S(2)}) collective-permute-start(bf16[64,16,128]{2,1,0:T(8,128)(2,1)S(1)} %collective-permute-done.15.refs_9_), channel_id=1, source_target_pairs={{0,8},{2,10},{4,12},{6,14},{8,0},{10,2},{12,4},{14,6},{16,24},{18,... | collective-permute-start | bytes 786440 | tf_op jit(solution)/shard_map/pathway_delta/ppermute | solution.py:498
  122.2 10.4 %collective-permute-start.18 = (bf16[4,1552,128]{2,1,0:T(8,128)(2,1)}, bf16[4,1552,128]{2,1,0:T(8,128)(2,1)S(1)}, u32[]{:S(2)}, u32[]{:S(2)}) collective-permute-start(bf16[4,1552,128]{2,1,0:T(8,128)(2,1)} %get-tuple-element.61), channel_id=1, source_target_pairs={{0,1},{1,0},{2,3},{3,2},{4,5},{5,4},{6,7},{7,6},{8,9},{9,8},{10,11... | collective-permute-start | bytes 4767752 | tf_op jit(solution)/shard_map/grad_pathway/ppermute | solution.py:501
  129.1 15.7 %all-to-all-start.1 = ((bf16[4,32,3072]{2,1,0:T(8,128)(2,1)}), bf16[4,32,3072]{2,1,0:T(8,128)(2,1)S(1)}, u32[]{:S(2)}, u32[]{:S(2)}) async-start(bf16[4,32,3072]{2,1,0:T(8,128)(2,1)} %get-tuple-element.59), calls=%async_computation.1 | async-start | bytes 1572864 | tf_op jit(solution)/shard_map/link_grads/all_to_all | solution.py:504
  135.3 18.9 %collective-permute-start.21 = (bf16[1552,128]{1,0:T(8,128)(2,1)}, bf16[1552,128]{1,0:T(8,128)(2,1)S(1)}, u32[]{:S(2)}, u32[]{:S(2)}) collective-permute-start(bf16[1552,128]{1,0:T(8,128)(2,1)} %get-tuple-element.69), channel_id=1, source_target_pairs={{0,6},{2,4},{4,2},{6,0},{8,14},{10,12},{12,10},{14,8},{16,22},{18,... | collective-permute-start | bytes 1191944 | tf_op jit(solution)/shard_map/grad_pathway/ppermute | solution.py:494
  138.1 23.4 %collective-permute-start.20 = (bf16[1552,128]{1,0:T(8,128)(2,1)S(1)}, bf16[1552,128]{1,0:T(8,128)(2,1)S(1)}, u32[]{:S(2)}, u32[]{:S(2)}) collective-permute-start(bf16[1552,128]{1,0:T(8,128)(2,1)S(1)} %get-tuple-element.70), channel_id=1, source_target_pairs={{0,4},{2,6},{4,0},{6,2},{8,12},{10,14},{12,8},{14,10},{16,20},{18,... | collective-permute-start | bytes 1191944 | tf_op jit(solution)/shard_map/grad_pathway/ppermute | solution.py:494
  138.7 22.8 %collective-permute-start.19 = (bf16[1552,128]{1,0:T(8,128)(2,1)S(1)}, bf16[1552,128]{1,0:T(8,128)(2,1)S(1)}, u32[]{:S(2)}, u32[]{:S(2)}) collective-permute-start(bf16[1552,128]{1,0:T(8,128)(2,1)S(1)} %get-tuple-element.71), channel_id=1, source_target_pairs={{0,2},{2,0},{4,6},{6,4},{8,10},{10,8},{12,14},{14,12},{16,18},{18,... | collective-permute-start | bytes 1191944 | tf_op jit(solution)/shard_map/grad_pathway/ppermute | solution.py:494
  162.3 9.1 %collective-permute-start.22 = (bf16[16,49152]{1,0:T(8,128)(2,1)}, bf16[16,49152]{1,0:T(8,128)(2,1)S(1)}, u32[]{:S(2)}, u32[]{:S(2)}) collective-permute-start(bf16[16,49152]{1,0:T(8,128)(2,1)} %gene_backward.1), channel_id=1, source_target_pairs={{0,1},{1,0},{2,3},{3,2},{4,5},{5,4},{6,7},{7,6},{8,9},{9,8},{10,11... | collective-permute-start | bytes 4718600 | tf_op jit(solution)/shard_map/grad_gene/ppermute | solution.py:501
  (27 other events, 288.1 us)

commit v3 on v2

--- a/solution.py
+++ b/solution.py
@@ -15,7 +15,7 @@
 ROWS = 16
 SUBLANES = 8
 UNROLL = 12
-VMEM_LIMIT = 56 * 1024 * 1024
+MIB = 1024 * 1024
 
 smem = pl.BlockSpec(memory_space=pltpu.SMEM)
 vmem = pl.BlockSpec(memory_space=pltpu.VMEM)
@@ -32,9 +32,9 @@
     return jnp.dot(left, right, preferred_element_type=jnp.float32)
 
 
-def chunk_blocks(var_count):
+def chunk_blocks(var_count, most):
     total = var_count // BLOCK
-    return next(n for n in (8, 6, 4, 3, 2, 1) if total % n == 0)
+    return next(n for n in range(most, 0, -1) if total % n == 0)
 
 
 def window_edges(lengths, gene_count, gene, start):
@@ -117,7 +117,7 @@
     samples, var_count = genotypes.shape
     units = gene_weight.shape[0]
     gene_count = lengths.shape[0]
-    blocks = chunk_blocks(var_count)
+    blocks = chunk_blocks(var_count, 16)
     return pl.pallas_call(
         functools.partial(gene_forward_kernel, gene_count, blocks),
         out_shape=jax.ShapeDtypeStruct((samples, gene_count * units), jnp.bfloat16),
@@ -129,7 +129,7 @@
             pltpu.VMEM(((gene_count + WINDOW) * units, samples), jnp.float32),
             pltpu.SemaphoreType.DMA((2, var_count // (blocks * BLOCK))),
         ],
-        compiler_params=pltpu.CompilerParams(vmem_limit_bytes=VMEM_LIMIT),
+        compiler_params=pltpu.CompilerParams(vmem_limit_bytes=52 * MIB),
         cost_estimate=pl.CostEstimate(
             flops=2 * WINDOW * units * samples * var_count,
             bytes_accessed=2 * (samples + units) * var_count,
@@ -201,7 +201,7 @@
 def gene_backward(genotypes, delta, lengths, units):
     samples, var_count = genotypes.shape
     gene_count = lengths.shape[0]
-    blocks = chunk_blocks(var_count)
+    blocks = chunk_blocks(var_count, 8)
     return pl.pallas_call(
         functools.partial(gene_backward_kernel, gene_count, blocks),
         out_shape=jax.ShapeDtypeStruct((units, var_count), jnp.bfloat16),
@@ -213,7 +213,7 @@
             pltpu.VMEM(((gene_count + WINDOW) * units, samples), jnp.float32),
             pltpu.SemaphoreType.DMA((2, var_count // (blocks * BLOCK))),
         ],
-        compiler_params=pltpu.CompilerParams(vmem_limit_bytes=VMEM_LIMIT),
+        compiler_params=pltpu.CompilerParams(vmem_limit_bytes=52 * MIB),
         cost_estimate=pl.CostEstimate(
             flops=2 * WINDOW * units * samples * var_count,
             bytes_accessed=4 * (samples + units) * var_count,
@@ -270,7 +270,7 @@
         in_specs=[smem, vmem, vmem],
         out_specs=vmem,
         scratch_shapes=[pltpu.VMEM((width // LANES, half, LANES), jnp.float32)],
-        compiler_params=pltpu.CompilerParams(vmem_limit_bytes=VMEM_LIMIT),
+        compiler_params=pltpu.CompilerParams(vmem_limit_bytes=8 * MIB),
         cost_estimate=pl.CostEstimate(flops=10**6, bytes_accessed=4 * 10**6, transcendentals=0),
         name="fold_links",
     )(which, raw, head)
@@ -296,6 +296,7 @@
 
     lax.fori_loop(0, links // ROWS, body, 0, unroll=2)
     head = sum(part[part.shape[0] - extra :, :].astype(jnp.float32) for part in parts)
+    head = head[: extra // 2] + head[extra // 2 :]
     for c in range(units // 2):
         lanes = slice(c * LANES, (c + 1) * LANES)
         out[:links, lanes] = wide[c]
@@ -311,7 +312,7 @@
         in_specs=[vmem] * len(parts),
         out_specs=vmem,
         scratch_shapes=[pltpu.VMEM((units // 2, rows, LANES), jnp.float32)],
-        compiler_params=pltpu.CompilerParams(vmem_limit_bytes=VMEM_LIMIT),
+        compiler_params=pltpu.CompilerParams(vmem_limit_bytes=10 * MIB),
         cost_estimate=pl.CostEstimate(flops=10**6, bytes_accessed=4 * 10**6, transcendentals=0),
         name="unfold_sum",
     )(*parts)
@@ -375,7 +376,7 @@
         in_specs=[smem, smem, smem, vmem] + [vmem] * len(weights),
         out_specs=[vmem] * shards,
         scratch_shapes=[pltpu.VMEM((slot_count, ROWS, LANES), jnp.float32)] * 2,
-        compiler_params=pltpu.CompilerParams(vmem_limit_bytes=VMEM_LIMIT),
+        compiler_params=pltpu.CompilerParams(vmem_limit_bytes=slot_count * ROWS * LANES * 10 + 8 * MIB),
         cost_estimate=pl.CostEstimate(
             flops=4 * 10**9, bytes_accessed=8 * 10**6, transcendentals=0
         ),
@@ -383,9 +384,9 @@
     )(place, members, slots, hidden, *weights)
 
 
-def link_backward_kernel(half_genes, units, far, place, members, slots, hidden, head, *refs):
-    weights, deltas = refs[:GROUP], refs[GROUP : -3 if far else -4]
-    out, grads, table = refs[-3:]
+def link_backward_kernel(half_genes, units, place, members, slots, hidden, head, *refs):
+    weights, deltas = refs[: 2 * GROUP], refs[2 * GROUP : -4]
+    out, keeps, gives, table = refs[-4:]
     quarter, core = place[0], place[1]
     tiles = LANES // units
     samples = hidden.shape[1]
@@ -401,15 +402,13 @@
         (row_gene == lane_gene + i * (LANES // samples)).astype(jnp.float32)
         for i in range(tiles * samples // LANES)
     ]
-    half = core ^ far
-    begin = pl.multiple_of(0 if far else half * (half_genes * units), LANES)
-    if not far:
-        other = pl.multiple_of((1 - half) * (half_genes * units), LANES)
-        out[:, :, pl.ds(other, half_genes * units)] = refs[-4][...]
-    for piece in range(GROUP):
+    for index in range(2 * GROUP):
+        piece = index % GROUP
+        grads = gives if index // GROUP else keeps
         source = quarter ^ piece
-
-        def body(t, _, piece=piece, source=source):
+        half = core ^ (index // GROUP)
+
+        def body(t, _, index=index, piece=piece, grads=grads, source=source, half=half):
             first = half * half_genes + t * tiles
             at = pl.multiple_of(first * units, LANES)
             here = pl.multiple_of(t * LANES, LANES)
@@ -422,12 +421,11 @@
                 parts.append(one * low + swap_halves(two) * high)
                 parts.append(swap_halves(one) * low + two * high)
             right = jnp.concatenate(parts, axis=0)
-            wide = nt_dot(right, weights[piece][pl.ds(here, LANES), :])
+            wide = nt_dot(right, weights[index][pl.ds(here, LANES), :])
             back = wide[:samples] * keep[0]
             for r in range(1, tiles):
                 back += wide[r * samples : (r + 1) * samples] * keep[r]
-            back = (back * (1.0 - own * own)).astype(out.dtype)
-            out[source, :, pl.ds(pl.multiple_of(begin + here, LANES), LANES)] = back
+            out[source, :, pl.ds(at, LANES)] = (back * (1.0 - own * own)).astype(out.dtype)
             flat = jnp.concatenate([own] * (LANES // samples), axis=0).T
             left = jnp.concatenate([(flat * fit).astype(jnp.bfloat16) for fit in fits], axis=1)
             grads[piece, pl.ds(here, LANES), :] = nn_dot(left, right).astype(grads.dtype)
@@ -436,28 +434,25 @@
         lax.fori_loop(0, half_genes // tiles, body, 0, unroll=UNROLL)
         count = head.shape[0] // (2 * GROUP)
         lines = head[pl.ds(pl.multiple_of((2 * source + half) * count, count), count), :]
-        lines = jnp.concatenate([lines, jnp.zeros_like(lines)], axis=0)
+        coarse = lines.astype(grads.dtype).astype(jnp.float32)
+        lines = jnp.concatenate([coarse, lines - coarse], axis=0)
         grads[piece, half_genes * units :, :] = lines.astype(grads.dtype)
 
 
-def link_backward(place, members, slots, hidden, head, weights, deltas, far, units):
-    group, samples, width = hidden.shape
-    rows = width // 2
+def link_backward(place, members, slots, hidden, head, weights, deltas, units):
+    rows = hidden.shape[2] // 2
     extra = head.shape[0] // GROUP
     grads = jax.ShapeDtypeStruct((GROUP, rows + extra, LANES), jnp.bfloat16)
-    outside = far is None
-    back = jax.ShapeDtypeStruct((group, samples, rows if outside else width), jnp.bfloat16)
-    more = [] if outside else [far]
-    operands = [*weights, *deltas, *more]
+    operands = [*weights, *deltas]
     return pl.pallas_call(
-        functools.partial(link_backward_kernel, rows // units, units, int(outside)),
-        out_shape=[back, grads],
+        functools.partial(link_backward_kernel, rows // units, units),
+        out_shape=[jax.ShapeDtypeStruct(hidden.shape, jnp.bfloat16), grads, grads],
         in_specs=[smem, smem, smem] + [vmem] * (2 + len(operands)),
-        out_specs=[vmem, vmem],
+        out_specs=[vmem] * 3,
         scratch_shapes=[pltpu.VMEM((slots.shape[0], ROWS, LANES), jnp.bfloat16)],
-        compiler_params=pltpu.CompilerParams(vmem_limit_bytes=VMEM_LIMIT),
+        compiler_params=pltpu.CompilerParams(vmem_limit_bytes=56 * MIB),
         cost_estimate=pl.CostEstimate(
-            flops=3 * 10**9, bytes_accessed=20 * 10**6, transcendentals=0
+            flops=6 * 10**9, bytes_accessed=20 * 10**6, transcendentals=0
         ),
         name="link_backward",
     )(place, members, slots, hidden, head, *operands)
@@ -589,12 +584,8 @@
     with jax.named_scope("link_grads"):
         head_part = head_part.reshape(-1, LANES)
         extra = head_part.shape[0] // GROUP
-        back, give = link_backward(
-            place, members, slots, hidden, head_part, far, deltas, None, units
-        )
-        back, give, *deltas = lax.optimization_barrier((back, give, *deltas))
-        back, keep = link_backward(
-            place, members, slots, hidden, head_part, near, deltas, back, units
+        back, keep, give = link_backward(
+            place, members, slots, hidden, head_part, near + far, deltas, units
         )
         back = spread(back, in_plane).reshape(samples, gene_count * units)
 
@@ -612,16 +603,14 @@
     with jax.named_scope("grad_pathway"):
         rows, *parts = lax.optimization_barrier((rows, *parts))
         own = unfold_sum(parts, units, extra)
-        theirs = swap_core(own)
+        grad_gene = rows.astype(jnp.float32) + swap_core(rows).astype(jnp.float32)
+        theirs, grad_gene = lax.optimization_barrier((swap_core(own), grad_gene))
         links = pathway_weight.shape[0] // 2
         first = jnp.where(core == 0, own, theirs)
         second = jnp.where(core == 0, theirs, own)
         grad_pathway = jnp.concatenate([first[:links], second[:links]], axis=0)
         width = extra // 2 * LANES
         grad_head = jnp.concatenate([first[links, :width], second[links, :width]])
-
-    with jax.named_scope("grad_gene"):
-        grad_gene = rows.astype(jnp.float32) + swap_core(rows).astype(jnp.float32)
 
     return (grad_gene, grad_pathway, grad_head)
 

time: 175 us -> 168 us (0.960)
  waiting for transfers between devices: 67.4 us -> 83 us
  Pallas kernels: 47 us -> 35.4 us
  starting transfers between devices: 39.1 us -> 29.7 us
  other arithmetic: 12.1 us -> 9.53 us
  local copies, waits for them, and re-layouts: 6.78 us -> 8.78 us
    ppermute x12, waiting for transfers between devices: 44.9 us -> 56.6 us  [swap_along(): return lax.ppermute(x, 'genes', pairs)]
    ppermute x12, starting transfers between devices: 22.5 us -> 13.2 us  [swap_along(): return lax.ppermute(x, 'genes', pairs)]
    ppermute x6, waiting for transfers between devices: 8.43 us -> 13 us  [swap_plane(): return lax.ppermute(x, 'genes', pairs)]
    pallas_call x2, Pallas kernels: 4.91 us -> 1.16 us  [fold_links(): pl.pallas_call(functools.partial(fold_kernel, units), out_shape=jax.Shape...]
    pallas_call x2 -> x1, Pallas kernels: 13.3 us -> 10.3 us  [link_backward(): pl.pallas_call(functools.partial(link_backward_kernel, rows // units, uni...]
    unnamed x50 -> x58, local copies, waits for them, and re-layouts: 3.64 us -> 6.25 us
    pallas_call x1, Pallas kernels: 2.99 us -> 0.73 us  [unfold_sum(): pl.pallas_call(functools.partial(unfold_kernel, units, extra), out_shape=...]
    convert_element_type x2, other arithmetic: 2.1 us -> 0.14 us  [on_device(): passed = [x.astype(jnp.bfloat16) for x in passed]]
  transfers between devices with their start and end apart: 26 -> 26, of which waited for: 15 -> 19; matrix products, arithmetic and copies ran while one was open for 8% -> 6% of each run, Pallas kernels for 17% -> 10%
where the time goes in v3:
time: 168 us
  waiting for transfers between devices  83 us (49%)
  Pallas kernels  35.4 us (21%)
  starting transfers between devices  29.7 us (18%)
  other arithmetic  9.53 us (6%)
  local copies, waits for them, and re-layouts  8.78 us (5%)
    ppermute x12, waiting for transfers between devices, swap_along(): return lax.ppermute(x, 'genes', pairs)  56.6 us
    ppermute x12, starting transfers between devices, swap_along(): return lax.ppermute(x, 'genes', pairs)  13.2 us
    ppermute x6, waiting for transfers between devices, swap_plane(): return lax.ppermute(x, 'genes', pairs)  13 us
    all_to_all x2, waiting for transfers between devices, spread(): lax.all_to_all(x, 'genes', split_axis=0, concat_axis=0, tiled=True, axis_...  10.8 us
    pallas_call x1, Pallas kernels, link_backward(): pl.pallas_call(functools.partial(link_backward_kernel, rows // units, uni...  10.3 us
    pallas_call x1, Pallas kernels, gene_forward(): pl.pallas_call(functools.partial(gene_forward_kernel, gene_count, blocks)...  9.31 us
    ppermute x6, starting transfers between devices, swap_plane(): return lax.ppermute(x, 'genes', pairs)  8.11 us
    all_to_all x2, starting transfers between devices, spread(): lax.all_to_all(x, 'genes', split_axis=0, concat_axis=0, tiled=True, axis_...  7.76 us
  transfers between devices with their start and end apart: 26, of which 19 were waited for; matrix products, arithmetic and copies ran while one was open for 6% of the time, Pallas kernels for 10%

profile of v3, /device:TPU:0, one launch (start us, length us, event | category | flops | bytes accessed | tf_op | source)
XLA Modules:
  0.0 167.6 jit_solution(4942533393377508219)
XLA Ops:
  3.1 4.0 %collective-permute-start.2 = (bf16[1552,128]{1,0:T(8,128)(2,1)S(1)}, bf16[1552,128]{1,0:T(8,128)(2,1)S(1)}, u32[]{:S(2)}, u32[]{:S(2)}) collective-permute-start(bf16[1552,128]{1,0:T(8,128)(2,1)S(1)} %fold_links.2.refs_0_), channel_id=1, source_target_pairs={{0,6},{2,4},{4,2},{6,0},{8,14},{10,12},{12,10},{14,8},{16,22},{18,... | collective-permute-start | bytes 1191944 | tf_op jit(solution)/shard_map/link_weights/ppermute | solution.py:489
  8.3 9.3 %gene_forward.1 = bf16[128,3072]{1,0:T(8,128)(2,1)} custom-call(s32[192]{0:T(256)S(1)} %copy-done.9, bf16[128,49152]{1,0:T(8,128)(2,1)} %geno_hbm.3, bf16[16,49152]{1,0:T(8,128)(2,1)} %weight_hbm.1), custom_call_target="tpu_custom_call" | custom-call | flops 1006632960 | bytes 14155776 | tf_op jit(solution)/shard_map/hidden/gene_forward/pallas_call | solution.py:121
  17.7 4.3 %all-to-all-start = ((bf16[4,32,3072]{2,1,0:T(8,128)(2,1)}), bf16[4,32,3072]{2,1,0:T(8,128)(2,1)S(1)}, u32[]{:S(2)}, u32[]{:S(2)}) async-start(bf16[4,32,3072]{2,1,0:T(8,128)(2,1)} %bitcast.3), calls=%async_computation | async-start | bytes 1572864 | tf_op jit(solution)/shard_map/hidden/all_to_all | solution.py:499
  27.0 6.5 %all-to-all-done.hidden = bf16[4,32,3072]{2,1,0:T(8,128)(2,1)S(1)} async-done(((bf16[4,32,3072]{2,1,0:T(8,128)(2,1)}), bf16[4,32,3072]{2,1,0:T(8,128)(2,1)S(1)}, u32[]{:S(2)}, u32[]{:S(2)}) %all-to-all-start) | async-done | bytes 786464 | tf_op jit(solution)/shard_map/hidden/all_to_all | solution.py:499
  35.3 7.2 %link_forward.1 = (bf16[64,16,128]{2,1,0:T(8,128)(2,1)S(1)}, bf16[64,16,128]{2,1,0:T(8,128)(2,1)S(1)}, bf16[64,16,128]{2,1,0:T(8,128)(2,1)S(1)}, bf16[64,16,128]...) custom-call(s32[2]{0:T(128)S(1)} %pad_add_fusion.place, ...), custom_call_target="tpu_custom_call" | custom-call | flops 4000000000 | bytes 8000000 | tf_op jit(solution)/shard_map/pathway_sum/link_forward/pallas_call | solution.py:373
  44.7 7.1 %collective-permute-done.6 = bf16[64,16,128]{2,1,0:T(8,128)(2,1)S(1)} collective-permute-done((bf16[64,16,128]{2,1,0:T(8,128)(2,1)S(1)}, bf16[64,16,128]{2,1,0:T(8,128)(2,1)S(1)}, u32[]{:S(2)}, u32[]{:S(2)}) %collective-permute-start.6) | collective-permute-done | bytes 262176 | tf_op jit(solution)/shard_map/pathway_sum/ppermute | solution.py:493
  56.1 6.0 %collective-permute-done.9 = bf16[64,16,128]{2,1,0:T(8,128)(2,1)S(1)} collective-permute-done((bf16[64,16,128]{2,1,0:T(8,128)(2,1)S(1)}, bf16[64,16,128]{2,1,0:T(8,128)(2,1)S(1)}, u32[]{:S(2)}, u32[]{:S(2)}) %collective-permute-start.9) | collective-permute-done | bytes 262176 | tf_op jit(solution)/shard_map/pathway_sum/ppermute | solution.py:493
  65.1 8.3 %collective-permute-done.8 = bf16[64,16,128]{2,1,0:T(8,128)(2,1)S(1)} collective-permute-done((bf16[64,16,128]{2,1,0:T(8,128)(2,1)S(1)}, bf16[64,16,128]{2,1,0:T(8,128)(2,1)S(1)}, u32[]{:S(2)}, u32[]{:S(2)}) %collective-permute-start.8) | collective-permute-done | bytes 262176 | tf_op jit(solution)/shard_map/pathway_sum/ppermute | solution.py:493
  73.7 3.4 %collective-permute-done.10 = bf16[64,16,128]{2,1,0:T(8,128)(2,1)S(1)} collective-permute-done((bf16[64,16,128]{2,1,0:T(8,128)(2,1)S(1)}, bf16[64,16,128]{2,1,0:T(8,128)(2,1)S(1)}, u32[]{:S(2)}, u32[]{:S(2)}) %collective-permute-start.10) | collective-permute-done | bytes 262176 | tf_op jit(solution)/shard_map/pathway_sum/ppermute | solution.py:493
  77.1 6.1 %collective-permute-done.11 = bf16[64,16,128]{2,1,0:T(8,128)(2,1)S(1)} collective-permute-done((bf16[64,16,128]{2,1,0:T(8,128)(2,1)S(1)}, bf16[64,16,128]{2,1,0:T(8,128)(2,1)S(1)}, u32[]{:S(2)}, u32[]{:S(2)}) %collective-permute-start.11) | collective-permute-done | bytes 262176 | tf_op jit(solution)/shard_map/pathway_sum/ppermute | solution.py:493
  86.4 7.6 %collective-permute-done.14.refs_12_ = bf16[64,16,128]{2,1,0:T(8,128)(2,1)S(1)} collective-permute-done((bf16[64,16,128]{2,1,0:T(8,128)(2,1)S(1)}, bf16[64,16,128]{2,1,0:T(8,128)(2,1)S(1)}, u32[]{:S(2)}, u32[]{:S(2)}) %collective-permute-start.14) | collective-permute-done | bytes 262176 | tf_op jit(solution)/shard_map/pathway_delta/ppermute | solution.py:493
  95.4 3.3 %collective-permute-done.15.refs_13_ = bf16[64,16,128]{2,1,0:T(8,128)(2,1)S(1)} collective-permute-done((bf16[64,16,128]{2,1,0:T(8,128)(2,1)S(1)}, bf16[64,16,128]{2,1,0:T(8,128)(2,1)S(1)}, u32[]{:S(2)}, u32[]{:S(2)}) %collective-permute-start.15) | collective-permute-done | bytes 262176 | tf_op jit(solution)/shard_map/pathway_delta/ppermute | solution.py:493
  100.1 5.6 %collective-permute-done.13.refs_11_ = bf16[64,16,128]{2,1,0:T(8,128)(2,1)S(1)} collective-permute-done((bf16[64,16,128]{2,1,0:T(8,128)(2,1)S(1)}, bf16[64,16,128]{2,1,0:T(8,128)(2,1)S(1)}, u32[]{:S(2)}, u32[]{:S(2)}) %collective-permute-start.13) | collective-permute-done | bytes 262176 | tf_op jit(solution)/shard_map/pathway_delta/ppermute | solution.py:493
  105.7 5.6 %collective-permute-done.16.refs_14_ = bf16[64,16,128]{2,1,0:T(8,128)(2,1)S(1)} collective-permute-done((bf16[64,16,128]{2,1,0:T(8,128)(2,1)S(1)}, bf16[64,16,128]{2,1,0:T(8,128)(2,1)S(1)}, u32[]{:S(2)}, u32[]{:S(2)}) %collective-permute-start.16) | collective-permute-done | bytes 262176 | tf_op jit(solution)/shard_map/pathway_delta/ppermute | solution.py:493
  111.4 3.5 %collective-permute-done.17.refs_15_ = bf16[64,16,128]{2,1,0:T(8,128)(2,1)S(1)} collective-permute-done((bf16[64,16,128]{2,1,0:T(8,128)(2,1)S(1)}, bf16[64,16,128]{2,1,0:T(8,128)(2,1)S(1)}, u32[]{:S(2)}, u32[]{:S(2)}) %collective-permute-start.17) | collective-permute-done | bytes 262176 | tf_op jit(solution)/shard_map/pathway_delta/ppermute | solution.py:493
  115.6 10.3 %link_backward.1 = (bf16[4,32,3072]{2,1,0:T(8,128)(2,1)}, bf16[4,1552,128]{2,1,0:T(8,128)(2,1)}, bf16[4,1552,128]{2,1,0:T(8,128)(2,1)}) custom-call(s32[2]{0:T(128)} %copy-done.16, s32[2,768]{1,0:T(2,128)} %copy-done.8, s32[512]{0:T(512)} %copy-done.11, bf16[4,32,3072]{2,1,0:T(8,128)(2,1)} %copy-done.3, f32[64,128]{1,0:T(8,128)} %reshape.72.head, ...), custom_call_target="tpu_custom_call" | custom-call | flops 6000000000 | bytes 20000000 | tf_op jit(solution)/shard_map/link_grads/link_backward/pallas_call | solution.py:447
  125.9 3.5 %all-to-all-start.1 = ((bf16[4,32,3072]{2,1,0:T(8,128)(2,1)}), bf16[4,32,3072]{2,1,0:T(8,128)(2,1)S(1)}, u32[]{:S(2)}, u32[]{:S(2)}) async-start(bf16[4,32,3072]{2,1,0:T(8,128)(2,1)} %get-tuple-element.39), calls=%async_computation.1 | async-start | bytes 1572864 | tf_op jit(solution)/shard_map/link_grads/all_to_all | solution.py:499
  130.7 3.0 %fusion.3 = (bf16[1552,128]{1,0:T(8,128)(2,1)}, bf16[1552,128]{1,0:T(8,128)(2,1)S(1)}, bf16[1552,128]{1,0:T(8,128)(2,1)S(1)}, bf16[1552,128]{1,0:T(8,128)(2,1)S(1)}) fusion(bf16[4,1552,128]{2,1,0:T(8,128)(2,1)} %copy-done.18, bf16[4,1552,128]{2,1,0:T(8,128)(2,1)} %get-tuple-element.40), kind=kLoop, calls=%fused_computation.19 | loop fusion | flops 3178496 | bytes 4767744 | tf_op jit(solution)/shard_map/grad_pathway/convert_element_type | solution.py:595
  133.7 2.8 %collective-permute-start.21 = (bf16[1552,128]{1,0:T(8,128)(2,1)}, bf16[1552,128]{1,0:T(8,128)(2,1)S(1)}, u32[]{:S(2)}, u32[]{:S(2)}) collective-permute-start(bf16[1552,128]{1,0:T(8,128)(2,1)} %get-tuple-element.51), channel_id=1, source_target_pairs={{0,6},{2,4},{4,2},{6,0},{8,14},{10,12},{12,10},{14,8},{16,22},{18,... | collective-permute-start | bytes 1191944 | tf_op jit(solution)/shard_map/grad_pathway/ppermute | solution.py:489
  137.2 4.3 %all-to-all-done.1 = bf16[4,32,3072]{2,1,0:T(8,128)(2,1)S(1)} async-done(((bf16[4,32,3072]{2,1,0:T(8,128)(2,1)}), bf16[4,32,3072]{2,1,0:T(8,128)(2,1)S(1)}, u32[]{:S(2)}, u32[]{:S(2)}) %all-to-all-start.1) | async-done | bytes 786464 | tf_op jit(solution)/shard_map/link_grads/all_to_all | solution.py:499
  141.5 6.7 %gene_backward.1 = bf16[16,49152]{1,0:T(8,128)(2,1)} custom-call(s32[192]{0:T(256)S(1)} %copy-done.10, bf16[128,49152]{1,0:T(8,128)(2,1)} %geno_hbm.3, bf16[128,3072]{1,0:T(8,128)(2,1)S(1)} %bitcast.27), custom_call_target="tpu_custom_call" | custom-call | flops 1006632960 | bytes 28311552 | tf_op jit(solution)/shard_map/grad_gene/gene_backward/pallas_call | solution.py:205
  148.3 2.7 %collective-permute-done.21.refs_3_ = bf16[1552,128]{1,0:T(8,128)(2,1)S(1)} collective-permute-done((bf16[1552,128]{1,0:T(8,128)(2,1)}, bf16[1552,128]{1,0:T(8,128)(2,1)S(1)}, u32[]{:S(2)}, u32[]{:S(2)}) %collective-permute-start.21) | collective-permute-done | bytes 397344 | tf_op jit(solution)/shard_map/grad_pathway/ppermute | solution.py:489
  151.0 7.1 %collective-permute-done.20.refs_2_ = bf16[1552,128]{1,0:T(8,128)(2,1)S(1)} collective-permute-done((bf16[1552,128]{1,0:T(8,128)(2,1)S(1)}, bf16[1552,128]{1,0:T(8,128)(2,1)S(1)}, u32[]{:S(2)}, u32[]{:S(2)}) %collective-permute-start.20) | collective-permute-done | bytes 397344 | tf_op jit(solution)/shard_map/grad_pathway/ppermute | solution.py:489
  162.0 3.4 %convert_add_fusion = f32[16,49152]{1,0:T(8,128)} fusion(bf16[16,49152]{1,0:T(8,128)(2,1)} %collective-permute-done.23, bf16[16,49152]{1,0:T(8,128)(2,1)S(1)} %copy-done.17), kind=kLoop, calls=%fused_computation | loop fusion | flops 2359296 | bytes 6291456 | tf_op jit(solution)/shard_map/grad_pathway/add | solution.py:606
  (134 shorter events, 34.8 us)
Async XLA Ops:
  3.1 20.1 %collective-permute-start.2 = (bf16[1552,128]{1,0:T(8,128)(2,1)S(1)}, bf16[1552,128]{1,0:T(8,128)(2,1)S(1)}, u32[]{:S(2)}, u32[]{:S(2)}) collective-permute-start(bf16[1552,128]{1,0:T(8,128)(2,1)S(1)} %fold_links.2.refs_0_), channel_id=1, source_target_pairs={{0,6},{2,4},{4,2},{6,0},{8,14},{10,12},{12,10},{14,8},{16,22},{18,... | collective-permute-start | bytes 1191944 | tf_op jit(solution)/shard_map/link_weights/ppermute | solution.py:489
  7.0 18.1 %collective-permute-start.1 = (bf16[1552,128]{1,0:T(8,128)(2,1)S(1)}, bf16[1552,128]{1,0:T(8,128)(2,1)S(1)}, u32[]{:S(2)}, u32[]{:S(2)}) collective-permute-start(bf16[1552,128]{1,0:T(8,128)(2,1)S(1)} %fold_links.2.refs_0_), channel_id=1, source_target_pairs={{0,4},{2,6},{4,0},{6,2},{8,12},{10,14},{12,8},{14,10},{16,20},{18,... | collective-permute-start | bytes 1191944 | tf_op jit(solution)/shard_map/link_weights/ppermute | solution.py:489
  7.5 18.8 %collective-permute-start = (bf16[1552,128]{1,0:T(8,128)(2,1)S(1)}, bf16[1552,128]{1,0:T(8,128)(2,1)}, u32[]{:S(2)}, u32[]{:S(2)}) collective-permute-start(bf16[1552,128]{1,0:T(8,128)(2,1)S(1)} %fold_links.2.refs_0_), channel_id=1, source_target_pairs={{0,2},{2,0},{4,6},{6,4},{8,10},{10,8},{12,14},{14,12},{16,18},{18,... | collective-permute-start | bytes 1191944 | tf_op jit(solution)/shard_map/link_weights/ppermute | solution.py:489
  17.7 15.8 %all-to-all-start = ((bf16[4,32,3072]{2,1,0:T(8,128)(2,1)}), bf16[4,32,3072]{2,1,0:T(8,128)(2,1)S(1)}, u32[]{:S(2)}, u32[]{:S(2)}) async-start(bf16[4,32,3072]{2,1,0:T(8,128)(2,1)} %bitcast.3), calls=%async_computation | async-start | bytes 1572864 | tf_op jit(solution)/shard_map/hidden/all_to_all | solution.py:499
  23.2 10.4 %collective-permute-start.5 = (bf16[1552,128]{1,0:T(8,128)(2,1)S(1)}, bf16[1552,128]{1,0:T(8,128)(2,1)S(1)}, u32[]{:S(2)}, u32[]{:S(2)}) collective-permute-start(bf16[1552,128]{1,0:T(8,128)(2,1)S(1)} %collective-permute-done.2.refs_3_), channel_id=1, source_target_pairs={{0,1},{1,0},{2,3},{3,2},{4,5},{5,4},{6,7},{7,6},{8,9},{9,8},{10,11... | collective-permute-start | bytes 1191944 | tf_op jit(solution)/shard_map/link_weights/ppermute | solution.py:496
  25.2 9.1 %collective-permute-start.4 = (bf16[1552,128]{1,0:T(8,128)(2,1)S(1)}, bf16[1552,128]{1,0:T(8,128)(2,1)}, u32[]{:S(2)}, u32[]{:S(2)}) collective-permute-start(bf16[1552,128]{1,0:T(8,128)(2,1)S(1)} %collective-permute-done.1.refs_2_), channel_id=1, source_target_pairs={{0,1},{1,0},{2,3},{3,2},{4,5},{5,4},{6,7},{7,6},{8,9},{9,8},{10,11... | collective-permute-start | bytes 1191944 | tf_op jit(solution)/shard_map/link_weights/ppermute | solution.py:496
  26.3 8.0 %collective-permute-start.3 = (bf16[1552,128]{1,0:T(8,128)(2,1)}, bf16[1552,128]{1,0:T(8,128)(2,1)}, u32[]{:S(2)}, u32[]{:S(2)}) collective-permute-start(bf16[1552,128]{1,0:T(8,128)(2,1)} %collective-permute-done.refs_1_), channel_id=1, source_target_pairs={{0,1},{1,0},{2,3},{3,2},{4,5},{5,4},{6,7},{7,6},{8,9},{9,8},{10,11... | collective-permute-start | bytes 1191944 | tf_op jit(solution)/shard_map/link_weights/ppermute | solution.py:496
  42.5 9.3 %collective-permute-start.6 = (bf16[64,16,128]{2,1,0:T(8,128)(2,1)S(1)}, bf16[64,16,128]{2,1,0:T(8,128)(2,1)S(1)}, u32[]{:S(2)}, u32[]{:S(2)}) collective-permute-start(bf16[64,16,128]{2,1,0:T(8,128)(2,1)S(1)} %get-tuple-element.30), channel_id=1, source_target_pairs={{0,8},{2,10},{4,12},{6,14},{8,0},{10,2},{12,4},{14,6},{16,24},{18,... | collective-permute-start | bytes 786440 | tf_op jit(solution)/shard_map/pathway_sum/ppermute | solution.py:493
  44.2 17.9 %collective-permute-start.9 = (bf16[64,16,128]{2,1,0:T(8,128)(2,1)S(1)}, bf16[64,16,128]{2,1,0:T(8,128)(2,1)S(1)}, u32[]{:S(2)}, u32[]{:S(2)}) collective-permute-start(bf16[64,16,128]{2,1,0:T(8,128)(2,1)S(1)} %get-tuple-element.35), channel_id=1, source_target_pairs={{0,8},{2,10},{4,12},{6,14},{8,0},{10,2},{12,4},{14,6},{16,24},{18,... | collective-permute-start | bytes 786440 | tf_op jit(solution)/shard_map/pathway_sum/ppermute | solution.py:493
  51.9 21.5 %collective-permute-start.7 = (bf16[64,16,128]{2,1,0:T(8,128)(2,1)S(1)}, bf16[64,16,128]{2,1,0:T(8,128)(2,1)S(1)}, u32[]{:S(2)}, u32[]{:S(2)}) collective-permute-start(bf16[64,16,128]{2,1,0:T(8,128)(2,1)S(1)} %add_convert_fusion.5), channel_id=1, source_target_pairs={{0,16},{2,18},{4,20},{6,22},{8,24},{10,26},{12,28},{14,30},{16,0},... | collective-permute-start | bytes 786440 | tf_op jit(solution)/shard_map/pathway_sum/ppermute | solution.py:493
  54.5 18.8 %collective-permute-start.8 = (bf16[64,16,128]{2,1,0:T(8,128)(2,1)S(1)}, bf16[64,16,128]{2,1,0:T(8,128)(2,1)S(1)}, u32[]{:S(2)}, u32[]{:S(2)}) collective-permute-start(bf16[64,16,128]{2,1,0:T(8,128)(2,1)S(1)} %get-tuple-element.32), channel_id=1, source_target_pairs={{0,8},{2,10},{4,12},{6,14},{8,0},{10,2},{12,4},{14,6},{16,24},{18,... | collective-permute-start | bytes 786440 | tf_op jit(solution)/shard_map/pathway_sum/ppermute | solution.py:493
  62.2 14.9 %collective-permute-start.10 = (bf16[64,16,128]{2,1,0:T(8,128)(2,1)S(1)}, bf16[64,16,128]{2,1,0:T(8,128)(2,1)S(1)}, u32[]{:S(2)}, u32[]{:S(2)}) collective-permute-start(bf16[64,16,128]{2,1,0:T(8,128)(2,1)S(1)} %add_convert_fusion.4), channel_id=1, source_target_pairs={{0,16},{2,18},{4,20},{6,22},{8,24},{10,26},{12,28},{14,30},{16,0},... | collective-permute-start | bytes 786440 | tf_op jit(solution)/shard_map/pathway_sum/ppermute | solution.py:493
  62.3 20.9 %collective-permute-start.11 = (bf16[64,16,128]{2,1,0:T(8,128)(2,1)S(1)}, bf16[64,16,128]{2,1,0:T(8,128)(2,1)S(1)}, u32[]{:S(2)}, u32[]{:S(2)}) collective-permute-start(bf16[64,16,128]{2,1,0:T(8,128)(2,1)S(1)} %get-tuple-element.38), channel_id=1, source_target_pairs={{0,8},{2,10},{4,12},{6,14},{8,0},{10,2},{12,4},{14,6},{16,24},{18,... | collective-permute-start | bytes 786440 | tf_op jit(solution)/shard_map/pathway_sum/ppermute | solution.py:493
  73.6 20.4 %collective-permute-start.14 = (bf16[64,16,128]{2,1,0:T(8,128)(2,1)S(1)}, bf16[64,16,128]{2,1,0:T(8,128)(2,1)S(1)}, u32[]{:S(2)}, u32[]{:S(2)}) collective-permute-start(bf16[64,16,128]{2,1,0:T(8,128)(2,1)S(1)} %multiply_convert_fusion.1.refs_8_), channel_id=1, source_target_pairs={{0,16},{2,18},{4,20},{6,22},{8,24},{10,26},{12,28},{14,30},{16,0},... | collective-permute-start | bytes 786440 | tf_op jit(solution)/shard_map/pathway_delta/ppermute | solution.py:493
  83.7 15.1 %collective-permute-start.15 = (bf16[64,16,128]{2,1,0:T(8,128)(2,1)S(1)}, bf16[64,16,128]{2,1,0:T(8,128)(2,1)S(1)}, u32[]{:S(2)}, u32[]{:S(2)}) collective-permute-start(bf16[64,16,128]{2,1,0:T(8,128)(2,1)S(1)} %get-tuple-element.57.refs_9_), channel_id=1, source_target_pairs={{0,16},{2,18},{4,20},{6,22},{8,24},{10,26},{12,28},{14,30},{16,0},... | collective-permute-start | bytes 786440 | tf_op jit(solution)/shard_map/pathway_delta/ppermute | solution.py:493
  83.9 16.2 %collective-permute-start.12 = (bf16[64,16,128]{2,1,0:T(8,128)(2,1)S(1)}, bf16[64,16,128]{2,1,0:T(8,128)(2,1)S(1)}, u32[]{:S(2)}, u32[]{:S(2)}) collective-permute-start(bf16[64,16,128]{2,1,0:T(8,128)(2,1)S(1)} %multiply_convert_fusion.1.refs_8_), channel_id=1, source_target_pairs={{0,8},{2,10},{4,12},{6,14},{8,0},{10,2},{12,4},{14,6},{16,24},{18,... | collective-permute-start | bytes 786440 | tf_op jit(solution)/shard_map/pathway_delta/ppermute | solution.py:493
  86.4 19.4 %collective-permute-start.13 = (bf16[64,16,128]{2,1,0:T(8,128)(2,1)S(1)}, bf16[64,16,128]{2,1,0:T(8,128)(2,1)S(1)}, u32[]{:S(2)}, u32[]{:S(2)}) collective-permute-start(bf16[64,16,128]{2,1,0:T(8,128)(2,1)S(1)} %get-tuple-element.57.refs_9_), channel_id=1, source_target_pairs={{0,8},{2,10},{4,12},{6,14},{8,0},{10,2},{12,4},{14,6},{16,24},{18,... | collective-permute-start | bytes 786440 | tf_op jit(solution)/shard_map/pathway_delta/ppermute | solution.py:493
  94.0 17.3 %collective-permute-start.16 = (bf16[64,16,128]{2,1,0:T(8,128)(2,1)S(1)}, bf16[64,16,128]{2,1,0:T(8,128)(2,1)S(1)}, u32[]{:S(2)}, u32[]{:S(2)}) collective-permute-start(bf16[64,16,128]{2,1,0:T(8,128)(2,1)S(1)} %collective-permute-done.14.refs_12_), channel_id=1, source_target_pairs={{0,8},{2,10},{4,12},{6,14},{8,0},{10,2},{12,4},{14,6},{16,24},{18,... | collective-permute-start | bytes 786440 | tf_op jit(solution)/shard_map/pathway_delta/ppermute | solution.py:493
  98.8 16.0 %collective-permute-start.17 = (bf16[64,16,128]{2,1,0:T(8,128)(2,1)S(1)}, bf16[64,16,128]{2,1,0:T(8,128)(2,1)S(1)}, u32[]{:S(2)}, u32[]{:S(2)}) collective-permute-start(bf16[64,16,128]{2,1,0:T(8,128)(2,1)S(1)} %collective-permute-done.15.refs_13_), channel_id=1, source_target_pairs={{0,8},{2,10},{4,12},{6,14},{8,0},{10,2},{12,4},{14,6},{16,24},{18,... | collective-permute-start | bytes 786440 | tf_op jit(solution)/shard_map/pathway_delta/ppermute | solution.py:493
  125.9 15.6 %all-to-all-start.1 = ((bf16[4,32,3072]{2,1,0:T(8,128)(2,1)}), bf16[4,32,3072]{2,1,0:T(8,128)(2,1)S(1)}, u32[]{:S(2)}, u32[]{:S(2)}) async-start(bf16[4,32,3072]{2,1,0:T(8,128)(2,1)} %get-tuple-element.39), calls=%async_computation.1 | async-start | bytes 1572864 | tf_op jit(solution)/shard_map/link_grads/all_to_all | solution.py:499
  133.7 17.3 %collective-permute-start.21 = (bf16[1552,128]{1,0:T(8,128)(2,1)}, bf16[1552,128]{1,0:T(8,128)(2,1)S(1)}, u32[]{:S(2)}, u32[]{:S(2)}) collective-permute-start(bf16[1552,128]{1,0:T(8,128)(2,1)} %get-tuple-element.51), channel_id=1, source_target_pairs={{0,6},{2,4},{4,2},{6,0},{8,14},{10,12},{12,10},{14,8},{16,22},{18,... | collective-permute-start | bytes 1191944 | tf_op jit(solution)/shard_map/grad_pathway/ppermute | solution.py:489
  136.5 21.6 %collective-permute-start.20 = (bf16[1552,128]{1,0:T(8,128)(2,1)S(1)}, bf16[1552,128]{1,0:T(8,128)(2,1)S(1)}, u32[]{:S(2)}, u32[]{:S(2)}) collective-permute-start(bf16[1552,128]{1,0:T(8,128)(2,1)S(1)} %get-tuple-element.52), channel_id=1, source_target_pairs={{0,4},{2,6},{4,0},{6,2},{8,12},{10,14},{12,8},{14,10},{16,20},{18,... | collective-permute-start | bytes 1191944 | tf_op jit(solution)/shard_map/grad_pathway/ppermute | solution.py:489
  137.0 21.2 %collective-permute-start.19 = (bf16[1552,128]{1,0:T(8,128)(2,1)S(1)}, bf16[1552,128]{1,0:T(8,128)(2,1)S(1)}, u32[]{:S(2)}, u32[]{:S(2)}) collective-permute-start(bf16[1552,128]{1,0:T(8,128)(2,1)S(1)} %get-tuple-element.53), channel_id=1, source_target_pairs={{0,2},{2,0},{4,6},{6,4},{8,10},{10,8},{12,14},{14,12},{16,18},{18,... | collective-permute-start | bytes 1191944 | tf_op jit(solution)/shard_map/grad_pathway/ppermute | solution.py:489
  159.0 6.4 %collective-permute-start.22 = (f32[200,1024]{1,0:T(8,128)S(1)}, f32[200,1024]{1,0:T(8,128)S(1)}, u32[]{:S(2)}, u32[]{:S(2)}) collective-permute-start(f32[200,1024]{1,0:T(8,128)S(1)} %unfold_sum.1), channel_id=1, source_target_pairs={{0,1},{1,0},{2,3},{3,2},{4,5},{5,4},{6,7},{7,6},{8,9},{9,8},{10,11... | collective-permute-start | bytes 2457608 | tf_op jit(solution)/shard_map/grad_pathway/ppermute | solution.py:496
  (31 other events, 362.1 us)

commit v4 on v3

--- a/solution.py
+++ b/solution.py
@@ -385,8 +385,8 @@
 
 
 def link_backward_kernel(half_genes, units, place, members, slots, hidden, head, *refs):
-    weights, deltas = refs[: 2 * GROUP], refs[2 * GROUP : -4]
-    out, keeps, gives, table = refs[-4:]
+    weights, deltas = refs[: 2 * GROUP], refs[2 * GROUP : -7]
+    out, keeps_hbm, gives_hbm, keeps, gives, table, sems = refs[-7:]
     quarter, core = place[0], place[1]
     tiles = LANES // units
     samples = hidden.shape[1]
@@ -402,6 +402,7 @@
         (row_gene == lane_gene + i * (LANES // samples)).astype(jnp.float32)
         for i in range(tiles * samples // LANES)
     ]
+    copies = []
     for index in range(2 * GROUP):
         piece = index % GROUP
         grads = gives if index // GROUP else keeps
@@ -437,6 +438,11 @@
         coarse = lines.astype(grads.dtype).astype(jnp.float32)
         lines = jnp.concatenate([coarse, lines - coarse], axis=0)
         grads[piece, half_genes * units :, :] = lines.astype(grads.dtype)
+        target = gives_hbm if index // GROUP else keeps_hbm
+        copies.append(pltpu.make_async_copy(grads.at[piece], target.at[piece], sems.at[index]))
+        copies[-1].start()
+    for copy in copies:
+        copy.wait()
 
 
 def link_backward(place, members, slots, hidden, head, weights, deltas, units):
@@ -448,8 +454,13 @@
         functools.partial(link_backward_kernel, rows // units, units),
         out_shape=[jax.ShapeDtypeStruct(hidden.shape, jnp.bfloat16), grads, grads],
         in_specs=[smem, smem, smem] + [vmem] * (2 + len(operands)),
-        out_specs=[vmem] * 3,
-        scratch_shapes=[pltpu.VMEM((slots.shape[0], ROWS, LANES), jnp.bfloat16)],
+        out_specs=[vmem, hbm, hbm],
+        scratch_shapes=[
+            pltpu.VMEM(grads.shape, grads.dtype),
+            pltpu.VMEM(grads.shape, grads.dtype),
+            pltpu.VMEM((slots.shape[0], ROWS, LANES), jnp.bfloat16),
+            pltpu.SemaphoreType.DMA((2 * GROUP,)),
+        ],
         compiler_params=pltpu.CompilerParams(vmem_limit_bytes=56 * MIB),
         cost_estimate=pl.CostEstimate(
             flops=6 * 10**9, bytes_accessed=20 * 10**6, transcendentals=0
@@ -568,7 +579,7 @@
         with jax.named_scope("pathway_delta"):
             two = [swap_along(x, 2) for x in own]
             one = [swap_along(x, 1) for x in own]
-            three = [swap_along(x, 1) for x in two]
+            three = [swap_along(x, 1) for x in two[:-1]] + [swap_along(own[-1], 3)]
             deltas = own + one + two + three
     else:
         with jax.named_scope("pathway_sum"):

time: 168 us -> 165 us (0.982)
  waiting for transfers between devices: 83 us -> 77.7 us
  starting transfers between devices: 29.7 us -> 32.4 us
    ppermute x12, waiting for transfers between devices: 56.6 us -> 51.4 us  [swap_along(): return lax.ppermute(x, 'genes', pairs)]
    ppermute x12, starting transfers between devices: 13.2 us -> 15.8 us  [swap_along(): return lax.ppermute(x, 'genes', pairs)]
  transfers between devices with their start and end apart: 26 -> 26, of which waited for: 19 -> 17; matrix products, arithmetic and copies ran while one was open for 6% -> 6% of each run, Pallas kernels for 10% -> 11%
where the time goes in v4:
time: 165 us
  waiting for transfers between devices  77.7 us (47%)
  Pallas kernels  35.4 us (21%)
  starting transfers between devices  32.4 us (20%)
  other arithmetic  9.53 us (6%)
  local copies, waits for them, and re-layouts  8.77 us (5%)
    ppermute x12, waiting for transfers between devices, swap_along(): return lax.ppermute(x, 'genes', pairs)  51.4 us
    ppermute x12, starting transfers between devices, swap_along(): return lax.ppermute(x, 'genes', pairs)  15.8 us
    ppermute x6, waiting for transfers between devices, swap_plane(): return lax.ppermute(x, 'genes', pairs)  12.9 us
    all_to_all x2, waiting for transfers between devices, spread(): lax.all_to_all(x, 'genes', split_axis=0, concat_axis=0, tiled=True, axis_...  10.9 us
    pallas_call x1, Pallas kernels, link_backward(): pl.pallas_call(functools.partial(link_backward_kernel, rows // units, uni...  10.2 us
    pallas_call x1, Pallas kernels, gene_forward(): pl.pallas_call(functools.partial(gene_forward_kernel, gene_count, blocks)...  9.31 us
    ppermute x6, starting transfers between devices, swap_plane(): return lax.ppermute(x, 'genes', pairs)  8.11 us
    all_to_all x2, starting transfers between devices, spread(): lax.all_to_all(x, 'genes', split_axis=0, concat_axis=0, tiled=True, axis_...  7.76 us
  transfers between devices with their start and end apart: 26, of which 17 were waited for; matrix products, arithmetic and copies ran while one was open for 6% of the time, Pallas kernels for 11%

profile of v4, /device:TPU:0, one launch (start us, length us, event | category | flops | bytes accessed | tf_op | source)
XLA Modules:
  0.0 165.0 jit_solution(15884690726888291308)
XLA Ops:
  3.1 4.0 %collective-permute-start.2 = (bf16[1552,128]{1,0:T(8,128)(2,1)S(1)}, bf16[1552,128]{1,0:T(8,128)(2,1)S(1)}, u32[]{:S(2)}, u32[]{:S(2)}) collective-permute-start(bf16[1552,128]{1,0:T(8,128)(2,1)S(1)} %fold_links.2.refs_0_), channel_id=1, source_target_pairs={{0,6},{2,4},{4,2},{6,0},{8,14},{10,12},{12,10},{14,8},{16,22},{18,... | collective-permute-start | bytes 1191944 | tf_op jit(solution)/shard_map/link_weights/ppermute | solution.py:500
  8.3 9.3 %gene_forward.1 = bf16[128,3072]{1,0:T(8,128)(2,1)} custom-call(s32[192]{0:T(256)S(1)} %copy-done.9, bf16[128,49152]{1,0:T(8,128)(2,1)} %geno_hbm.3, bf16[16,49152]{1,0:T(8,128)(2,1)} %weight_hbm.1), custom_call_target="tpu_custom_call" | custom-call | flops 1006632960 | bytes 14155776 | tf_op jit(solution)/shard_map/hidden/gene_forward/pallas_call | solution.py:121
  17.7 4.3 %all-to-all-start = ((bf16[4,32,3072]{2,1,0:T(8,128)(2,1)}), bf16[4,32,3072]{2,1,0:T(8,128)(2,1)S(1)}, u32[]{:S(2)}, u32[]{:S(2)}) async-start(bf16[4,32,3072]{2,1,0:T(8,128)(2,1)} %bitcast.3), calls=%async_computation | async-start | bytes 1572864 | tf_op jit(solution)/shard_map/hidden/all_to_all | solution.py:510
  27.0 6.5 %all-to-all-done.hidden = bf16[4,32,3072]{2,1,0:T(8,128)(2,1)S(1)} async-done(((bf16[4,32,3072]{2,1,0:T(8,128)(2,1)}), bf16[4,32,3072]{2,1,0:T(8,128)(2,1)S(1)}, u32[]{:S(2)}, u32[]{:S(2)}) %all-to-all-start) | async-done | bytes 786464 | tf_op jit(solution)/shard_map/hidden/all_to_all | solution.py:510
  35.3 7.2 %link_forward.1 = (bf16[64,16,128]{2,1,0:T(8,128)(2,1)S(1)}, bf16[64,16,128]{2,1,0:T(8,128)(2,1)S(1)}, bf16[64,16,128]{2,1,0:T(8,128)(2,1)S(1)}, bf16[64,16,128]...) custom-call(s32[2]{0:T(128)S(1)} %pad_add_fusion.place, ...), custom_call_target="tpu_custom_call" | custom-call | flops 4000000000 | bytes 8000000 | tf_op jit(solution)/shard_map/pathway_sum/link_forward/pallas_call | solution.py:373
  44.7 7.1 %collective-permute-done.6 = bf16[64,16,128]{2,1,0:T(8,128)(2,1)S(1)} collective-permute-done((bf16[64,16,128]{2,1,0:T(8,128)(2,1)S(1)}, bf16[64,16,128]{2,1,0:T(8,128)(2,1)S(1)}, u32[]{:S(2)}, u32[]{:S(2)}) %collective-permute-start.6) | collective-permute-done | bytes 262176 | tf_op jit(solution)/shard_map/pathway_sum/ppermute | solution.py:504
  51.9 2.6 %collective-permute-start.7 = (bf16[64,16,128]{2,1,0:T(8,128)(2,1)S(1)}, bf16[64,16,128]{2,1,0:T(8,128)(2,1)S(1)}, u32[]{:S(2)}, u32[]{:S(2)}) collective-permute-start(bf16[64,16,128]{2,1,0:T(8,128)(2,1)S(1)} %add_convert_fusion.5), channel_id=1, source_target_pairs={{0,16},{2,18},{4,20},{6,22},{8,24},{10,26},{12,28},{14,30},{16,0},... | collective-permute-start | bytes 786440 | tf_op jit(solution)/shard_map/pathway_sum/ppermute | solution.py:504
  56.1 6.0 %collective-permute-done.9 = bf16[64,16,128]{2,1,0:T(8,128)(2,1)S(1)} collective-permute-done((bf16[64,16,128]{2,1,0:T(8,128)(2,1)S(1)}, bf16[64,16,128]{2,1,0:T(8,128)(2,1)S(1)}, u32[]{:S(2)}, u32[]{:S(2)}) %collective-permute-start.9) | collective-permute-done | bytes 262176 | tf_op jit(solution)/shard_map/pathway_sum/ppermute | solution.py:504
  62.3 2.4 %collective-permute-start.11 = (bf16[64,16,128]{2,1,0:T(8,128)(2,1)S(1)}, bf16[64,16,128]{2,1,0:T(8,128)(2,1)S(1)}, u32[]{:S(2)}, u32[]{:S(2)}) collective-permute-start(bf16[64,16,128]{2,1,0:T(8,128)(2,1)S(1)} %get-tuple-element.38), channel_id=1, source_target_pairs={{0,8},{2,10},{4,12},{6,14},{8,0},{10,2},{12,4},{14,6},{16,24},{18,... | collective-permute-start | bytes 786440 | tf_op jit(solution)/shard_map/pathway_sum/ppermute | solution.py:504
  65.1 8.3 %collective-permute-done.8 = bf16[64,16,128]{2,1,0:T(8,128)(2,1)S(1)} collective-permute-done((bf16[64,16,128]{2,1,0:T(8,128)(2,1)S(1)}, bf16[64,16,128]{2,1,0:T(8,128)(2,1)S(1)}, u32[]{:S(2)}, u32[]{:S(2)}) %collective-permute-start.8) | collective-permute-done | bytes 262176 | tf_op jit(solution)/shard_map/pathway_sum/ppermute | solution.py:504
  77.1 7.5 %collective-permute-done.11 = bf16[64,16,128]{2,1,0:T(8,128)(2,1)S(1)} collective-permute-done((bf16[64,16,128]{2,1,0:T(8,128)(2,1)S(1)}, bf16[64,16,128]{2,1,0:T(8,128)(2,1)S(1)}, u32[]{:S(2)}, u32[]{:S(2)}) %collective-permute-start.11) | collective-permute-done | bytes 262176 | tf_op jit(solution)/shard_map/pathway_sum/ppermute | solution.py:504
  87.0 2.6 %collective-permute-start.13 = (bf16[64,16,128]{2,1,0:T(8,128)(2,1)S(1)}, bf16[64,16,128]{2,1,0:T(8,128)(2,1)S(1)}, u32[]{:S(2)}, u32[]{:S(2)}) collective-permute-start(bf16[64,16,128]{2,1,0:T(8,128)(2,1)S(1)} %get-tuple-element.57.refs_9_), channel_id=1, source_target_pairs={{0,8},{2,10},{4,12},{6,14},{8,0},{10,2},{12,4},{14,6},{16,24},{18,... | collective-permute-start | bytes 786440 | tf_op jit(solution)/shard_map/pathway_delta/ppermute | solution.py:504
  91.5 7.5 %collective-permute-done.17.refs_15_ = bf16[64,16,128]{2,1,0:T(8,128)(2,1)S(1)} collective-permute-done((bf16[64,16,128]{2,1,0:T(8,128)(2,1)S(1)}, bf16[64,16,128]{2,1,0:T(8,128)(2,1)S(1)}, u32[]{:S(2)}, u32[]{:S(2)}) %collective-permute-start.17) | collective-permute-done | bytes 262176 | tf_op jit(solution)/shard_map/pathway_delta/ppermute | solution.py:504
  99.0 11.0 %collective-permute-done.15.refs_13_ = bf16[64,16,128]{2,1,0:T(8,128)(2,1)S(1)} collective-permute-done((bf16[64,16,128]{2,1,0:T(8,128)(2,1)S(1)}, bf16[64,16,128]{2,1,0:T(8,128)(2,1)S(1)}, u32[]{:S(2)}, u32[]{:S(2)}) %collective-permute-start.15) | collective-permute-done | bytes 262176 | tf_op jit(solution)/shard_map/pathway_delta/ppermute | solution.py:504
  113.0 10.2 %link_backward.1 = (bf16[4,32,3072]{2,1,0:T(8,128)(2,1)}, bf16[4,1552,128]{2,1,0:T(8,128)(2,1)}, bf16[4,1552,128]{2,1,0:T(8,128)(2,1)}) custom-call(s32[2]{0:T(128)} %copy-done.16, s32[2,768]{1,0:T(2,128)} %copy-done.8, s32[512]{0:T(512)} %copy-done.11, bf16[4,32,3072]{2,1,0:T(8,128)(2,1)} %copy-done.3, f32[64,128]{1,0:T(8,128)} %reshape.72.head, ...), custom_call_target="tpu_custom_call" | custom-call | flops 6000000000 | bytes 20000000 | tf_op jit(solution)/shard_map/link_grads/link_backward/pallas_call | solution.py:453
  123.3 3.5 %all-to-all-start.1 = ((bf16[4,32,3072]{2,1,0:T(8,128)(2,1)}), bf16[4,32,3072]{2,1,0:T(8,128)(2,1)S(1)}, u32[]{:S(2)}, u32[]{:S(2)}) async-start(bf16[4,32,3072]{2,1,0:T(8,128)(2,1)} %get-tuple-element.39), calls=%async_computation.1 | async-start | bytes 1572864 | tf_op jit(solution)/shard_map/link_grads/all_to_all | solution.py:510
  128.1 3.0 %fusion.3 = (bf16[1552,128]{1,0:T(8,128)(2,1)}, bf16[1552,128]{1,0:T(8,128)(2,1)S(1)}, bf16[1552,128]{1,0:T(8,128)(2,1)S(1)}, bf16[1552,128]{1,0:T(8,128)(2,1)S(1)}) fusion(bf16[4,1552,128]{2,1,0:T(8,128)(2,1)} %copy-done.18, bf16[4,1552,128]{2,1,0:T(8,128)(2,1)} %get-tuple-element.40), kind=kLoop, calls=%fused_computation.19 | loop fusion | flops 3178496 | bytes 4767744 | tf_op jit(solution)/shard_map/grad_pathway/convert_element_type | solution.py:606
  131.1 2.8 %collective-permute-start.21 = (bf16[1552,128]{1,0:T(8,128)(2,1)}, bf16[1552,128]{1,0:T(8,128)(2,1)S(1)}, u32[]{:S(2)}, u32[]{:S(2)}) collective-permute-start(bf16[1552,128]{1,0:T(8,128)(2,1)} %get-tuple-element.51), channel_id=1, source_target_pairs={{0,6},{2,4},{4,2},{6,0},{8,14},{10,12},{12,10},{14,8},{16,22},{18,... | collective-permute-start | bytes 1191944 | tf_op jit(solution)/shard_map/grad_pathway/ppermute | solution.py:500
  134.6 4.3 %all-to-all-done.1 = bf16[4,32,3072]{2,1,0:T(8,128)(2,1)S(1)} async-done(((bf16[4,32,3072]{2,1,0:T(8,128)(2,1)}), bf16[4,32,3072]{2,1,0:T(8,128)(2,1)S(1)}, u32[]{:S(2)}, u32[]{:S(2)}) %all-to-all-start.1) | async-done | bytes 786464 | tf_op jit(solution)/shard_map/link_grads/all_to_all | solution.py:510
  138.9 6.8 %gene_backward.1 = bf16[16,49152]{1,0:T(8,128)(2,1)} custom-call(s32[192]{0:T(256)S(1)} %copy-done.10, bf16[128,49152]{1,0:T(8,128)(2,1)} %geno_hbm.3, bf16[128,3072]{1,0:T(8,128)(2,1)S(1)} %bitcast.27), custom_call_target="tpu_custom_call" | custom-call | flops 1006632960 | bytes 28311552 | tf_op jit(solution)/shard_map/grad_gene/gene_backward/pallas_call | solution.py:205
  145.8 2.6 %collective-permute-done.21.refs_3_ = bf16[1552,128]{1,0:T(8,128)(2,1)S(1)} collective-permute-done((bf16[1552,128]{1,0:T(8,128)(2,1)}, bf16[1552,128]{1,0:T(8,128)(2,1)S(1)}, u32[]{:S(2)}, u32[]{:S(2)}) %collective-permute-start.21) | collective-permute-done | bytes 397344 | tf_op jit(solution)/shard_map/grad_pathway/ppermute | solution.py:500
  148.4 7.2 %collective-permute-done.20.refs_2_ = bf16[1552,128]{1,0:T(8,128)(2,1)S(1)} collective-permute-done((bf16[1552,128]{1,0:T(8,128)(2,1)S(1)}, bf16[1552,128]{1,0:T(8,128)(2,1)S(1)}, u32[]{:S(2)}, u32[]{:S(2)}) %collective-permute-start.20) | collective-permute-done | bytes 397344 | tf_op jit(solution)/shard_map/grad_pathway/ppermute | solution.py:500
  156.9 2.4 %collective-permute-done.23 = bf16[16,49152]{1,0:T(8,128)(2,1)} collective-permute-done((bf16[16,49152]{1,0:T(8,128)(2,1)}, bf16[16,49152]{1,0:T(8,128)(2,1)}, u32[]{:S(2)}, u32[]{:S(2)}) %collective-permute-start.23) | collective-permute-done | bytes 1572896 | tf_op jit(solution)/shard_map/grad_pathway/ppermute | solution.py:507
  159.4 3.4 %convert_add_fusion = f32[16,49152]{1,0:T(8,128)} fusion(bf16[16,49152]{1,0:T(8,128)(2,1)} %collective-permute-done.23, bf16[16,49152]{1,0:T(8,128)(2,1)S(1)} %copy-done.17), kind=kLoop, calls=%fused_computation | loop fusion | flops 2359296 | bytes 6291456 | tf_op jit(solution)/shard_map/grad_pathway/add | solution.py:617
  (134 shorter events, 31.3 us)
Async XLA Ops:
  3.1 20.1 %collective-permute-start.2 = (bf16[1552,128]{1,0:T(8,128)(2,1)S(1)}, bf16[1552,128]{1,0:T(8,128)(2,1)S(1)}, u32[]{:S(2)}, u32[]{:S(2)}) collective-permute-start(bf16[1552,128]{1,0:T(8,128)(2,1)S(1)} %fold_links.2.refs_0_), channel_id=1, source_target_pairs={{0,6},{2,4},{4,2},{6,0},{8,14},{10,12},{12,10},{14,8},{16,22},{18,... | collective-permute-start | bytes 1191944 | tf_op jit(solution)/shard_map/link_weights/ppermute | solution.py:500
  7.0 18.1 %collective-permute-start.1 = (bf16[1552,128]{1,0:T(8,128)(2,1)S(1)}, bf16[1552,128]{1,0:T(8,128)(2,1)S(1)}, u32[]{:S(2)}, u32[]{:S(2)}) collective-permute-start(bf16[1552,128]{1,0:T(8,128)(2,1)S(1)} %fold_links.2.refs_0_), channel_id=1, source_target_pairs={{0,4},{2,6},{4,0},{6,2},{8,12},{10,14},{12,8},{14,10},{16,20},{18,... | collective-permute-start | bytes 1191944 | tf_op jit(solution)/shard_map/link_weights/ppermute | solution.py:500
  7.5 18.8 %collective-permute-start = (bf16[1552,128]{1,0:T(8,128)(2,1)S(1)}, bf16[1552,128]{1,0:T(8,128)(2,1)}, u32[]{:S(2)}, u32[]{:S(2)}) collective-permute-start(bf16[1552,128]{1,0:T(8,128)(2,1)S(1)} %fold_links.2.refs_0_), channel_id=1, source_target_pairs={{0,2},{2,0},{4,6},{6,4},{8,10},{10,8},{12,14},{14,12},{16,18},{18,... | collective-permute-start | bytes 1191944 | tf_op jit(solution)/shard_map/link_weights/ppermute | solution.py:500
  17.7 15.8 %all-to-all-start = ((bf16[4,32,3072]{2,1,0:T(8,128)(2,1)}), bf16[4,32,3072]{2,1,0:T(8,128)(2,1)S(1)}, u32[]{:S(2)}, u32[]{:S(2)}) async-start(bf16[4,32,3072]{2,1,0:T(8,128)(2,1)} %bitcast.3), calls=%async_computation | async-start | bytes 1572864 | tf_op jit(solution)/shard_map/hidden/all_to_all | solution.py:510
  23.2 10.4 %collective-permute-start.5 = (bf16[1552,128]{1,0:T(8,128)(2,1)S(1)}, bf16[1552,128]{1,0:T(8,128)(2,1)S(1)}, u32[]{:S(2)}, u32[]{:S(2)}) collective-permute-start(bf16[1552,128]{1,0:T(8,128)(2,1)S(1)} %collective-permute-done.2.refs_3_), channel_id=1, source_target_pairs={{0,1},{1,0},{2,3},{3,2},{4,5},{5,4},{6,7},{7,6},{8,9},{9,8},{10,11... | collective-permute-start | bytes 1191944 | tf_op jit(solution)/shard_map/link_weights/ppermute | solution.py:507
  25.2 9.1 %collective-permute-start.4 = (bf16[1552,128]{1,0:T(8,128)(2,1)S(1)}, bf16[1552,128]{1,0:T(8,128)(2,1)}, u32[]{:S(2)}, u32[]{:S(2)}) collective-permute-start(bf16[1552,128]{1,0:T(8,128)(2,1)S(1)} %collective-permute-done.1.refs_2_), channel_id=1, source_target_pairs={{0,1},{1,0},{2,3},{3,2},{4,5},{5,4},{6,7},{7,6},{8,9},{9,8},{10,11... | collective-permute-start | bytes 1191944 | tf_op jit(solution)/shard_map/link_weights/ppermute | solution.py:507
  26.3 8.0 %collective-permute-start.3 = (bf16[1552,128]{1,0:T(8,128)(2,1)}, bf16[1552,128]{1,0:T(8,128)(2,1)}, u32[]{:S(2)}, u32[]{:S(2)}) collective-permute-start(bf16[1552,128]{1,0:T(8,128)(2,1)} %collective-permute-done.refs_1_), channel_id=1, source_target_pairs={{0,1},{1,0},{2,3},{3,2},{4,5},{5,4},{6,7},{7,6},{8,9},{9,8},{10,11... | collective-permute-start | bytes 1191944 | tf_op jit(solution)/shard_map/link_weights/ppermute | solution.py:507
  42.6 9.3 %collective-permute-start.6 = (bf16[64,16,128]{2,1,0:T(8,128)(2,1)S(1)}, bf16[64,16,128]{2,1,0:T(8,128)(2,1)S(1)}, u32[]{:S(2)}, u32[]{:S(2)}) collective-permute-start(bf16[64,16,128]{2,1,0:T(8,128)(2,1)S(1)} %get-tuple-element.30), channel_id=1, source_target_pairs={{0,8},{2,10},{4,12},{6,14},{8,0},{10,2},{12,4},{14,6},{16,24},{18,... | collective-permute-start | bytes 786440 | tf_op jit(solution)/shard_map/pathway_sum/ppermute | solution.py:504
  44.2 17.9 %collective-permute-start.9 = (bf16[64,16,128]{2,1,0:T(8,128)(2,1)S(1)}, bf16[64,16,128]{2,1,0:T(8,128)(2,1)S(1)}, u32[]{:S(2)}, u32[]{:S(2)}) collective-permute-start(bf16[64,16,128]{2,1,0:T(8,128)(2,1)S(1)} %get-tuple-element.35), channel_id=1, source_target_pairs={{0,8},{2,10},{4,12},{6,14},{8,0},{10,2},{12,4},{14,6},{16,24},{18,... | collective-permute-start | bytes 786440 | tf_op jit(solution)/shard_map/pathway_sum/ppermute | solution.py:504
  51.9 21.5 %collective-permute-start.7 = (bf16[64,16,128]{2,1,0:T(8,128)(2,1)S(1)}, bf16[64,16,128]{2,1,0:T(8,128)(2,1)S(1)}, u32[]{:S(2)}, u32[]{:S(2)}) collective-permute-start(bf16[64,16,128]{2,1,0:T(8,128)(2,1)S(1)} %add_convert_fusion.5), channel_id=1, source_target_pairs={{0,16},{2,18},{4,20},{6,22},{8,24},{10,26},{12,28},{14,30},{16,0},... | collective-permute-start | bytes 786440 | tf_op jit(solution)/shard_map/pathway_sum/ppermute | solution.py:504
  54.5 18.8 %collective-permute-start.8 = (bf16[64,16,128]{2,1,0:T(8,128)(2,1)S(1)}, bf16[64,16,128]{2,1,0:T(8,128)(2,1)S(1)}, u32[]{:S(2)}, u32[]{:S(2)}) collective-permute-start(bf16[64,16,128]{2,1,0:T(8,128)(2,1)S(1)} %get-tuple-element.32), channel_id=1, source_target_pairs={{0,8},{2,10},{4,12},{6,14},{8,0},{10,2},{12,4},{14,6},{16,24},{18,... | collective-permute-start | bytes 786440 | tf_op jit(solution)/shard_map/pathway_sum/ppermute | solution.py:504
  62.2 14.9 %collective-permute-start.10 = (bf16[64,16,128]{2,1,0:T(8,128)(2,1)S(1)}, bf16[64,16,128]{2,1,0:T(8,128)(2,1)S(1)}, u32[]{:S(2)}, u32[]{:S(2)}) collective-permute-start(bf16[64,16,128]{2,1,0:T(8,128)(2,1)S(1)} %add_convert_fusion.4), channel_id=1, source_target_pairs={{0,16},{2,18},{4,20},{6,22},{8,24},{10,26},{12,28},{14,30},{16,0},... | collective-permute-start | bytes 786440 | tf_op jit(solution)/shard_map/pathway_sum/ppermute | solution.py:504
  62.3 22.3 %collective-permute-start.11 = (bf16[64,16,128]{2,1,0:T(8,128)(2,1)S(1)}, bf16[64,16,128]{2,1,0:T(8,128)(2,1)S(1)}, u32[]{:S(2)}, u32[]{:S(2)}) collective-permute-start(bf16[64,16,128]{2,1,0:T(8,128)(2,1)S(1)} %get-tuple-element.38), channel_id=1, source_target_pairs={{0,8},{2,10},{4,12},{6,14},{8,0},{10,2},{12,4},{14,6},{16,24},{18,... | collective-permute-start | bytes 786440 | tf_op jit(solution)/shard_map/pathway_sum/ppermute | solution.py:504
  73.6 16.0 %collective-permute-start.14 = (bf16[64,16,128]{2,1,0:T(8,128)(2,1)S(1)}, bf16[64,16,128]{2,1,0:T(8,128)(2,1)S(1)}, u32[]{:S(2)}, u32[]{:S(2)}) collective-permute-start(bf16[64,16,128]{2,1,0:T(8,128)(2,1)S(1)} %multiply_convert_fusion.1.refs_8_), channel_id=1, source_target_pairs={{0,16},{2,18},{4,20},{6,22},{8,24},{10,26},{12,28},{14,30},{16,0},... | collective-permute-start | bytes 786440 | tf_op jit(solution)/shard_map/pathway_delta/ppermute | solution.py:504
  73.7 17.8 %collective-permute-start.12 = (bf16[64,16,128]{2,1,0:T(8,128)(2,1)S(1)}, bf16[64,16,128]{2,1,0:T(8,128)(2,1)S(1)}, u32[]{:S(2)}, u32[]{:S(2)}) collective-permute-start(bf16[64,16,128]{2,1,0:T(8,128)(2,1)S(1)} %multiply_convert_fusion.1.refs_8_), channel_id=1, source_target_pairs={{0,8},{2,10},{4,12},{6,14},{8,0},{10,2},{12,4},{14,6},{16,24},{18,... | collective-permute-start | bytes 786440 | tf_op jit(solution)/shard_map/pathway_delta/ppermute | solution.py:504
  85.1 13.9 %collective-permute-start.17 = (bf16[64,16,128]{2,1,0:T(8,128)(2,1)S(1)}, bf16[64,16,128]{2,1,0:T(8,128)(2,1)S(1)}, u32[]{:S(2)}, u32[]{:S(2)}) collective-permute-start(bf16[64,16,128]{2,1,0:T(8,128)(2,1)S(1)} %get-tuple-element.57.refs_9_), channel_id=1, source_target_pairs={{0,24},{2,26},{4,28},{6,30},{8,16},{10,18},{12,20},{14,22},{16,8},... | collective-permute-start | bytes 786440 | tf_op jit(solution)/shard_map/pathway_delta/ppermute | solution.py:504
  87.0 23.0 %collective-permute-start.15 = (bf16[64,16,128]{2,1,0:T(8,128)(2,1)S(1)}, bf16[64,16,128]{2,1,0:T(8,128)(2,1)S(1)}, u32[]{:S(2)}, u32[]{:S(2)}) collective-permute-start(bf16[64,16,128]{2,1,0:T(8,128)(2,1)S(1)} %get-tuple-element.57.refs_9_), channel_id=1, source_target_pairs={{0,16},{2,18},{4,20},{6,22},{8,24},{10,26},{12,28},{14,30},{16,0},... | collective-permute-start | bytes 786440 | tf_op jit(solution)/shard_map/pathway_delta/ppermute | solution.py:504
  87.0 23.0 %collective-permute-start.13 = (bf16[64,16,128]{2,1,0:T(8,128)(2,1)S(1)}, bf16[64,16,128]{2,1,0:T(8,128)(2,1)S(1)}, u32[]{:S(2)}, u32[]{:S(2)}) collective-permute-start(bf16[64,16,128]{2,1,0:T(8,128)(2,1)S(1)} %get-tuple-element.57.refs_9_), channel_id=1, source_target_pairs={{0,8},{2,10},{4,12},{6,14},{8,0},{10,2},{12,4},{14,6},{16,24},{18,... | collective-permute-start | bytes 786440 | tf_op jit(solution)/shard_map/pathway_delta/ppermute | solution.py:504
  89.6 22.6 %collective-permute-start.16 = (bf16[64,16,128]{2,1,0:T(8,128)(2,1)S(1)}, bf16[64,16,128]{2,1,0:T(8,128)(2,1)S(1)}, u32[]{:S(2)}, u32[]{:S(2)}) collective-permute-start(bf16[64,16,128]{2,1,0:T(8,128)(2,1)S(1)} %collective-permute-done.14.refs_12_), channel_id=1, source_target_pairs={{0,8},{2,10},{4,12},{6,14},{8,0},{10,2},{12,4},{14,6},{16,24},{18,... | collective-permute-start | bytes 786440 | tf_op jit(solution)/shard_map/pathway_delta/ppermute | solution.py:504
  123.3 15.6 %all-to-all-start.1 = ((bf16[4,32,3072]{2,1,0:T(8,128)(2,1)}), bf16[4,32,3072]{2,1,0:T(8,128)(2,1)S(1)}, u32[]{:S(2)}, u32[]{:S(2)}) async-start(bf16[4,32,3072]{2,1,0:T(8,128)(2,1)} %get-tuple-element.39), calls=%async_computation.1 | async-start | bytes 1572864 | tf_op jit(solution)/shard_map/link_grads/all_to_all | solution.py:510
  131.1 17.3 %collective-permute-start.21 = (bf16[1552,128]{1,0:T(8,128)(2,1)}, bf16[1552,128]{1,0:T(8,128)(2,1)S(1)}, u32[]{:S(2)}, u32[]{:S(2)}) collective-permute-start(bf16[1552,128]{1,0:T(8,128)(2,1)} %get-tuple-element.51), channel_id=1, source_target_pairs={{0,6},{2,4},{4,2},{6,0},{8,14},{10,12},{12,10},{14,8},{16,22},{18,... | collective-permute-start | bytes 1191944 | tf_op jit(solution)/shard_map/grad_pathway/ppermute | solution.py:500
  133.9 21.7 %collective-permute-start.20 = (bf16[1552,128]{1,0:T(8,128)(2,1)S(1)}, bf16[1552,128]{1,0:T(8,128)(2,1)S(1)}, u32[]{:S(2)}, u32[]{:S(2)}) collective-permute-start(bf16[1552,128]{1,0:T(8,128)(2,1)S(1)} %get-tuple-element.52), channel_id=1, source_target_pairs={{0,4},{2,6},{4,0},{6,2},{8,12},{10,14},{12,8},{14,10},{16,20},{18,... | collective-permute-start | bytes 1191944 | tf_op jit(solution)/shard_map/grad_pathway/ppermute | solution.py:500
  134.4 21.2 %collective-permute-start.19 = (bf16[1552,128]{1,0:T(8,128)(2,1)S(1)}, bf16[1552,128]{1,0:T(8,128)(2,1)S(1)}, u32[]{:S(2)}, u32[]{:S(2)}) collective-permute-start(bf16[1552,128]{1,0:T(8,128)(2,1)S(1)} %get-tuple-element.53), channel_id=1, source_target_pairs={{0,2},{2,0},{4,6},{6,4},{8,10},{10,8},{12,14},{14,12},{16,18},{18,... | collective-permute-start | bytes 1191944 | tf_op jit(solution)/shard_map/grad_pathway/ppermute | solution.py:500
  156.4 6.4 %collective-permute-start.22 = (f32[200,1024]{1,0:T(8,128)S(1)}, f32[200,1024]{1,0:T(8,128)S(1)}, u32[]{:S(2)}, u32[]{:S(2)}) collective-permute-start(f32[200,1024]{1,0:T(8,128)S(1)} %unfold_sum.1), channel_id=1, source_target_pairs={{0,1},{1,0},{2,3},{3,2},{4,5},{5,4},{6,7},{7,6},{8,9},{9,8},{10,11... | collective-permute-start | bytes 2457608 | tf_op jit(solution)/shard_map/grad_pathway/ppermute | solution.py:507
  (31 other events, 352.5 us)

commit v5 on v4

--- a/solution.py
+++ b/solution.py
@@ -67,24 +67,33 @@
     cols = blocks * BLOCK
     chunks = geno.shape[1] // cols
 
-    def copies(c):
-        at = pl.ds(pl.multiple_of(c * cols, cols), cols)
+    def copies(c, start, size):
+        at = pl.ds(pl.multiple_of(start, BLOCK), size)
         return (
             pltpu.make_async_copy(geno_hbm.at[:, at], geno.at[:, at], sems.at[0, c]),
             pltpu.make_async_copy(weight_hbm.at[:, at], weight.at[:, at], sems.at[1, c]),
         )
 
-    for c in range(chunks):
-        for copy in copies(c):
+    whole = chunks - 1
+    pieces = [blocks // 2, blocks // 4, blocks // 4] if blocks % 4 == 0 else [blocks]
+    taper, begin = [], whole * cols
+    for c, count in enumerate(pieces):
+        taper.append((whole + c, begin, count))
+        begin += count * BLOCK
+    for c in range(whole):
+        for copy in copies(c, c * cols, cols):
+            copy.start()
+    for c, begin, count in taper:
+        for copy in copies(c, begin, count * BLOCK):
             copy.start()
     pre[...] = jnp.zeros_like(pre)
 
-    def chunk(c, carry):
+    def chunk(c, first, count, carry):
         gene, start = carry
-        for copy in copies(c):
+        for copy in copies(c, first, count * BLOCK):
             copy.wait()
-        for i in range(blocks):
-            base = c * cols + i * BLOCK
+        for i in range(count):
+            base = first + i * BLOCK
             at = pl.ds(pl.multiple_of(base, BLOCK), BLOCK)
             edges = window_edges(lengths, gene_count, gene, start)
             marks = reached(edges, base)
@@ -100,7 +109,10 @@
             gene, start = next_window(edges, gene, base + BLOCK)
         return gene, start
 
-    lax.fori_loop(0, chunks, chunk, (jnp.int32(0), jnp.int32(0)))
+    carry = (jnp.int32(0), jnp.int32(0))
+    carry = lax.fori_loop(0, whole, lambda c, x: chunk(c, c * cols, blocks, x), carry)
+    for c, begin, count in taper:
+        carry = chunk(c, begin, count, carry)
 
     def body(i, _):
         at = pl.multiple_of(i * LANES, LANES)
@@ -127,7 +139,7 @@
             pltpu.VMEM(genotypes.shape, jnp.bfloat16),
             pltpu.VMEM(gene_weight.shape, jnp.bfloat16),
             pltpu.VMEM(((gene_count + WINDOW) * units, samples), jnp.float32),
-            pltpu.SemaphoreType.DMA((2, var_count // (blocks * BLOCK))),
+            pltpu.SemaphoreType.DMA((2, var_count // (blocks * BLOCK) + 2)),
         ],
         compiler_params=pltpu.CompilerParams(vmem_limit_bytes=52 * MIB),
         cost_estimate=pl.CostEstimate(

time: 165 us -> 165 us (level)
  no operation moved by 1% of the time
where the time goes in v5:
time: 165 us
  waiting for transfers between devices  77.3 us (47%)
  Pallas kernels  35.9 us (22%)
  starting transfers between devices  32.4 us (20%)
  other arithmetic  9.53 us (6%)
  local copies, waits for them, and re-layouts  8.77 us (5%)
    ppermute x12, waiting for transfers between devices, swap_along(): return lax.ppermute(x, 'genes', pairs)  51.5 us
    ppermute x12, starting transfers between devices, swap_along(): return lax.ppermute(x, 'genes', pairs)  15.8 us
    ppermute x6, waiting for transfers between devices, swap_plane(): return lax.ppermute(x, 'genes', pairs)  12.4 us
    all_to_all x2, waiting for transfers between devices, spread(): lax.all_to_all(x, 'genes', split_axis=0, concat_axis=0, tiled=True, axis_...  10.9 us
    pallas_call x1, Pallas kernels, link_backward(): pl.pallas_call(functools.partial(link_backward_kernel, rows // units, uni...  10.3 us
    pallas_call x1, Pallas kernels, gene_forward(): pl.pallas_call(functools.partial(gene_forward_kernel, gene_count, blocks)...  9.63 us
    ppermute x6, starting transfers between devices, swap_plane(): return lax.ppermute(x, 'genes', pairs)  8.11 us
    all_to_all x2, starting transfers between devices, spread(): lax.all_to_all(x, 'genes', split_axis=0, concat_axis=0, tiled=True, axis_...  7.77 us
  transfers between devices with their start and end apart: 26, of which 17 were waited for; matrix products, arithmetic and copies ran while one was open for 6% of the time, Pallas kernels for 11%

profile of v5, /device:TPU:0, one launch (start us, length us, event | category | flops | bytes accessed | tf_op | source)
XLA Modules:
  0.0 165.0 jit_solution(17103021911509688766)
XLA Ops:
  3.1 4.0 %collective-permute-start.2 = (bf16[1552,128]{1,0:T(8,128)(2,1)S(1)}, bf16[1552,128]{1,0:T(8,128)(2,1)S(1)}, u32[]{:S(2)}, u32[]{:S(2)}) collective-permute-start(bf16[1552,128]{1,0:T(8,128)(2,1)S(1)} %fold_links.2.refs_0_), channel_id=1, source_target_pairs={{0,6},{2,4},{4,2},{6,0},{8,14},{10,12},{12,10},{14,8},{16,22},{18,... | collective-permute-start | bytes 1191944 | tf_op jit(solution)/shard_map/link_weights/ppermute | solution.py:512
  8.3 9.6 %gene_forward.1 = bf16[128,3072]{1,0:T(8,128)(2,1)} custom-call(s32[192]{0:T(256)S(1)} %copy-done.9, bf16[128,49152]{1,0:T(8,128)(2,1)} %geno_hbm.3, bf16[16,49152]{1,0:T(8,128)(2,1)} %weight_hbm.1), custom_call_target="tpu_custom_call" | custom-call | flops 1006632960 | bytes 14155776 | tf_op jit(solution)/shard_map/hidden/gene_forward/pallas_call | solution.py:133
  18.0 4.3 %all-to-all-start = ((bf16[4,32,3072]{2,1,0:T(8,128)(2,1)}), bf16[4,32,3072]{2,1,0:T(8,128)(2,1)S(1)}, u32[]{:S(2)}, u32[]{:S(2)}) async-start(bf16[4,32,3072]{2,1,0:T(8,128)(2,1)} %bitcast.3), calls=%async_computation | async-start | bytes 1572864 | tf_op jit(solution)/shard_map/hidden/all_to_all | solution.py:522
  27.0 6.5 %all-to-all-done.hidden = bf16[4,32,3072]{2,1,0:T(8,128)(2,1)S(1)} async-done(((bf16[4,32,3072]{2,1,0:T(8,128)(2,1)}), bf16[4,32,3072]{2,1,0:T(8,128)(2,1)S(1)}, u32[]{:S(2)}, u32[]{:S(2)}) %all-to-all-start) | async-done | bytes 786464 | tf_op jit(solution)/shard_map/hidden/all_to_all | solution.py:522
  35.3 7.2 %link_forward.1 = (bf16[64,16,128]{2,1,0:T(8,128)(2,1)S(1)}, bf16[64,16,128]{2,1,0:T(8,128)(2,1)S(1)}, bf16[64,16,128]{2,1,0:T(8,128)(2,1)S(1)}, bf16[64,16,128]...) custom-call(s32[2]{0:T(128)S(1)} %pad_add_fusion.place, ...), custom_call_target="tpu_custom_call" | custom-call | flops 4000000000 | bytes 8000000 | tf_op jit(solution)/shard_map/pathway_sum/link_forward/pallas_call | solution.py:385
  44.7 7.1 %collective-permute-done.6 = bf16[64,16,128]{2,1,0:T(8,128)(2,1)S(1)} collective-permute-done((bf16[64,16,128]{2,1,0:T(8,128)(2,1)S(1)}, bf16[64,16,128]{2,1,0:T(8,128)(2,1)S(1)}, u32[]{:S(2)}, u32[]{:S(2)}) %collective-permute-start.6) | collective-permute-done | bytes 262176 | tf_op jit(solution)/shard_map/pathway_sum/ppermute | solution.py:516
  51.9 2.6 %collective-permute-start.7 = (bf16[64,16,128]{2,1,0:T(8,128)(2,1)S(1)}, bf16[64,16,128]{2,1,0:T(8,128)(2,1)S(1)}, u32[]{:S(2)}, u32[]{:S(2)}) collective-permute-start(bf16[64,16,128]{2,1,0:T(8,128)(2,1)S(1)} %add_convert_fusion.5), channel_id=1, source_target_pairs={{0,16},{2,18},{4,20},{6,22},{8,24},{10,26},{12,28},{14,30},{16,0},... | collective-permute-start | bytes 786440 | tf_op jit(solution)/shard_map/pathway_sum/ppermute | solution.py:516
  56.1 6.0 %collective-permute-done.9 = bf16[64,16,128]{2,1,0:T(8,128)(2,1)S(1)} collective-permute-done((bf16[64,16,128]{2,1,0:T(8,128)(2,1)S(1)}, bf16[64,16,128]{2,1,0:T(8,128)(2,1)S(1)}, u32[]{:S(2)}, u32[]{:S(2)}) %collective-permute-start.9) | collective-permute-done | bytes 262176 | tf_op jit(solution)/shard_map/pathway_sum/ppermute | solution.py:516
  62.3 2.4 %collective-permute-start.11 = (bf16[64,16,128]{2,1,0:T(8,128)(2,1)S(1)}, bf16[64,16,128]{2,1,0:T(8,128)(2,1)S(1)}, u32[]{:S(2)}, u32[]{:S(2)}) collective-permute-start(bf16[64,16,128]{2,1,0:T(8,128)(2,1)S(1)} %get-tuple-element.38), channel_id=1, source_target_pairs={{0,8},{2,10},{4,12},{6,14},{8,0},{10,2},{12,4},{14,6},{16,24},{18,... | collective-permute-start | bytes 786440 | tf_op jit(solution)/shard_map/pathway_sum/ppermute | solution.py:516
  65.1 8.3 %collective-permute-done.8 = bf16[64,16,128]{2,1,0:T(8,128)(2,1)S(1)} collective-permute-done((bf16[64,16,128]{2,1,0:T(8,128)(2,1)S(1)}, bf16[64,16,128]{2,1,0:T(8,128)(2,1)S(1)}, u32[]{:S(2)}, u32[]{:S(2)}) %collective-permute-start.8) | collective-permute-done | bytes 262176 | tf_op jit(solution)/shard_map/pathway_sum/ppermute | solution.py:516
  77.1 7.5 %collective-permute-done.11 = bf16[64,16,128]{2,1,0:T(8,128)(2,1)S(1)} collective-permute-done((bf16[64,16,128]{2,1,0:T(8,128)(2,1)S(1)}, bf16[64,16,128]{2,1,0:T(8,128)(2,1)S(1)}, u32[]{:S(2)}, u32[]{:S(2)}) %collective-permute-start.11) | collective-permute-done | bytes 262176 | tf_op jit(solution)/shard_map/pathway_sum/ppermute | solution.py:516
  87.0 2.6 %collective-permute-start.13 = (bf16[64,16,128]{2,1,0:T(8,128)(2,1)S(1)}, bf16[64,16,128]{2,1,0:T(8,128)(2,1)S(1)}, u32[]{:S(2)}, u32[]{:S(2)}) collective-permute-start(bf16[64,16,128]{2,1,0:T(8,128)(2,1)S(1)} %get-tuple-element.57.refs_9_), channel_id=1, source_target_pairs={{0,8},{2,10},{4,12},{6,14},{8,0},{10,2},{12,4},{14,6},{16,24},{18,... | collective-permute-start | bytes 786440 | tf_op jit(solution)/shard_map/pathway_delta/ppermute | solution.py:516
  91.5 7.5 %collective-permute-done.17.refs_15_ = bf16[64,16,128]{2,1,0:T(8,128)(2,1)S(1)} collective-permute-done((bf16[64,16,128]{2,1,0:T(8,128)(2,1)S(1)}, bf16[64,16,128]{2,1,0:T(8,128)(2,1)S(1)}, u32[]{:S(2)}, u32[]{:S(2)}) %collective-permute-start.17) | collective-permute-done | bytes 262176 | tf_op jit(solution)/shard_map/pathway_delta/ppermute | solution.py:516
  99.0 11.0 %collective-permute-done.15.refs_13_ = bf16[64,16,128]{2,1,0:T(8,128)(2,1)S(1)} collective-permute-done((bf16[64,16,128]{2,1,0:T(8,128)(2,1)S(1)}, bf16[64,16,128]{2,1,0:T(8,128)(2,1)S(1)}, u32[]{:S(2)}, u32[]{:S(2)}) %collective-permute-start.15) | collective-permute-done | bytes 262176 | tf_op jit(solution)/shard_map/pathway_delta/ppermute | solution.py:516
  113.0 10.3 %link_backward.1 = (bf16[4,32,3072]{2,1,0:T(8,128)(2,1)}, bf16[4,1552,128]{2,1,0:T(8,128)(2,1)}, bf16[4,1552,128]{2,1,0:T(8,128)(2,1)}) custom-call(s32[2]{0:T(128)} %copy-done.16, s32[2,768]{1,0:T(2,128)} %copy-done.8, s32[512]{0:T(512)} %copy-done.11, bf16[4,32,3072]{2,1,0:T(8,128)(2,1)} %copy-done.3, f32[64,128]{1,0:T(8,128)} %reshape.72.head, ...), custom_call_target="tpu_custom_call" | custom-call | flops 6000000000 | bytes 20000000 | tf_op jit(solution)/shard_map/link_grads/link_backward/pallas_call | solution.py:465
  123.3 3.5 %all-to-all-start.1 = ((bf16[4,32,3072]{2,1,0:T(8,128)(2,1)}), bf16[4,32,3072]{2,1,0:T(8,128)(2,1)S(1)}, u32[]{:S(2)}, u32[]{:S(2)}) async-start(bf16[4,32,3072]{2,1,0:T(8,128)(2,1)} %get-tuple-element.39), calls=%async_computation.1 | async-start | bytes 1572864 | tf_op jit(solution)/shard_map/link_grads/all_to_all | solution.py:522
  128.1 3.0 %fusion.3 = (bf16[1552,128]{1,0:T(8,128)(2,1)}, bf16[1552,128]{1,0:T(8,128)(2,1)S(1)}, bf16[1552,128]{1,0:T(8,128)(2,1)S(1)}, bf16[1552,128]{1,0:T(8,128)(2,1)S(1)}) fusion(bf16[4,1552,128]{2,1,0:T(8,128)(2,1)} %copy-done.18, bf16[4,1552,128]{2,1,0:T(8,128)(2,1)} %get-tuple-element.40), kind=kLoop, calls=%fused_computation.19 | loop fusion | flops 3178496 | bytes 4767744 | tf_op jit(solution)/shard_map/grad_pathway/convert_element_type | solution.py:618
  131.1 2.8 %collective-permute-start.21 = (bf16[1552,128]{1,0:T(8,128)(2,1)}, bf16[1552,128]{1,0:T(8,128)(2,1)S(1)}, u32[]{:S(2)}, u32[]{:S(2)}) collective-permute-start(bf16[1552,128]{1,0:T(8,128)(2,1)} %get-tuple-element.51), channel_id=1, source_target_pairs={{0,6},{2,4},{4,2},{6,0},{8,14},{10,12},{12,10},{14,8},{16,22},{18,... | collective-permute-start | bytes 1191944 | tf_op jit(solution)/shard_map/grad_pathway/ppermute | solution.py:512
  134.6 4.3 %all-to-all-done.1 = bf16[4,32,3072]{2,1,0:T(8,128)(2,1)S(1)} async-done(((bf16[4,32,3072]{2,1,0:T(8,128)(2,1)}), bf16[4,32,3072]{2,1,0:T(8,128)(2,1)S(1)}, u32[]{:S(2)}, u32[]{:S(2)}) %all-to-all-start.1) | async-done | bytes 786464 | tf_op jit(solution)/shard_map/link_grads/all_to_all | solution.py:522
  139.0 6.8 %gene_backward.1 = bf16[16,49152]{1,0:T(8,128)(2,1)} custom-call(s32[192]{0:T(256)S(1)} %copy-done.10, bf16[128,49152]{1,0:T(8,128)(2,1)} %geno_hbm.3, bf16[128,3072]{1,0:T(8,128)(2,1)S(1)} %bitcast.27), custom_call_target="tpu_custom_call" | custom-call | flops 1006632960 | bytes 28311552 | tf_op jit(solution)/shard_map/grad_gene/gene_backward/pallas_call | solution.py:217
  145.7 2.7 %collective-permute-done.21.refs_3_ = bf16[1552,128]{1,0:T(8,128)(2,1)S(1)} collective-permute-done((bf16[1552,128]{1,0:T(8,128)(2,1)}, bf16[1552,128]{1,0:T(8,128)(2,1)S(1)}, u32[]{:S(2)}, u32[]{:S(2)}) %collective-permute-start.21) | collective-permute-done | bytes 397344 | tf_op jit(solution)/shard_map/grad_pathway/ppermute | solution.py:512
  148.4 7.2 %collective-permute-done.20.refs_2_ = bf16[1552,128]{1,0:T(8,128)(2,1)S(1)} collective-permute-done((bf16[1552,128]{1,0:T(8,128)(2,1)S(1)}, bf16[1552,128]{1,0:T(8,128)(2,1)S(1)}, u32[]{:S(2)}, u32[]{:S(2)}) %collective-permute-start.20) | collective-permute-done | bytes 397344 | tf_op jit(solution)/shard_map/grad_pathway/ppermute | solution.py:512
  157.0 2.4 %collective-permute-done.23 = bf16[16,49152]{1,0:T(8,128)(2,1)} collective-permute-done((bf16[16,49152]{1,0:T(8,128)(2,1)}, bf16[16,49152]{1,0:T(8,128)(2,1)}, u32[]{:S(2)}, u32[]{:S(2)}) %collective-permute-start.23) | collective-permute-done | bytes 1572896 | tf_op jit(solution)/shard_map/grad_pathway/ppermute | solution.py:519
  159.4 3.4 %convert_add_fusion = f32[16,49152]{1,0:T(8,128)} fusion(bf16[16,49152]{1,0:T(8,128)(2,1)} %collective-permute-done.23, bf16[16,49152]{1,0:T(8,128)(2,1)S(1)} %copy-done.17), kind=kLoop, calls=%fused_computation | loop fusion | flops 2359296 | bytes 6291456 | tf_op jit(solution)/shard_map/grad_pathway/add | solution.py:629
  (134 shorter events, 30.9 us)
Async XLA Ops:
  3.1 20.6 %collective-permute-start.2 = (bf16[1552,128]{1,0:T(8,128)(2,1)S(1)}, bf16[1552,128]{1,0:T(8,128)(2,1)S(1)}, u32[]{:S(2)}, u32[]{:S(2)}) collective-permute-start(bf16[1552,128]{1,0:T(8,128)(2,1)S(1)} %fold_links.2.refs_0_), channel_id=1, source_target_pairs={{0,6},{2,4},{4,2},{6,0},{8,14},{10,12},{12,10},{14,8},{16,22},{18,... | collective-permute-start | bytes 1191944 | tf_op jit(solution)/shard_map/link_weights/ppermute | solution.py:512
  7.0 17.9 %collective-permute-start.1 = (bf16[1552,128]{1,0:T(8,128)(2,1)S(1)}, bf16[1552,128]{1,0:T(8,128)(2,1)S(1)}, u32[]{:S(2)}, u32[]{:S(2)}) collective-permute-start(bf16[1552,128]{1,0:T(8,128)(2,1)S(1)} %fold_links.2.refs_0_), channel_id=1, source_target_pairs={{0,4},{2,6},{4,0},{6,2},{8,12},{10,14},{12,8},{14,10},{16,20},{18,... | collective-permute-start | bytes 1191944 | tf_op jit(solution)/shard_map/link_weights/ppermute | solution.py:512
  7.5 18.8 %collective-permute-start = (bf16[1552,128]{1,0:T(8,128)(2,1)S(1)}, bf16[1552,128]{1,0:T(8,128)(2,1)}, u32[]{:S(2)}, u32[]{:S(2)}) collective-permute-start(bf16[1552,128]{1,0:T(8,128)(2,1)S(1)} %fold_links.2.refs_0_), channel_id=1, source_target_pairs={{0,2},{2,0},{4,6},{6,4},{8,10},{10,8},{12,14},{14,12},{16,18},{18,... | collective-permute-start | bytes 1191944 | tf_op jit(solution)/shard_map/link_weights/ppermute | solution.py:512
  18.0 15.5 %all-to-all-start = ((bf16[4,32,3072]{2,1,0:T(8,128)(2,1)}), bf16[4,32,3072]{2,1,0:T(8,128)(2,1)S(1)}, u32[]{:S(2)}, u32[]{:S(2)}) async-start(bf16[4,32,3072]{2,1,0:T(8,128)(2,1)} %bitcast.3), calls=%async_computation | async-start | bytes 1572864 | tf_op jit(solution)/shard_map/hidden/all_to_all | solution.py:522
  23.7 9.8 %collective-permute-start.5 = (bf16[1552,128]{1,0:T(8,128)(2,1)S(1)}, bf16[1552,128]{1,0:T(8,128)(2,1)S(1)}, u32[]{:S(2)}, u32[]{:S(2)}) collective-permute-start(bf16[1552,128]{1,0:T(8,128)(2,1)S(1)} %collective-permute-done.2.refs_3_), channel_id=1, source_target_pairs={{0,1},{1,0},{2,3},{3,2},{4,5},{5,4},{6,7},{7,6},{8,9},{9,8},{10,11... | collective-permute-start | bytes 1191944 | tf_op jit(solution)/shard_map/link_weights/ppermute | solution.py:519
  24.9 9.4 %collective-permute-start.4 = (bf16[1552,128]{1,0:T(8,128)(2,1)S(1)}, bf16[1552,128]{1,0:T(8,128)(2,1)}, u32[]{:S(2)}, u32[]{:S(2)}) collective-permute-start(bf16[1552,128]{1,0:T(8,128)(2,1)S(1)} %collective-permute-done.1.refs_2_), channel_id=1, source_target_pairs={{0,1},{1,0},{2,3},{3,2},{4,5},{5,4},{6,7},{7,6},{8,9},{9,8},{10,11... | collective-permute-start | bytes 1191944 | tf_op jit(solution)/shard_map/link_weights/ppermute | solution.py:519
  26.3 8.0 %collective-permute-start.3 = (bf16[1552,128]{1,0:T(8,128)(2,1)}, bf16[1552,128]{1,0:T(8,128)(2,1)}, u32[]{:S(2)}, u32[]{:S(2)}) collective-permute-start(bf16[1552,128]{1,0:T(8,128)(2,1)} %collective-permute-done.refs_1_), channel_id=1, source_target_pairs={{0,1},{1,0},{2,3},{3,2},{4,5},{5,4},{6,7},{7,6},{8,9},{9,8},{10,11... | collective-permute-start | bytes 1191944 | tf_op jit(solution)/shard_map/link_weights/ppermute | solution.py:519
  42.5 9.3 %collective-permute-start.6 = (bf16[64,16,128]{2,1,0:T(8,128)(2,1)S(1)}, bf16[64,16,128]{2,1,0:T(8,128)(2,1)S(1)}, u32[]{:S(2)}, u32[]{:S(2)}) collective-permute-start(bf16[64,16,128]{2,1,0:T(8,128)(2,1)S(1)} %get-tuple-element.30), channel_id=1, source_target_pairs={{0,8},{2,10},{4,12},{6,14},{8,0},{10,2},{12,4},{14,6},{16,24},{18,... | collective-permute-start | bytes 786440 | tf_op jit(solution)/shard_map/pathway_sum/ppermute | solution.py:516
  44.2 17.9 %collective-permute-start.9 = (bf16[64,16,128]{2,1,0:T(8,128)(2,1)S(1)}, bf16[64,16,128]{2,1,0:T(8,128)(2,1)S(1)}, u32[]{:S(2)}, u32[]{:S(2)}) collective-permute-start(bf16[64,16,128]{2,1,0:T(8,128)(2,1)S(1)} %get-tuple-element.35), channel_id=1, source_target_pairs={{0,8},{2,10},{4,12},{6,14},{8,0},{10,2},{12,4},{14,6},{16,24},{18,... | collective-permute-start | bytes 786440 | tf_op jit(solution)/shard_map/pathway_sum/ppermute | solution.py:516
  51.9 21.5 %collective-permute-start.7 = (bf16[64,16,128]{2,1,0:T(8,128)(2,1)S(1)}, bf16[64,16,128]{2,1,0:T(8,128)(2,1)S(1)}, u32[]{:S(2)}, u32[]{:S(2)}) collective-permute-start(bf16[64,16,128]{2,1,0:T(8,128)(2,1)S(1)} %add_convert_fusion.5), channel_id=1, source_target_pairs={{0,16},{2,18},{4,20},{6,22},{8,24},{10,26},{12,28},{14,30},{16,0},... | collective-permute-start | bytes 786440 | tf_op jit(solution)/shard_map/pathway_sum/ppermute | solution.py:516
  54.6 18.8 %collective-permute-start.8 = (bf16[64,16,128]{2,1,0:T(8,128)(2,1)S(1)}, bf16[64,16,128]{2,1,0:T(8,128)(2,1)S(1)}, u32[]{:S(2)}, u32[]{:S(2)}) collective-permute-start(bf16[64,16,128]{2,1,0:T(8,128)(2,1)S(1)} %get-tuple-element.32), channel_id=1, source_target_pairs={{0,8},{2,10},{4,12},{6,14},{8,0},{10,2},{12,4},{14,6},{16,24},{18,... | collective-permute-start | bytes 786440 | tf_op jit(solution)/shard_map/pathway_sum/ppermute | solution.py:516
  62.2 14.9 %collective-permute-start.10 = (bf16[64,16,128]{2,1,0:T(8,128)(2,1)S(1)}, bf16[64,16,128]{2,1,0:T(8,128)(2,1)S(1)}, u32[]{:S(2)}, u32[]{:S(2)}) collective-permute-start(bf16[64,16,128]{2,1,0:T(8,128)(2,1)S(1)} %add_convert_fusion.4), channel_id=1, source_target_pairs={{0,16},{2,18},{4,20},{6,22},{8,24},{10,26},{12,28},{14,30},{16,0},... | collective-permute-start | bytes 786440 | tf_op jit(solution)/shard_map/pathway_sum/ppermute | solution.py:516
  62.3 22.3 %collective-permute-start.11 = (bf16[64,16,128]{2,1,0:T(8,128)(2,1)S(1)}, bf16[64,16,128]{2,1,0:T(8,128)(2,1)S(1)}, u32[]{:S(2)}, u32[]{:S(2)}) collective-permute-start(bf16[64,16,128]{2,1,0:T(8,128)(2,1)S(1)} %get-tuple-element.38), channel_id=1, source_target_pairs={{0,8},{2,10},{4,12},{6,14},{8,0},{10,2},{12,4},{14,6},{16,24},{18,... | collective-permute-start | bytes 786440 | tf_op jit(solution)/shard_map/pathway_sum/ppermute | solution.py:516
  73.6 16.0 %collective-permute-start.14 = (bf16[64,16,128]{2,1,0:T(8,128)(2,1)S(1)}, bf16[64,16,128]{2,1,0:T(8,128)(2,1)S(1)}, u32[]{:S(2)}, u32[]{:S(2)}) collective-permute-start(bf16[64,16,128]{2,1,0:T(8,128)(2,1)S(1)} %multiply_convert_fusion.1.refs_8_), channel_id=1, source_target_pairs={{0,16},{2,18},{4,20},{6,22},{8,24},{10,26},{12,28},{14,30},{16,0},... | collective-permute-start | bytes 786440 | tf_op jit(solution)/shard_map/pathway_delta/ppermute | solution.py:516
  73.7 17.8 %collective-permute-start.12 = (bf16[64,16,128]{2,1,0:T(8,128)(2,1)S(1)}, bf16[64,16,128]{2,1,0:T(8,128)(2,1)S(1)}, u32[]{:S(2)}, u32[]{:S(2)}) collective-permute-start(bf16[64,16,128]{2,1,0:T(8,128)(2,1)S(1)} %multiply_convert_fusion.1.refs_8_), channel_id=1, source_target_pairs={{0,8},{2,10},{4,12},{6,14},{8,0},{10,2},{12,4},{14,6},{16,24},{18,... | collective-permute-start | bytes 786440 | tf_op jit(solution)/shard_map/pathway_delta/ppermute | solution.py:516
  85.1 13.9 %collective-permute-start.17 = (bf16[64,16,128]{2,1,0:T(8,128)(2,1)S(1)}, bf16[64,16,128]{2,1,0:T(8,128)(2,1)S(1)}, u32[]{:S(2)}, u32[]{:S(2)}) collective-permute-start(bf16[64,16,128]{2,1,0:T(8,128)(2,1)S(1)} %get-tuple-element.57.refs_9_), channel_id=1, source_target_pairs={{0,24},{2,26},{4,28},{6,30},{8,16},{10,18},{12,20},{14,22},{16,8},... | collective-permute-start | bytes 786440 | tf_op jit(solution)/shard_map/pathway_delta/ppermute | solution.py:516
  87.0 23.0 %collective-permute-start.15 = (bf16[64,16,128]{2,1,0:T(8,128)(2,1)S(1)}, bf16[64,16,128]{2,1,0:T(8,128)(2,1)S(1)}, u32[]{:S(2)}, u32[]{:S(2)}) collective-permute-start(bf16[64,16,128]{2,1,0:T(8,128)(2,1)S(1)} %get-tuple-element.57.refs_9_), channel_id=1, source_target_pairs={{0,16},{2,18},{4,20},{6,22},{8,24},{10,26},{12,28},{14,30},{16,0},... | collective-permute-start | bytes 786440 | tf_op jit(solution)/shard_map/pathway_delta/ppermute | solution.py:516
  87.0 23.0 %collective-permute-start.13 = (bf16[64,16,128]{2,1,0:T(8,128)(2,1)S(1)}, bf16[64,16,128]{2,1,0:T(8,128)(2,1)S(1)}, u32[]{:S(2)}, u32[]{:S(2)}) collective-permute-start(bf16[64,16,128]{2,1,0:T(8,128)(2,1)S(1)} %get-tuple-element.57.refs_9_), channel_id=1, source_target_pairs={{0,8},{2,10},{4,12},{6,14},{8,0},{10,2},{12,4},{14,6},{16,24},{18,... | collective-permute-start | bytes 786440 | tf_op jit(solution)/shard_map/pathway_delta/ppermute | solution.py:516
  89.6 22.6 %collective-permute-start.16 = (bf16[64,16,128]{2,1,0:T(8,128)(2,1)S(1)}, bf16[64,16,128]{2,1,0:T(8,128)(2,1)S(1)}, u32[]{:S(2)}, u32[]{:S(2)}) collective-permute-start(bf16[64,16,128]{2,1,0:T(8,128)(2,1)S(1)} %collective-permute-done.14.refs_12_), channel_id=1, source_target_pairs={{0,8},{2,10},{4,12},{6,14},{8,0},{10,2},{12,4},{14,6},{16,24},{18,... | collective-permute-start | bytes 786440 | tf_op jit(solution)/shard_map/pathway_delta/ppermute | solution.py:516
  123.3 15.6 %all-to-all-start.1 = ((bf16[4,32,3072]{2,1,0:T(8,128)(2,1)}), bf16[4,32,3072]{2,1,0:T(8,128)(2,1)S(1)}, u32[]{:S(2)}, u32[]{:S(2)}) async-start(bf16[4,32,3072]{2,1,0:T(8,128)(2,1)} %get-tuple-element.39), calls=%async_computation.1 | async-start | bytes 1572864 | tf_op jit(solution)/shard_map/link_grads/all_to_all | solution.py:522
  131.1 17.3 %collective-permute-start.21 = (bf16[1552,128]{1,0:T(8,128)(2,1)}, bf16[1552,128]{1,0:T(8,128)(2,1)S(1)}, u32[]{:S(2)}, u32[]{:S(2)}) collective-permute-start(bf16[1552,128]{1,0:T(8,128)(2,1)} %get-tuple-element.51), channel_id=1, source_target_pairs={{0,6},{2,4},{4,2},{6,0},{8,14},{10,12},{12,10},{14,8},{16,22},{18,... | collective-permute-start | bytes 1191944 | tf_op jit(solution)/shard_map/grad_pathway/ppermute | solution.py:512
  133.9 21.7 %collective-permute-start.20 = (bf16[1552,128]{1,0:T(8,128)(2,1)S(1)}, bf16[1552,128]{1,0:T(8,128)(2,1)S(1)}, u32[]{:S(2)}, u32[]{:S(2)}) collective-permute-start(bf16[1552,128]{1,0:T(8,128)(2,1)S(1)} %get-tuple-element.52), channel_id=1, source_target_pairs={{0,4},{2,6},{4,0},{6,2},{8,12},{10,14},{12,8},{14,10},{16,20},{18,... | collective-permute-start | bytes 1191944 | tf_op jit(solution)/shard_map/grad_pathway/ppermute | solution.py:512
  134.5 21.2 %collective-permute-start.19 = (bf16[1552,128]{1,0:T(8,128)(2,1)S(1)}, bf16[1552,128]{1,0:T(8,128)(2,1)S(1)}, u32[]{:S(2)}, u32[]{:S(2)}) collective-permute-start(bf16[1552,128]{1,0:T(8,128)(2,1)S(1)} %get-tuple-element.53), channel_id=1, source_target_pairs={{0,2},{2,0},{4,6},{6,4},{8,10},{10,8},{12,14},{14,12},{16,18},{18,... | collective-permute-start | bytes 1191944 | tf_op jit(solution)/shard_map/grad_pathway/ppermute | solution.py:512
  156.4 6.4 %collective-permute-start.22 = (f32[200,1024]{1,0:T(8,128)S(1)}, f32[200,1024]{1,0:T(8,128)S(1)}, u32[]{:S(2)}, u32[]{:S(2)}) collective-permute-start(f32[200,1024]{1,0:T(8,128)S(1)} %unfold_sum.1), channel_id=1, source_target_pairs={{0,1},{1,0},{2,3},{3,2},{4,5},{5,4},{6,7},{7,6},{8,9},{9,8},{10,11... | collective-permute-start | bytes 2457608 | tf_op jit(solution)/shard_map/grad_pathway/ppermute | solution.py:519
  (31 other events, 351.1 us)

commit v6 on v5

--- a/solution.py
+++ b/solution.py
@@ -473,7 +473,7 @@
             pltpu.VMEM((slots.shape[0], ROWS, LANES), jnp.bfloat16),
             pltpu.SemaphoreType.DMA((2 * GROUP,)),
         ],
-        compiler_params=pltpu.CompilerParams(vmem_limit_bytes=56 * MIB),
+        compiler_params=pltpu.CompilerParams(vmem_limit_bytes=53 * MIB),
         cost_estimate=pl.CostEstimate(
             flops=6 * 10**9, bytes_accessed=20 * 10**6, transcendentals=0
         ),

time: 165 us -> 165 us (level)
    unnamed x58 -> x46, local copies, waits for them, and re-layouts: 6.25 us -> 6.24 us
where the time goes in v6:
time: 165 us
  waiting for transfers between devices  77.9 us (47%)
  Pallas kernels  35.7 us (22%)
  starting transfers between devices  32.4 us (20%)
  other arithmetic  9.55 us (6%)
  local copies, waits for them, and re-layouts  8.16 us (5%)
    ppermute x12, waiting for transfers between devices, swap_along(): return lax.ppermute(x, 'genes', pairs)  52 us
    ppermute x12, starting transfers between devices, swap_along(): return lax.ppermute(x, 'genes', pairs)  15.8 us
    ppermute x6, waiting for transfers between devices, swap_plane(): return lax.ppermute(x, 'genes', pairs)  12.4 us
    all_to_all x2, waiting for transfers between devices, spread(): lax.all_to_all(x, 'genes', split_axis=0, concat_axis=0, tiled=True, axis_...  10.8 us
    pallas_call x1, Pallas kernels, link_backward(): pl.pallas_call(functools.partial(link_backward_kernel, rows // units, uni...  10 us
    pallas_call x1, Pallas kernels, gene_forward(): pl.pallas_call(functools.partial(gene_forward_kernel, gene_count, blocks)...  9.64 us
    ppermute x6, starting transfers between devices, swap_plane(): return lax.ppermute(x, 'genes', pairs)  8.11 us
    all_to_all x2, starting transfers between devices, spread(): lax.all_to_all(x, 'genes', split_axis=0, concat_axis=0, tiled=True, axis_...  7.76 us
  transfers between devices with their start and end apart: 26, of which 17 were waited for; matrix products, arithmetic and copies ran while one was open for 6% of the time, Pallas kernels for 11%

profile of v6, /device:TPU:0, one launch (start us, length us, event | category | flops | bytes accessed | tf_op | source)
XLA Modules:
  0.0 164.7 jit_solution(291745232532715576)
XLA Ops:
  3.1 4.0 %collective-permute-start.2 = (bf16[1552,128]{1,0:T(8,128)(2,1)S(1)}, bf16[1552,128]{1,0:T(8,128)(2,1)S(1)}, u32[]{:S(2)}, u32[]{:S(2)}) collective-permute-start(bf16[1552,128]{1,0:T(8,128)(2,1)S(1)} %fold_links.2.refs_0_), channel_id=1, source_target_pairs={{0,6},{2,4},{4,2},{6,0},{8,14},{10,12},{12,10},{14,8},{16,22},{18,... | collective-permute-start | bytes 1191944 | tf_op jit(solution)/shard_map/link_weights/ppermute | solution.py:512
  8.3 9.6 %gene_forward.1 = bf16[128,3072]{1,0:T(8,128)(2,1)} custom-call(s32[192]{0:T(256)S(1)} %copy-done.8, bf16[128,49152]{1,0:T(8,128)(2,1)} %geno_hbm.3, bf16[16,49152]{1,0:T(8,128)(2,1)} %weight_hbm.1), custom_call_target="tpu_custom_call" | custom-call | flops 1006632960 | bytes 14155776 | tf_op jit(solution)/shard_map/hidden/gene_forward/pallas_call | solution.py:133
  18.1 4.3 %all-to-all-start = ((bf16[4,32,3072]{2,1,0:T(8,128)(2,1)}), bf16[4,32,3072]{2,1,0:T(8,128)(2,1)S(1)}, u32[]{:S(2)}, u32[]{:S(2)}) async-start(bf16[4,32,3072]{2,1,0:T(8,128)(2,1)} %bitcast.3), calls=%async_computation | async-start | bytes 1572864 | tf_op jit(solution)/shard_map/hidden/all_to_all | solution.py:522
  27.0 6.5 %all-to-all-done.hidden = bf16[4,32,3072]{2,1,0:T(8,128)(2,1)S(1)} async-done(((bf16[4,32,3072]{2,1,0:T(8,128)(2,1)}), bf16[4,32,3072]{2,1,0:T(8,128)(2,1)S(1)}, u32[]{:S(2)}, u32[]{:S(2)}) %all-to-all-start) | async-done | bytes 786464 | tf_op jit(solution)/shard_map/hidden/all_to_all | solution.py:522
  35.3 7.2 %link_forward.1 = (bf16[64,16,128]{2,1,0:T(8,128)(2,1)S(1)}, bf16[64,16,128]{2,1,0:T(8,128)(2,1)S(1)}, bf16[64,16,128]{2,1,0:T(8,128)(2,1)S(1)}, bf16[64,16,128]...) custom-call(s32[2]{0:T(128)S(1)} %pad_add_fusion.place, ...), custom_call_target="tpu_custom_call" | custom-call | flops 4000000000 | bytes 8000000 | tf_op jit(solution)/shard_map/pathway_sum/link_forward/pallas_call | solution.py:385
  44.7 7.1 %collective-permute-done.6 = bf16[64,16,128]{2,1,0:T(8,128)(2,1)S(1)} collective-permute-done((bf16[64,16,128]{2,1,0:T(8,128)(2,1)S(1)}, bf16[64,16,128]{2,1,0:T(8,128)(2,1)S(1)}, u32[]{:S(2)}, u32[]{:S(2)}) %collective-permute-start.6) | collective-permute-done | bytes 262176 | tf_op jit(solution)/shard_map/pathway_sum/ppermute | solution.py:516
  51.9 2.6 %collective-permute-start.7 = (bf16[64,16,128]{2,1,0:T(8,128)(2,1)S(1)}, bf16[64,16,128]{2,1,0:T(8,128)(2,1)S(1)}, u32[]{:S(2)}, u32[]{:S(2)}) collective-permute-start(bf16[64,16,128]{2,1,0:T(8,128)(2,1)S(1)} %add_convert_fusion.5), channel_id=1, source_target_pairs={{0,16},{2,18},{4,20},{6,22},{8,24},{10,26},{12,28},{14,30},{16,0},... | collective-permute-start | bytes 786440 | tf_op jit(solution)/shard_map/pathway_sum/ppermute | solution.py:516
  56.1 6.0 %collective-permute-done.9 = bf16[64,16,128]{2,1,0:T(8,128)(2,1)S(1)} collective-permute-done((bf16[64,16,128]{2,1,0:T(8,128)(2,1)S(1)}, bf16[64,16,128]{2,1,0:T(8,128)(2,1)S(1)}, u32[]{:S(2)}, u32[]{:S(2)}) %collective-permute-start.9) | collective-permute-done | bytes 262176 | tf_op jit(solution)/shard_map/pathway_sum/ppermute | solution.py:516
  62.3 2.4 %collective-permute-start.11 = (bf16[64,16,128]{2,1,0:T(8,128)(2,1)S(1)}, bf16[64,16,128]{2,1,0:T(8,128)(2,1)S(1)}, u32[]{:S(2)}, u32[]{:S(2)}) collective-permute-start(bf16[64,16,128]{2,1,0:T(8,128)(2,1)S(1)} %get-tuple-element.38), channel_id=1, source_target_pairs={{0,8},{2,10},{4,12},{6,14},{8,0},{10,2},{12,4},{14,6},{16,24},{18,... | collective-permute-start | bytes 786440 | tf_op jit(solution)/shard_map/pathway_sum/ppermute | solution.py:516
  65.0 8.3 %collective-permute-done.8 = bf16[64,16,128]{2,1,0:T(8,128)(2,1)S(1)} collective-permute-done((bf16[64,16,128]{2,1,0:T(8,128)(2,1)S(1)}, bf16[64,16,128]{2,1,0:T(8,128)(2,1)S(1)}, u32[]{:S(2)}, u32[]{:S(2)}) %collective-permute-start.8) | collective-permute-done | bytes 262176 | tf_op jit(solution)/shard_map/pathway_sum/ppermute | solution.py:516
  77.1 7.5 %collective-permute-done.11 = bf16[64,16,128]{2,1,0:T(8,128)(2,1)S(1)} collective-permute-done((bf16[64,16,128]{2,1,0:T(8,128)(2,1)S(1)}, bf16[64,16,128]{2,1,0:T(8,128)(2,1)S(1)}, u32[]{:S(2)}, u32[]{:S(2)}) %collective-permute-start.11) | collective-permute-done | bytes 262176 | tf_op jit(solution)/shard_map/pathway_sum/ppermute | solution.py:516
  87.0 2.6 %collective-permute-start.13 = (bf16[64,16,128]{2,1,0:T(8,128)(2,1)S(1)}, bf16[64,16,128]{2,1,0:T(8,128)(2,1)S(1)}, u32[]{:S(2)}, u32[]{:S(2)}) collective-permute-start(bf16[64,16,128]{2,1,0:T(8,128)(2,1)S(1)} %get-tuple-element.57.refs_9_), channel_id=1, source_target_pairs={{0,8},{2,10},{4,12},{6,14},{8,0},{10,2},{12,4},{14,6},{16,24},{18,... | collective-permute-start | bytes 786440 | tf_op jit(solution)/shard_map/pathway_delta/ppermute | solution.py:516
  91.4 7.5 %collective-permute-done.17.refs_15_ = bf16[64,16,128]{2,1,0:T(8,128)(2,1)S(1)} collective-permute-done((bf16[64,16,128]{2,1,0:T(8,128)(2,1)S(1)}, bf16[64,16,128]{2,1,0:T(8,128)(2,1)S(1)}, u32[]{:S(2)}, u32[]{:S(2)}) %collective-permute-start.17) | collective-permute-done | bytes 262176 | tf_op jit(solution)/shard_map/pathway_delta/ppermute | solution.py:516
  99.0 11.0 %collective-permute-done.15.refs_13_ = bf16[64,16,128]{2,1,0:T(8,128)(2,1)S(1)} collective-permute-done((bf16[64,16,128]{2,1,0:T(8,128)(2,1)S(1)}, bf16[64,16,128]{2,1,0:T(8,128)(2,1)S(1)}, u32[]{:S(2)}, u32[]{:S(2)}) %collective-permute-start.15) | collective-permute-done | bytes 262176 | tf_op jit(solution)/shard_map/pathway_delta/ppermute | solution.py:516
  112.9 10.0 %link_backward.1 = (bf16[4,32,3072]{2,1,0:T(8,128)(2,1)}, bf16[4,1552,128]{2,1,0:T(8,128)(2,1)}, bf16[4,1552,128]{2,1,0:T(8,128)(2,1)}) custom-call(s32[2]{0:T(128)S(1)} %pad_add_fusion.place, s32[2,768]{1,0:T(2,128)S(1)} %dynamic-slice_bitcast_fusion.members, s32[512]{0:T(512)S(1)} %broadcast_xor_fusion.slots, bf16[4,32,3072]{2,1,0:T(8,128)(2,1)} %copy-done.3, ...), custom_call_target="tpu_custom_call" | custom-call | flops 6000000000 | bytes 20000000 | tf_op jit(solution)/shard_map/link_grads/link_backward/pallas_call | solution.py:465
  123.0 3.5 %all-to-all-start.1 = ((bf16[4,32,3072]{2,1,0:T(8,128)(2,1)}), bf16[4,32,3072]{2,1,0:T(8,128)(2,1)S(1)}, u32[]{:S(2)}, u32[]{:S(2)}) async-start(bf16[4,32,3072]{2,1,0:T(8,128)(2,1)} %get-tuple-element.39), calls=%async_computation.1 | async-start | bytes 1572864 | tf_op jit(solution)/shard_map/link_grads/all_to_all | solution.py:522
  127.8 3.0 %fusion.3 = (bf16[1552,128]{1,0:T(8,128)(2,1)}, bf16[1552,128]{1,0:T(8,128)(2,1)S(1)}, bf16[1552,128]{1,0:T(8,128)(2,1)S(1)}, bf16[1552,128]{1,0:T(8,128)(2,1)S(1)}) fusion(bf16[4,1552,128]{2,1,0:T(8,128)(2,1)} %copy-done.15, bf16[4,1552,128]{2,1,0:T(8,128)(2,1)} %get-tuple-element.40), kind=kLoop, calls=%fused_computation.19 | loop fusion | flops 3178496 | bytes 4767744 | tf_op jit(solution)/shard_map/grad_pathway/convert_element_type | solution.py:618
  130.9 2.8 %collective-permute-start.21 = (bf16[1552,128]{1,0:T(8,128)(2,1)}, bf16[1552,128]{1,0:T(8,128)(2,1)S(1)}, u32[]{:S(2)}, u32[]{:S(2)}) collective-permute-start(bf16[1552,128]{1,0:T(8,128)(2,1)} %get-tuple-element.51), channel_id=1, source_target_pairs={{0,6},{2,4},{4,2},{6,0},{8,14},{10,12},{12,10},{14,8},{16,22},{18,... | collective-permute-start | bytes 1191944 | tf_op jit(solution)/shard_map/grad_pathway/ppermute | solution.py:512
  134.4 4.3 %all-to-all-done.1 = bf16[4,32,3072]{2,1,0:T(8,128)(2,1)S(1)} async-done(((bf16[4,32,3072]{2,1,0:T(8,128)(2,1)}), bf16[4,32,3072]{2,1,0:T(8,128)(2,1)S(1)}, u32[]{:S(2)}, u32[]{:S(2)}) %all-to-all-start.1) | async-done | bytes 786464 | tf_op jit(solution)/shard_map/link_grads/all_to_all | solution.py:522
  138.7 6.8 %gene_backward.1 = bf16[16,49152]{1,0:T(8,128)(2,1)} custom-call(s32[192]{0:T(256)S(1)} %copy-done.9, bf16[128,49152]{1,0:T(8,128)(2,1)} %geno_hbm.3, bf16[128,3072]{1,0:T(8,128)(2,1)S(1)} %bitcast.27), custom_call_target="tpu_custom_call" | custom-call | flops 1006632960 | bytes 28311552 | tf_op jit(solution)/shard_map/grad_gene/gene_backward/pallas_call | solution.py:217
  145.5 2.7 %collective-permute-done.21.refs_3_ = bf16[1552,128]{1,0:T(8,128)(2,1)S(1)} collective-permute-done((bf16[1552,128]{1,0:T(8,128)(2,1)}, bf16[1552,128]{1,0:T(8,128)(2,1)S(1)}, u32[]{:S(2)}, u32[]{:S(2)}) %collective-permute-start.21) | collective-permute-done | bytes 397344 | tf_op jit(solution)/shard_map/grad_pathway/ppermute | solution.py:512
  148.1 7.2 %collective-permute-done.20.refs_2_ = bf16[1552,128]{1,0:T(8,128)(2,1)S(1)} collective-permute-done((bf16[1552,128]{1,0:T(8,128)(2,1)S(1)}, bf16[1552,128]{1,0:T(8,128)(2,1)S(1)}, u32[]{:S(2)}, u32[]{:S(2)}) %collective-permute-start.20) | collective-permute-done | bytes 397344 | tf_op jit(solution)/shard_map/grad_pathway/ppermute | solution.py:512
  156.7 2.4 %collective-permute-done.23 = bf16[16,49152]{1,0:T(8,128)(2,1)} collective-permute-done((bf16[16,49152]{1,0:T(8,128)(2,1)}, bf16[16,49152]{1,0:T(8,128)(2,1)}, u32[]{:S(2)}, u32[]{:S(2)}) %collective-permute-start.23) | collective-permute-done | bytes 1572896 | tf_op jit(solution)/shard_map/grad_pathway/ppermute | solution.py:519
  159.1 3.4 %convert_add_fusion = f32[16,49152]{1,0:T(8,128)} fusion(bf16[16,49152]{1,0:T(8,128)(2,1)} %collective-permute-done.23, bf16[16,49152]{1,0:T(8,128)(2,1)S(1)} %copy-done.14), kind=kLoop, calls=%fused_computation | loop fusion | flops 2359296 | bytes 6291456 | tf_op jit(solution)/shard_map/grad_pathway/add | solution.py:629
  (122 shorter events, 31.0 us)
Async XLA Ops:
  3.1 20.6 %collective-permute-start.2 = (bf16[1552,128]{1,0:T(8,128)(2,1)S(1)}, bf16[1552,128]{1,0:T(8,128)(2,1)S(1)}, u32[]{:S(2)}, u32[]{:S(2)}) collective-permute-start(bf16[1552,128]{1,0:T(8,128)(2,1)S(1)} %fold_links.2.refs_0_), channel_id=1, source_target_pairs={{0,6},{2,4},{4,2},{6,0},{8,14},{10,12},{12,10},{14,8},{16,22},{18,... | collective-permute-start | bytes 1191944 | tf_op jit(solution)/shard_map/link_weights/ppermute | solution.py:512
  7.0 17.9 %collective-permute-start.1 = (bf16[1552,128]{1,0:T(8,128)(2,1)S(1)}, bf16[1552,128]{1,0:T(8,128)(2,1)S(1)}, u32[]{:S(2)}, u32[]{:S(2)}) collective-permute-start(bf16[1552,128]{1,0:T(8,128)(2,1)S(1)} %fold_links.2.refs_0_), channel_id=1, source_target_pairs={{0,4},{2,6},{4,0},{6,2},{8,12},{10,14},{12,8},{14,10},{16,20},{18,... | collective-permute-start | bytes 1191944 | tf_op jit(solution)/shard_map/link_weights/ppermute | solution.py:512
  7.5 18.8 %collective-permute-start = (bf16[1552,128]{1,0:T(8,128)(2,1)S(1)}, bf16[1552,128]{1,0:T(8,128)(2,1)}, u32[]{:S(2)}, u32[]{:S(2)}) collective-permute-start(bf16[1552,128]{1,0:T(8,128)(2,1)S(1)} %fold_links.2.refs_0_), channel_id=1, source_target_pairs={{0,2},{2,0},{4,6},{6,4},{8,10},{10,8},{12,14},{14,12},{16,18},{18,... | collective-permute-start | bytes 1191944 | tf_op jit(solution)/shard_map/link_weights/ppermute | solution.py:512
  18.1 15.5 %all-to-all-start = ((bf16[4,32,3072]{2,1,0:T(8,128)(2,1)}), bf16[4,32,3072]{2,1,0:T(8,128)(2,1)S(1)}, u32[]{:S(2)}, u32[]{:S(2)}) async-start(bf16[4,32,3072]{2,1,0:T(8,128)(2,1)} %bitcast.3), calls=%async_computation | async-start | bytes 1572864 | tf_op jit(solution)/shard_map/hidden/all_to_all | solution.py:522
  23.7 9.9 %collective-permute-start.5 = (bf16[1552,128]{1,0:T(8,128)(2,1)S(1)}, bf16[1552,128]{1,0:T(8,128)(2,1)S(1)}, u32[]{:S(2)}, u32[]{:S(2)}) collective-permute-start(bf16[1552,128]{1,0:T(8,128)(2,1)S(1)} %collective-permute-done.2.refs_3_), channel_id=1, source_target_pairs={{0,1},{1,0},{2,3},{3,2},{4,5},{5,4},{6,7},{7,6},{8,9},{9,8},{10,11... | collective-permute-start | bytes 1191944 | tf_op jit(solution)/shard_map/link_weights/ppermute | solution.py:519
  24.9 9.4 %collective-permute-start.4 = (bf16[1552,128]{1,0:T(8,128)(2,1)S(1)}, bf16[1552,128]{1,0:T(8,128)(2,1)}, u32[]{:S(2)}, u32[]{:S(2)}) collective-permute-start(bf16[1552,128]{1,0:T(8,128)(2,1)S(1)} %collective-permute-done.1.refs_2_), channel_id=1, source_target_pairs={{0,1},{1,0},{2,3},{3,2},{4,5},{5,4},{6,7},{7,6},{8,9},{9,8},{10,11... | collective-permute-start | bytes 1191944 | tf_op jit(solution)/shard_map/link_weights/ppermute | solution.py:519
  26.3 8.0 %collective-permute-start.3 = (bf16[1552,128]{1,0:T(8,128)(2,1)}, bf16[1552,128]{1,0:T(8,128)(2,1)}, u32[]{:S(2)}, u32[]{:S(2)}) collective-permute-start(bf16[1552,128]{1,0:T(8,128)(2,1)} %collective-permute-done.refs_1_), channel_id=1, source_target_pairs={{0,1},{1,0},{2,3},{3,2},{4,5},{5,4},{6,7},{7,6},{8,9},{9,8},{10,11... | collective-permute-start | bytes 1191944 | tf_op jit(solution)/shard_map/link_weights/ppermute | solution.py:519
  42.5 9.3 %collective-permute-start.6 = (bf16[64,16,128]{2,1,0:T(8,128)(2,1)S(1)}, bf16[64,16,128]{2,1,0:T(8,128)(2,1)S(1)}, u32[]{:S(2)}, u32[]{:S(2)}) collective-permute-start(bf16[64,16,128]{2,1,0:T(8,128)(2,1)S(1)} %get-tuple-element.30), channel_id=1, source_target_pairs={{0,8},{2,10},{4,12},{6,14},{8,0},{10,2},{12,4},{14,6},{16,24},{18,... | collective-permute-start | bytes 786440 | tf_op jit(solution)/shard_map/pathway_sum/ppermute | solution.py:516
  44.2 18.0 %collective-permute-start.9 = (bf16[64,16,128]{2,1,0:T(8,128)(2,1)S(1)}, bf16[64,16,128]{2,1,0:T(8,128)(2,1)S(1)}, u32[]{:S(2)}, u32[]{:S(2)}) collective-permute-start(bf16[64,16,128]{2,1,0:T(8,128)(2,1)S(1)} %get-tuple-element.35), channel_id=1, source_target_pairs={{0,8},{2,10},{4,12},{6,14},{8,0},{10,2},{12,4},{14,6},{16,24},{18,... | collective-permute-start | bytes 786440 | tf_op jit(solution)/shard_map/pathway_sum/ppermute | solution.py:516
  51.9 21.5 %collective-permute-start.7 = (bf16[64,16,128]{2,1,0:T(8,128)(2,1)S(1)}, bf16[64,16,128]{2,1,0:T(8,128)(2,1)S(1)}, u32[]{:S(2)}, u32[]{:S(2)}) collective-permute-start(bf16[64,16,128]{2,1,0:T(8,128)(2,1)S(1)} %add_convert_fusion.5), channel_id=1, source_target_pairs={{0,16},{2,18},{4,20},{6,22},{8,24},{10,26},{12,28},{14,30},{16,0},... | collective-permute-start | bytes 786440 | tf_op jit(solution)/shard_map/pathway_sum/ppermute | solution.py:516
  54.5 18.8 %collective-permute-start.8 = (bf16[64,16,128]{2,1,0:T(8,128)(2,1)S(1)}, bf16[64,16,128]{2,1,0:T(8,128)(2,1)S(1)}, u32[]{:S(2)}, u32[]{:S(2)}) collective-permute-start(bf16[64,16,128]{2,1,0:T(8,128)(2,1)S(1)} %get-tuple-element.32), channel_id=1, source_target_pairs={{0,8},{2,10},{4,12},{6,14},{8,0},{10,2},{12,4},{14,6},{16,24},{18,... | collective-permute-start | bytes 786440 | tf_op jit(solution)/shard_map/pathway_sum/ppermute | solution.py:516
  62.2 14.9 %collective-permute-start.10 = (bf16[64,16,128]{2,1,0:T(8,128)(2,1)S(1)}, bf16[64,16,128]{2,1,0:T(8,128)(2,1)S(1)}, u32[]{:S(2)}, u32[]{:S(2)}) collective-permute-start(bf16[64,16,128]{2,1,0:T(8,128)(2,1)S(1)} %add_convert_fusion.4), channel_id=1, source_target_pairs={{0,16},{2,18},{4,20},{6,22},{8,24},{10,26},{12,28},{14,30},{16,0},... | collective-permute-start | bytes 786440 | tf_op jit(solution)/shard_map/pathway_sum/ppermute | solution.py:516
  62.3 22.3 %collective-permute-start.11 = (bf16[64,16,128]{2,1,0:T(8,128)(2,1)S(1)}, bf16[64,16,128]{2,1,0:T(8,128)(2,1)S(1)}, u32[]{:S(2)}, u32[]{:S(2)}) collective-permute-start(bf16[64,16,128]{2,1,0:T(8,128)(2,1)S(1)} %get-tuple-element.38), channel_id=1, source_target_pairs={{0,8},{2,10},{4,12},{6,14},{8,0},{10,2},{12,4},{14,6},{16,24},{18,... | collective-permute-start | bytes 786440 | tf_op jit(solution)/shard_map/pathway_sum/ppermute | solution.py:516
  73.6 16.0 %collective-permute-start.14 = (bf16[64,16,128]{2,1,0:T(8,128)(2,1)S(1)}, bf16[64,16,128]{2,1,0:T(8,128)(2,1)S(1)}, u32[]{:S(2)}, u32[]{:S(2)}) collective-permute-start(bf16[64,16,128]{2,1,0:T(8,128)(2,1)S(1)} %multiply_convert_fusion.1.refs_8_), channel_id=1, source_target_pairs={{0,16},{2,18},{4,20},{6,22},{8,24},{10,26},{12,28},{14,30},{16,0},... | collective-permute-start | bytes 786440 | tf_op jit(solution)/shard_map/pathway_delta/ppermute | solution.py:516
  73.7 17.8 %collective-permute-start.12 = (bf16[64,16,128]{2,1,0:T(8,128)(2,1)S(1)}, bf16[64,16,128]{2,1,0:T(8,128)(2,1)S(1)}, u32[]{:S(2)}, u32[]{:S(2)}) collective-permute-start(bf16[64,16,128]{2,1,0:T(8,128)(2,1)S(1)} %multiply_convert_fusion.1.refs_8_), channel_id=1, source_target_pairs={{0,8},{2,10},{4,12},{6,14},{8,0},{10,2},{12,4},{14,6},{16,24},{18,... | collective-permute-start | bytes 786440 | tf_op jit(solution)/shard_map/pathway_delta/ppermute | solution.py:516
  85.1 13.9 %collective-permute-start.17 = (bf16[64,16,128]{2,1,0:T(8,128)(2,1)S(1)}, bf16[64,16,128]{2,1,0:T(8,128)(2,1)S(1)}, u32[]{:S(2)}, u32[]{:S(2)}) collective-permute-start(bf16[64,16,128]{2,1,0:T(8,128)(2,1)S(1)} %get-tuple-element.57.refs_9_), channel_id=1, source_target_pairs={{0,24},{2,26},{4,28},{6,30},{8,16},{10,18},{12,20},{14,22},{16,8},... | collective-permute-start | bytes 786440 | tf_op jit(solution)/shard_map/pathway_delta/ppermute | solution.py:516
  87.0 23.0 %collective-permute-start.15 = (bf16[64,16,128]{2,1,0:T(8,128)(2,1)S(1)}, bf16[64,16,128]{2,1,0:T(8,128)(2,1)S(1)}, u32[]{:S(2)}, u32[]{:S(2)}) collective-permute-start(bf16[64,16,128]{2,1,0:T(8,128)(2,1)S(1)} %get-tuple-element.57.refs_9_), channel_id=1, source_target_pairs={{0,16},{2,18},{4,20},{6,22},{8,24},{10,26},{12,28},{14,30},{16,0},... | collective-permute-start | bytes 786440 | tf_op jit(solution)/shard_map/pathway_delta/ppermute | solution.py:516
  87.0 23.0 %collective-permute-start.13 = (bf16[64,16,128]{2,1,0:T(8,128)(2,1)S(1)}, bf16[64,16,128]{2,1,0:T(8,128)(2,1)S(1)}, u32[]{:S(2)}, u32[]{:S(2)}) collective-permute-start(bf16[64,16,128]{2,1,0:T(8,128)(2,1)S(1)} %get-tuple-element.57.refs_9_), channel_id=1, source_target_pairs={{0,8},{2,10},{4,12},{6,14},{8,0},{10,2},{12,4},{14,6},{16,24},{18,... | collective-permute-start | bytes 786440 | tf_op jit(solution)/shard_map/pathway_delta/ppermute | solution.py:516
  89.5 22.6 %collective-permute-start.16 = (bf16[64,16,128]{2,1,0:T(8,128)(2,1)S(1)}, bf16[64,16,128]{2,1,0:T(8,128)(2,1)S(1)}, u32[]{:S(2)}, u32[]{:S(2)}) collective-permute-start(bf16[64,16,128]{2,1,0:T(8,128)(2,1)S(1)} %collective-permute-done.14.refs_12_), channel_id=1, source_target_pairs={{0,8},{2,10},{4,12},{6,14},{8,0},{10,2},{12,4},{14,6},{16,24},{18,... | collective-permute-start | bytes 786440 | tf_op jit(solution)/shard_map/pathway_delta/ppermute | solution.py:516
  123.0 15.6 %all-to-all-start.1 = ((bf16[4,32,3072]{2,1,0:T(8,128)(2,1)}), bf16[4,32,3072]{2,1,0:T(8,128)(2,1)S(1)}, u32[]{:S(2)}, u32[]{:S(2)}) async-start(bf16[4,32,3072]{2,1,0:T(8,128)(2,1)} %get-tuple-element.39), calls=%async_computation.1 | async-start | bytes 1572864 | tf_op jit(solution)/shard_map/link_grads/all_to_all | solution.py:522
  130.9 17.3 %collective-permute-start.21 = (bf16[1552,128]{1,0:T(8,128)(2,1)}, bf16[1552,128]{1,0:T(8,128)(2,1)S(1)}, u32[]{:S(2)}, u32[]{:S(2)}) collective-permute-start(bf16[1552,128]{1,0:T(8,128)(2,1)} %get-tuple-element.51), channel_id=1, source_target_pairs={{0,6},{2,4},{4,2},{6,0},{8,14},{10,12},{12,10},{14,8},{16,22},{18,... | collective-permute-start | bytes 1191944 | tf_op jit(solution)/shard_map/grad_pathway/ppermute | solution.py:512
  133.6 21.7 %collective-permute-start.20 = (bf16[1552,128]{1,0:T(8,128)(2,1)S(1)}, bf16[1552,128]{1,0:T(8,128)(2,1)S(1)}, u32[]{:S(2)}, u32[]{:S(2)}) collective-permute-start(bf16[1552,128]{1,0:T(8,128)(2,1)S(1)} %get-tuple-element.52), channel_id=1, source_target_pairs={{0,4},{2,6},{4,0},{6,2},{8,12},{10,14},{12,8},{14,10},{16,20},{18,... | collective-permute-start | bytes 1191944 | tf_op jit(solution)/shard_map/grad_pathway/ppermute | solution.py:512
  134.2 21.1 %collective-permute-start.19 = (bf16[1552,128]{1,0:T(8,128)(2,1)S(1)}, bf16[1552,128]{1,0:T(8,128)(2,1)S(1)}, u32[]{:S(2)}, u32[]{:S(2)}) collective-permute-start(bf16[1552,128]{1,0:T(8,128)(2,1)S(1)} %get-tuple-element.53), channel_id=1, source_target_pairs={{0,2},{2,0},{4,6},{6,4},{8,10},{10,8},{12,14},{14,12},{16,18},{18,... | collective-permute-start | bytes 1191944 | tf_op jit(solution)/shard_map/grad_pathway/ppermute | solution.py:512
  156.1 6.4 %collective-permute-start.22 = (f32[200,1024]{1,0:T(8,128)S(1)}, f32[200,1024]{1,0:T(8,128)S(1)}, u32[]{:S(2)}, u32[]{:S(2)}) collective-permute-start(f32[200,1024]{1,0:T(8,128)S(1)} %unfold_sum.1), channel_id=1, source_target_pairs={{0,1},{1,0},{2,3},{3,2},{4,5},{5,4},{6,7},{7,6},{8,9},{9,8},{10,11... | collective-permute-start | bytes 2457608 | tf_op jit(solution)/shard_map/grad_pathway/ppermute | solution.py:519
  (25 other events, 205.7 us)
